TPU v7x, 32 devices: a whole 2x2x4 slice. The times are simulated.
32 devices in a mesh: rep: 4 (over z), fsdp: 8 (over y, x, core).
Axes of the slice: x: 2, y: 2, z: 4, core: 2. Of those that a mesh axis runs over, the one named last changes fastest.
Arguments:
- latents: bfloat16 [32, 16, 16, 640], P(('rep', 'fsdp')), may hold values from -6 to 6
- cotangent: bfloat16 [32, 16, 16, 640], P(('rep', 'fsdp')), may hold values from -6 to 6
- conv_weight: bfloat16 [4, 5760, 640], P('rep', 'fsdp'), may hold values from -0.078125 to 0.078125
- norm_gain: float32 [4, 640], P('rep'), may hold values from 0.5 to 1.5
- norm_shift: float32 [4, 640], P('rep'), may hold values from -3 to 3
- partner_bit: int32 [8], replicated, may hold values from 0 to 1
Outputs:
- block_out: bfloat16 [32, 16, 16, 640], P(('rep', 'fsdp'))
- input_grad: bfloat16 [32, 16, 16, 640], P(('rep', 'fsdp'))
- weight_grad: float32 [4, 5760, 640], P('rep', 'fsdp')
- norm_grad: float32 [4, 2, 640], P('rep')
Inputs may be any that keep to these rules, and one draw needn't show every extreme that they name: In row shard f, replica r is paired with replica r with bit partner_bit[f] of its index flipped.
All inputs are finite; a program needn't handle non-finite values.
Results may differ from a plain program's by a relative error of at most 0.0065.
Values may be sent and summed in bfloat16 or wider, within the bound.
No kernel may reach another device: no remote copies, remote signals or barrier semaphores. Data moves between devices by JAX's collectives and lax.ppermute only.
A program may use at most 128 MiB of HBM per device.

v0:
```python
import functools

import jax
import jax.numpy as jnp
from jax import lax
from jax.experimental import pallas as pl
from jax.experimental.pallas import tpu as pltpu
from jax.sharding import PartitionSpec as P

GROUPS = 32


def partner(value, axis, stride):
    mask = 2**stride
    pairs = [(source, source ^ mask) for source in range(lax.axis_size(axis))]
    return lax.ppermute(value, axis, pairs)


def norm_forward(values_in, gain, shift, groups):
    count, side, chans = (values_in.shape[0], values_in.shape[1], values_in.shape[3])
    values = values_in.astype(jnp.float32).reshape(count, side * side, groups, chans // groups)
    center = jnp.mean(values, axis=(1, 3), keepdims=True)
    spread = jnp.mean(jnp.square(values - center), axis=(1, 3), keepdims=True)
    scale_inv = lax.rsqrt(spread + 1e-05)
    normed = (values - center) * scale_inv
    pre_act = normed * gain.reshape(groups, -1) + shift.reshape(groups, -1)
    return (normed, scale_inv, pre_act)


def make_patches(activation):
    count, side, chans = (activation.shape[0], activation.shape[1], activation.shape[3])
    padded = jnp.pad(activation, ((0, 0), (1, 1), (1, 1), (0, 0)))
    pieces = [
        padded[:, row_off : row_off + side, col_off : col_off + side, :]
        for row_off in range(3)
        for col_off in range(3)
    ]
    return jnp.concatenate(pieces, axis=-1).reshape(count * side * side, 9 * chans)


def fold_patches(patch_grad, count, side, chans):
    grads = patch_grad.reshape(count, side, side, 9, chans)
    total = jnp.zeros((count, side + 2, side + 2, chans), jnp.float32)
    for row_off in range(3):
        for col_off in range(3):
            tap = grads[:, :, :, row_off * 3 + col_off, :]
            total = total + jnp.pad(
                tap, ((0, 0), (row_off, 2 - row_off), (col_off, 2 - col_off), (0, 0))
            )
    return total[:, 1:-1, 1:-1, :]


def backward_rest(act_grad, normed, scale_inv, pre_act, gain, groups, inv_batch):
    count, side, chans = (act_grad.shape[0], act_grad.shape[1], act_grad.shape[3])
    act_grad = act_grad.reshape(count, side * side, groups, chans // groups)
    sigma = jax.nn.sigmoid(pre_act)
    pre_grad = act_grad * sigma * (1.0 + pre_act * (1.0 - sigma))
    gain_grad = jnp.sum(pre_grad * normed, axis=(0, 1)).reshape(-1) * inv_batch
    shift_grad = jnp.sum(pre_grad, axis=(0, 1)).reshape(-1) * inv_batch
    normed_grad = pre_grad * gain.reshape(groups, -1)
    first = jnp.mean(normed_grad, axis=(1, 3), keepdims=True)
    second = jnp.mean(normed_grad * normed, axis=(1, 3), keepdims=True)
    input_grad = scale_inv * (normed_grad - first - normed * second)
    return (
        input_grad.reshape(count, side, side, chans).astype(jnp.bfloat16),
        jnp.stack([gain_grad, shift_grad]),
    )


def shards_general(latents, cotangent, conv_weight, norm_gain, norm_shift, partner_bit):
    count, side, chans = (latents.shape[0], latents.shape[1], latents.shape[3])
    shard_total = lax.axis_size("fsdp")
    inv_batch = 1.0 / (count * shard_total)
    gain = norm_gain[0]
    normed, scale_inv, pre_act = norm_forward(latents, gain, norm_shift[0], GROUPS)
    activation = jax.nn.silu(pre_act).astype(jnp.bfloat16).reshape(count, side, side, chans)
    patches = make_patches(activation)
    cot_rows = cotangent.reshape(count * side * side, chans)
    weight_rows = conv_weight[0]
    output = jnp.dot(
        patches,
        lax.all_gather(weight_rows, "fsdp", axis=0, tiled=True),
        preferred_element_type=jnp.float32,
    )
    patch_grad = lax.dot_general(
        cot_rows,
        lax.all_gather(weight_rows, "fsdp", axis=0, tiled=True),
        (((1,), (1,)), ((), ())),
        preferred_element_type=jnp.float32,
    )
    block_out = output.astype(jnp.bfloat16).reshape(count, side, side, chans)
    act_grad = fold_patches(patch_grad, count, side, chans)
    input_grad, norm_term = backward_rest(
        act_grad, normed, scale_inv, pre_act, gain, GROUPS, inv_batch
    )
    weight_term = (
        lax.dot_general(
            patches, cot_rows, (((0,), (0,)), ((), ())), preferred_element_type=jnp.float32
        )
        * inv_batch
    )
    shard_rows = weight_rows.shape[0]
    term_pieces = weight_term.reshape(shard_total, shard_rows, chans)
    received = lax.all_to_all(
        term_pieces.astype(jnp.bfloat16), "fsdp", split_axis=0, concat_axis=0, tiled=True
    ).astype(term_pieces.dtype)
    weight_shard = jnp.sum(received, axis=0)
    bit_count = lax.axis_size("rep").bit_length() - 1
    shard_bit = lax.dynamic_index_in_dim(partner_bit, lax.axis_index("fsdp"), 0, keepdims=False)
    norm_bit = partner_bit[0]
    paired_norm = norm_term
    for bit_index in range(bit_count):
        other_norm = partner(norm_term, "rep", bit_index)
        paired_norm = jnp.where(norm_bit == bit_index, 0.5 * (norm_term + other_norm), paired_norm)
    norm_avg = lax.psum(paired_norm, "fsdp")
    weight_avg = weight_shard
    for bit_index in range(bit_count):
        other_weight = partner(weight_shard.astype(jnp.bfloat16), "rep", bit_index).astype(
            weight_shard.dtype
        )
        weight_avg = jnp.where(
            shard_bit == bit_index, 0.5 * (weight_shard + other_weight), weight_avg
        )
    return (block_out, input_grad, weight_avg[None], norm_avg[None])


CORE, ACROSS, ALONG = 1, 2, 4
VMEM_LIMIT = 12 * 1024 * 1024
F32, BF16 = jnp.float32, jnp.bfloat16


def swap(value, axis, mask):
    pairs = [(source, source ^ mask) for source in range(lax.axis_size(axis))]
    return lax.ppermute(value, axis, pairs)


def call(kernel, outs, args, scratch=(), order=(), copies_out=False, outside=()):
    vmem = pl.BlockSpec(memory_space=pltpu.VMEM)
    smem = pl.BlockSpec(memory_space=pltpu.SMEM)
    untouched = pl.BlockSpec(memory_space=pl.ANY)

    def body(*refs):
        kernel(*refs[: len(args)], *refs[len(args) + len(order) :])

    return pl.pallas_call(
        body,
        out_shape=tuple(outs),
        in_specs=[
            untouched if index in outside else smem if a.dtype == jnp.int32 else vmem
            for index, a in enumerate(args)
        ]
        + [untouched] * len(order),
        out_specs=tuple(untouched if copies_out else vmem for _ in outs),
        scratch_shapes=list(scratch),
        compiler_params=pltpu.CompilerParams(vmem_limit_bytes=VMEM_LIMIT),
    )(*args, *order)


def hold(values, order):
    untouched = pl.BlockSpec(memory_space=pl.ANY)
    return pl.pallas_call(
        lambda *refs: None,
        out_shape=tuple(shaped(value.shape, value.dtype) for value in values),
        in_specs=[untouched] * (len(values) + len(order)),
        out_specs=tuple(untouched for _ in values),
        input_output_aliases={index: index for index in range(len(values))},
        compiler_params=pltpu.CompilerParams(vmem_limit_bytes=1024 * 1024),
    )(*values, *order)


def shaped(shape, dtype):
    return jax.ShapeDtypeStruct(shape, dtype)


def matmul(left, right):
    return jnp.dot(left, right, preferred_element_type=F32)


def group_matrix(chans, groups, transpose):
    width = chans // groups
    shape = (128, chans) if transpose else (chans, 128)
    chan = lax.broadcasted_iota(jnp.int32, shape, 1 if transpose else 0)
    low = lax.broadcasted_iota(jnp.int32, shape, 0 if transpose else 1) * width
    return ((chan >= low) & (chan < low + width)).astype(F32)


def group_mean(columns, total, groups):
    chans = columns.shape[1]
    exact = dict(precision=lax.Precision.HIGHEST, preferred_element_type=F32)
    sums = jnp.dot(columns, group_matrix(chans, groups, False), **exact)
    return jnp.dot(sums, group_matrix(chans, groups, True), **exact) * (1.0 / total)


def col_sums(*values):
    rows = [jnp.sum(value, axis=0, keepdims=True) for value in values]
    fill = jnp.zeros((8 - len(rows), rows[0].shape[1]), F32)
    return jnp.concatenate(rows + [fill], axis=0)


def norm_kernel(groups, latent, params, act, stats):
    gain, shift = params[0:1], params[1:2]
    values = latent[...].astype(F32)
    total = values.shape[0] * values.shape[1] // groups
    center = group_mean(col_sums(values), total, groups)[0:1]
    moved = values - center
    spread = group_mean(col_sums(moved * moved), total, groups)[0:1]
    scale_inv = lax.rsqrt(spread + 1e-05)
    pre = moved * scale_inv * gain + shift
    act[...] = (pre / (1.0 + jnp.exp(-pre))).astype(BF16)
    stats[0:1] = center
    stats[1:2] = scale_inv


def tap_matrix(tap, side, transpose):
    shape = (side * side, side * side)
    here = lax.broadcasted_iota(jnp.int32, shape, 1 if transpose else 0)
    there = lax.broadcasted_iota(jnp.int32, shape, 0 if transpose else 1)
    row_off = lax.div(tap, 3)
    col_off = tap - 3 * row_off
    bits = side.bit_length() - 1
    rows = lax.shift_right_logical(there, bits) - lax.shift_right_logical(here, bits)
    cols = (there & (side - 1)) - (here & (side - 1))
    hit = (rows == row_off - 1) & (cols == col_off - 1)
    return hit.astype(F32).astype(BF16)


def prepare_kernel(side, taps, info, own, other, wide, turned, gather, scatter):
    rows, chans = own.shape
    area = side * side
    wide[...] = jnp.zeros_like(wide)
    wide[pl.ds(pl.multiple_of(info[1], 16), rows), :] = own[...]
    wide[pl.ds(pl.multiple_of(info[2], 16), rows), :] = other[...]
    for tap in range(taps):
        part = slice(tap * chans, (tap + 1) * chans)
        turned[part, :] = wide[part, :].T
        gather[tap * area : (tap + 1) * area, :] = tap_matrix(info[0] + tap, side, False)
        scatter[tap * area : (tap + 1) * area, :] = tap_matrix(info[0] + tap, side, True)


def move_into(target, index, taps, matrices, value):
    area, width = value.shape
    moved = matmul(matrices, value).astype(BF16)
    for tap in range(taps):
        target[index * area : (index + 1) * area, tap * width : (tap + 1) * width] = moved[
            tap * area : (tap + 1) * area
        ]


def split_latents(value, refs):
    area = refs[0].shape[0]
    for index, ref in enumerate(refs):
        ref[...] = value[index * area : (index + 1) * area].astype(ref.dtype)


def spread_kernel(taps, scatter, c0, c1, c2, moved):
    for index, ref in enumerate((c0, c1, c2)):
        move_into(moved, index, taps, scatter[...], ref[...])


def grad_kernel(turned, moved, g0, g1, g2):
    split_latents(matmul(moved[...], turned[...]), (g0, g1, g2))


def move_kernel(taps, scatter, top, bottom, moved):
    move_into(moved, 0, taps, scatter[...], jnp.concatenate([top[...], bottom[...]], axis=0))


def weight_kernel(taps, moved, a0, a1, a2, part, across):
    area, chans = a0.shape
    for index, ref in enumerate((a0, a1, a2)):
        across[:, index * area : (index + 1) * area] = ref[...].T
    for tap in range(taps):
        block = slice(tap * chans, (tap + 1) * chans)
        part[block, :] = matmul(across[...], moved[:, block])


def out_kernel(taps, gather, wide, a0, a1, a2, top, bottom, y0, y1, y2, y3, moved):
    last = jnp.concatenate([top[...], bottom[...]], axis=0)
    for index, value in enumerate((a0[...], a1[...], a2[...], last)):
        move_into(moved, index, taps, gather[...], value)
    split_latents(matmul(moved[...], wide[...]), (y0, y1, y2, y3))


def turn_twice(top, bottom, across):
    chans, half = top.shape[1], top.shape[0]
    for start in (0, chans):
        across[start : start + chans, :half] = top[...].T
        across[start : start + chans, half:] = bottom[...].T


def window_terms(start, rows, chans, across, moved, part):
    tap = lax.div(start, chans)
    offset = start - tap * chans
    picked = across[pl.ds(pl.multiple_of(offset, 16), rows), :]
    row = lax.broadcasted_iota(jnp.int32, picked.shape, 0)
    zero = jnp.zeros_like(picked)
    in_first = row < chans - offset
    left = jnp.concatenate(
        [jnp.where(in_first, picked, zero), jnp.where(in_first, zero, picked)], axis=1
    )
    right = jnp.concatenate(
        [moved[:, pl.ds(pl.multiple_of((tap + step) * chans, 128), chans)] for step in range(2)],
        axis=0,
    )
    return part[pl.ds(pl.multiple_of(start, 16), rows), :] + matmul(left, right)


def finish_kernel(factor, info, top, bottom, moved, part, send, across):
    turn_twice(top, bottom, across)
    terms = window_terms(info[2], send.shape[0], top.shape[1], across, moved, part)
    send[...] = (terms * factor).astype(BF16)


def keep_kernel(factor, info, turned, top, bottom, moved, part, keep, g3, across):
    turn_twice(top, bottom, across)
    keep[...] = window_terms(info[1], keep.shape[0], top.shape[1], across, moved, part) * factor
    g3[...] = matmul(moved[...], turned[...]).astype(BF16)


def sum_kernel(y0, y1, y2, y3, total):
    total[...] = (y0[...] + sum(ref[...].astype(F32) for ref in (y1, y2, y3))).astype(BF16)


def join_kernel(keep, got, narrow):
    narrow[...] = (keep[...] + got[...].astype(F32)).astype(BF16)


def pair_kernel(chunks, bit, own, pair1, pair2, mean, made, leave):
    size = own.shape[0] // chunks
    stores = []
    for index in range(chunks):
        rows = pl.ds(index * size, size)

        @pl.when(bit[0] == 0)
        def _():
            made[rows, :] = 0.5 * (own[rows, :].astype(F32) + pair1[rows, :].astype(F32))

        @pl.when(bit[0] != 0)
        def _():
            made[rows, :] = 0.5 * (own[rows, :].astype(F32) + pair2[rows, :].astype(F32))

        stores.append(pltpu.make_async_copy(made.at[rows], mean.at[rows], leave.at[index]))
        stores[-1].start()
    for store in stores:
        store.wait()


def back_kernel(groups, factor, latent, stats, params, g0, g1, g2, g3, grad, terms):
    gain, shift = params[0:1], params[1:2]
    values = latent[...].astype(F32)
    total = values.shape[0] * values.shape[1] // groups
    scale_inv = stats[1:2]
    normed = (values - stats[0:1]) * scale_inv
    pre = normed * gain + shift
    act_grad = g0[...] + sum(ref[...].astype(F32) for ref in (g1, g2, g3))
    sigma = 1.0 / (1.0 + jnp.exp(-pre))
    pre_grad = act_grad * sigma * (1.0 + pre * (1.0 - sigma))
    sums = col_sums(pre_grad * normed, pre_grad)
    terms[...] = sums[0:2] * factor
    means = group_mean(sums * gain, total, groups)
    grad[...] = (scale_inv * (pre_grad * gain - means[1:2] - normed * means[0:1])).astype(BF16)


def shards_plane(latents, cotangent, conv_weight, norm_gain, norm_shift, partner_bit):
    side, chans = latents.shape[1], latents.shape[3]
    area = side * side
    shard_total = lax.axis_size("fsdp")
    inv_batch = 1.0 / shard_total
    place = lax.axis_index("fsdp")
    weight = conv_weight[0]
    rows = weight.shape[0]
    starts = [2 * rows * chip for chip in range(shard_total // 2)]
    taps = max((start % chans + 2 * rows + chans - 1) // chans for start in starts)
    start = 2 * rows * (place // 2)
    first = jnp.minimum(start // chans, 9 - taps)
    offset = start - first * chans
    core = place % 2
    own_start, other_start = offset + rows * core, offset + rows * (1 - core)
    info = jnp.stack([first, own_start, other_start]).astype(jnp.int32)

    def columns(count, dtype=BF16):
        return shaped((count * area, taps * chans), dtype)

    plane, plane_b = shaped((area, chans), F32), shaped((area, chans), BF16)
    window = (taps * chans, chans)

    latent = latents.reshape(area, chans)
    cot0 = cotangent.reshape(area, chans)
    params = jnp.concatenate([norm_gain, norm_shift])
    other_weight = swap(weight, "fsdp", CORE)
    cot1 = swap(cot0, "fsdp", ACROSS)
    cot2 = swap(cot0, "fsdp", ALONG)
    act0, stats = call(
        functools.partial(norm_kernel, GROUPS),
        [plane_b, shaped((2, chans), F32)],
        [latent, params],
    )
    act2 = swap(act0, "fsdp", ALONG)
    act1 = swap(act0, "fsdp", ACROSS)
    wide, turned, gather, scatter = call(
        functools.partial(prepare_kernel, side, taps),
        [shaped(window, BF16)] * 2 + [shaped((taps * area, area), BF16)] * 2,
        [info, weight, other_weight],
        order=[stats],
    )
    (moved,) = call(
        functools.partial(spread_kernel, taps), [columns(3)], [scatter, cot0, cot1, cot2]
    )
    cot1, cot2 = hold([cot1, cot2], [moved])
    grad0, grad1, grad2 = call(grad_kernel, [plane, plane_b, plane_b], [turned, moved])
    half = area // 2
    cot3 = [swap(cot2[:half], "fsdp", ACROSS), swap(cot1[half:], "fsdp", ALONG)]
    act2, act1 = hold([act2, act1], [grad0])
    act3 = [swap(act2[:half], "fsdp", ACROSS), swap(act1[half:], "fsdp", ALONG)]
    (part,) = call(
        functools.partial(weight_kernel, taps),
        [shaped(window, F32)],
        [moved, act0, act1, act2],
        [pltpu.VMEM((chans, 3 * area), BF16)],
    )
    (moved3,) = call(
        functools.partial(move_kernel, taps), [columns(1)], [scatter, *cot3], order=[part]
    )
    (send,) = call(
        functools.partial(finish_kernel, inv_batch),
        [shaped((rows, chans), BF16)],
        [info, *act3, moved3, part],
        [pltpu.VMEM((2 * chans, area), BF16)],
    )
    got = swap(send, "fsdp", CORE)
    keep, grad3 = call(
        functools.partial(keep_kernel, inv_batch),
        [shaped((rows, chans), F32), plane_b],
        [info, turned, *act3, moved3, part],
        [pltpu.VMEM((2 * chans, area), BF16)],
    )
    (narrow,) = call(join_kernel, [shaped((rows, chans), BF16)], [keep, got])
    pair1 = swap(narrow, "rep", 1)
    pair2 = swap(narrow, "rep", 2)

    masks = (ACROSS, ALONG, ACROSS | ALONG)
    grads = hold([grad1, grad2, grad3], [narrow])
    grads = [swap(value, "fsdp", mask) for value, mask in zip(grads, masks)]
    out0, out1, out2, out3 = call(
        functools.partial(out_kernel, taps),
        [plane, plane_b, plane_b, plane_b],
        [gather, wide, act0, act1, act2, *act3],
        [pltpu.VMEM((4 * area, taps * chans), BF16)],
        order=[narrow],
    )
    out1, out2 = hold([out1, out2], [narrow])
    out1, out2 = swap(out1, "fsdp", ACROSS), swap(out2, "fsdp", ALONG)

    input_grad, terms = call(
        functools.partial(back_kernel, GROUPS, inv_batch),
        [plane_b, shaped((2, chans), F32)],
        [latent, stats, params, grad0, *grads],
        order=[out3],
    )
    (last,) = hold([out3], [terms])
    last = swap(last, "fsdp", ACROSS | ALONG)
    terms = terms + swap(terms, "fsdp", ACROSS)
    (terms,) = hold([terms], [out1, out2])
    for mask in (ALONG, CORE):
        terms = terms + swap(terms, "fsdp", mask)
    (block_out,) = call(sum_kernel, [plane_b], [out0, out1, out2, last])
    (terms,) = hold([terms], [block_out])
    norm_avg = lax.cond(
        partner_bit[0] == 0,
        lambda own: 0.5 * (own + swap(own, "rep", 1)),
        lambda own: 0.5 * (own + swap(own, "rep", 2)),
        terms,
    )
    shard_bit = lax.dynamic_slice_in_dim(partner_bit, place, 1)
    (weight_avg,) = call(
        functools.partial(pair_kernel, 5),
        [shaped((rows, chans), F32)],
        [shard_bit, narrow, pair1, pair2],
        [pltpu.VMEM((rows, chans), F32), pltpu.SemaphoreType.DMA((5,))],
        copies_out=True,
    )
    shape = (1, side, side, chans)
    return (block_out.reshape(shape), input_grad.reshape(shape), weight_avg[None], norm_avg[None])


def solution(mesh):
    in_specs = (
        P(("rep", "fsdp"), None, None, None),
        P(("rep", "fsdp"), None, None, None),
        P("rep", "fsdp", None),
        P("rep", None),
        P("rep", None),
        P(),
    )
    out_specs = (
        P(("rep", "fsdp"), None, None, None),
        P(("rep", "fsdp"), None, None, None),
        P("rep", "fsdp", None),
        P("rep", None, None),
    )
    planes = mesh.shape["fsdp"] == 8 and mesh.shape["rep"] == 4
    shards = shards_plane if planes else shards_general
    return jax.shard_map(shards, mesh=mesh, in_specs=in_specs, out_specs=out_specs, check_vma=False)
```

profile of v0, /device:TPU:0, one launch (start us, length us, event | category | flops | bytes accessed | tf_op | source)
XLA Modules:
  0.0 80.2 jit_solution(9825967785338801966)
XLA Ops:
  1.1 2.6 %collective-permute-start.6 = (bf16[256,640]{1,0:T(8,128)(2,1)}, bf16[256,640]{1,0:T(8,128)(2,1)S(1)}, u32[]{:S(2)}, u32[]{:S(2)}) collective-permute-start(bf16[256,640]{1,0:T(8,128)(2,1)} %bitcast.19), channel_id=1, source_target_pairs={{0,4},{1,5},{2,6},{3,7},{4,0},{5,1},{6,2},{7,3},{8,12},{9,13},{10,... | collective-permute-start | bytes 983048 | tf_op jit(solution)/shard_map/ppermute | solution.py:134
  3.7 1.5 %collective-permute-start.5 = (bf16[256,640]{1,0:T(8,128)(2,1)}, bf16[256,640]{1,0:T(8,128)(2,1)S(1)}, u32[]{:S(2)}, u32[]{:S(2)}) collective-permute-start(bf16[256,640]{1,0:T(8,128)(2,1)} %bitcast.20), channel_id=1, source_target_pairs={{0,2},{1,3},{2,0},{3,1},{4,6},{5,7},{6,4},{7,5},{8,10},{9,11},{10,... | collective-permute-start | bytes 983048 | tf_op jit(solution)/shard_map/ppermute | solution.py:134
  6.9 1.5 %shard_map.93 = (bf16[256,640]{1,0:T(8,128)(2,1)S(1)}, f32[2,640]{1,0:T(2,128)S(1)}) custom-call(bf16[256,640]{1,0:T(8,128)(2,1)S(1)} %bitcast.15, f32[2,640]{1,0:T(2,128)S(1)} %pad_maximum_fusion.refs_1_.refs_2_), custom_call_target="tpu_custom_call" | custom-call | tf_op jit(solution)/shard_map/pallas_call | solution.py:145
  9.2 1.2 %copy-done.3 = bf16[1,720,640]{2,1,0:T(8,128)(2,1)S(1)} copy-done((bf16[1,720,640]{2,1,0:T(8,128)(2,1)S(1)}, bf16[1,720,640]{2,1,0:T(8,128)(2,1)}, u32[]{:S(2)}) %copy-start.3) | copy-done | bytes 921624
  10.3 1.9 %shard_map.94 = (bf16[1920,640]{1,0:T(8,128)(2,1)S(1)}, bf16[1920,640]{1,0:T(8,128)(2,1)S(1)}, bf16[768,256]{1,0:T(8,128)(2,1)S(1)}, bf16[768,256]{1,0:T(8,128)(2,1)S(1)}) custom-call(s32[3]{0:T(128)S(1)} %pad_add_fusion.refs_0_, bf16[720,640]{1,0:T(8,128)(2,1)S(1)} %bitcast.18, bf16[720,640]{1,0:T(8,128)(2,1)S(1)} %collective-permute-done.2.refs_2_, ...), custom_call_target="tpu_custom_call" | custom-call | tf_op jit(solution)/shard_map/pallas_call | solution.py:145
  12.5 2.0 %collective-permute-done.5.refs_2_.refs_0_ = bf16[256,640]{1,0:T(8,128)(2,1)S(1)} collective-permute-done((bf16[256,640]{1,0:T(8,128)(2,1)}, bf16[256,640]{1,0:T(8,128)(2,1)S(1)}, u32[]{:S(2)}, u32[]{:S(2)}) %collective-permute-start.5) | collective-permute-done | bytes 327712 | tf_op jit(solution)/shard_map/ppermute | solution.py:134
  14.5 1.1 %shard_map.95.refs_1_.refs_2_.refs_0_ = bf16[768,1920]{1,0:T(8,128)(2,1)S(1)} custom-call(bf16[768,256]{1,0:T(8,128)(2,1)S(1)} %get-tuple-element.41.refs_0_, bf16[256,640]{1,0:T(8,128)(2,1)S(1)} %bitcast.21, bf16[256,640]{1,0:T(8,128)(2,1)S(1)} %collective-permute-done.5.refs_2_.refs_0_, bf16[256,640]{1,0:T(8,128)(2,1)S(1)} %collective-permute-done.6.refs_3_.refs_1_), custom_call_target="tpu_custom_call" | custom-call | tf_op jit(solution)/shard_map/pallas_call | solution.py:145
  15.8 1.9 %collective-permute-start.9 = (bf16[128,640]{1,0:T(8,128)(2,1)S(1)}, bf16[128,640]{1,0:T(8,128)(2,1)S(1)}, u32[]{:S(2)}, u32[]{:S(2)}) collective-permute-start(bf16[128,640]{1,0:T(8,128)(2,1)S(1)} %slice.17), channel_id=1, source_target_pairs={{0,2},{1,3},{2,0},{3,1},{4,6},{5,7},{6,4},{7,5},{8,10},{9,11},{10,... | collective-permute-start | bytes 491528 | tf_op jit(solution)/shard_map/ppermute | solution.py:134
  17.7 2.6 %shard_map.96 = (f32[256,640]{1,0:T(8,128)S(1)}, bf16[256,640]{1,0:T(8,128)(2,1)S(1)}, bf16[256,640]{1,0:T(8,128)(2,1)S(1)}) custom-call(bf16[1920,640]{1,0:T(8,128)(2,1)S(1)} %get-tuple-element.40.refs_0_.refs_1_, bf16[768,1920]{1,0:T(8,128)(2,1)S(1)} %shard_map.95.refs_1_.refs_2_.refs_0_), custom_call_target="tpu_custom_call" | custom-call | tf_op jit(solution)/shard_map/pallas_call | solution.py:145
  20.3 1.2 %collective-permute-done.4.refs_1_ = bf16[256,640]{1,0:T(8,128)(2,1)S(1)} collective-permute-done((bf16[256,640]{1,0:T(8,128)(2,1)S(1)}, bf16[256,640]{1,0:T(8,128)(2,1)S(1)}, u32[]{:S(2)}, u32[]{:S(2)}) %collective-permute-start.4) | collective-permute-done | bytes 327712 | tf_op jit(solution)/shard_map/ppermute | solution.py:134
  21.6 1.6 %collective-permute-start.7 = (bf16[128,640]{1,0:T(8,128)(2,1)S(1)}, bf16[128,640]{1,0:T(8,128)(2,1)S(1)}, u32[]{:S(2)}, u32[]{:S(2)}) collective-permute-start(bf16[128,640]{1,0:T(8,128)(2,1)S(1)} %slice.15), channel_id=1, source_target_pairs={{0,2},{1,3},{2,0},{3,1},{4,6},{5,7},{6,4},{7,5},{8,10},{9,11},{10,... | collective-permute-start | bytes 491528 | tf_op jit(solution)/shard_map/ppermute | solution.py:134
  23.6 2.5 %shard_map.99.refs_3_.refs_5_.refs_4_ = f32[1920,640]{1,0:T(8,128)S(1)} custom-call(bf16[768,1920]{1,0:T(8,128)(2,1)S(1)} %shard_map.95.refs_1_.refs_2_.refs_0_, bf16[256,640]{1,0:T(8,128)(2,1)S(1)} %get-tuple-element.39.refs_1_.refs_2_, bf16[256,640]{1,0:T(8,128)(2,1)S(1)} %get-tuple-element.43.refs_2_.refs_3_, ...), custom_call_target="tpu_custom_call" | custom-call | tf_op jit(solution)/shard_map/pallas_call | solution.py:145
  26.6 1.1 %collective-permute-done.7.refs_2_.refs_1_.refs_5_ = bf16[128,640]{1,0:T(8,128)(2,1)S(1)} collective-permute-done((bf16[128,640]{1,0:T(8,128)(2,1)S(1)}, bf16[128,640]{1,0:T(8,128)(2,1)S(1)}, u32[]{:S(2)}, u32[]{:S(2)}) %collective-permute-start.7) | collective-permute-done | bytes 163872 | tf_op jit(solution)/shard_map/ppermute | solution.py:134
  28.5 1.5 %shard_map.102 = bf16[720,640]{1,0:T(8,128)(2,1)S(1)} custom-call(s32[3]{0:T(128)S(1)} %pad_add_fusion.refs_0_, bf16[128,640]{1,0:T(8,128)(2,1)S(1)} %collective-permute-done.7.refs_2_.refs_1_.refs_5_, bf16[128,640]{1,0:T(8,128)(2,1)S(1)} %collective-permute-done.8.refs_3_.refs_2_.refs_6_, bf16[256,1920]{1,0:T(8,128)(2,1)S(1)} %shard_map.100.refs_4_.refs_3_, ...), custom_call_target="tpu_custom_call" | custom-call | tf_op jit(solution)/shard_map/pallas_call | solution.py:145
  30.1 2.3 %shard_map.101 = (f32[720,640]{1,0:T(8,128)S(1)}, bf16[256,640]{1,0:T(8,128)(2,1)S(1)}) custom-call(s32[3]{0:T(128)S(1)} %pad_add_fusion.refs_0_, bf16[1920,640]{1,0:T(8,128)(2,1)S(1)} %get-tuple-element.40.refs_0_.refs_1_, bf16[128,640]{1,0:T(8,128)(2,1)S(1)} %collective-permute-done.7.refs_2_.refs_1_.refs_5_, ...), custom_call_target="tpu_custom_call" | custom-call | tf_op jit(solution)/shard_map/pallas_call | solution.py:145
  32.7 2.7 %collective-permute-start.19 = (bf16[720,640]{1,0:T(8,128)(2,1)S(1)}, bf16[720,640]{1,0:T(8,128)(2,1)S(1)}, u32[]{:S(2)}, u32[]{:S(2)}) collective-permute-start(bf16[720,640]{1,0:T(8,128)(2,1)S(1)} %shard_map.103.refs_7_.refs_2_.refs_3_.refs_1_), channel_id=1, source_target_pairs={{0,16},{8,24},{16,0},{24,8},{1,17},{9,25},{17,1},{25,9},{2,18},{10... | collective-permute-start | bytes 2764808 | tf_op jit(solution)/shard_map/ppermute | solution.py:134
  35.4 1.6 %collective-permute-start.18 = (bf16[720,640]{1,0:T(8,128)(2,1)S(1)}, bf16[720,640]{1,0:T(8,128)(2,1)}, u32[]{:S(2)}, u32[]{:S(2)}) collective-permute-start(bf16[720,640]{1,0:T(8,128)(2,1)S(1)} %shard_map.103.refs_7_.refs_2_.refs_3_.refs_1_), channel_id=1, source_target_pairs={{0,8},{8,0},{16,24},{24,16},{1,9},{9,1},{17,25},{25,17},{2,10},{10... | collective-permute-start | bytes 2764808 | tf_op jit(solution)/shard_map/ppermute | solution.py:134
  38.3 2.2 %collective-permute-start.16 = (bf16[256,640]{1,0:T(8,128)(2,1)S(1)}, bf16[256,640]{1,0:T(8,128)(2,1)S(1)}, u32[]{:S(2)}, u32[]{:S(2)}) collective-permute-start(bf16[256,640]{1,0:T(8,128)(2,1)S(1)} %get-tuple-element.59), channel_id=1, source_target_pairs={{0,6},{1,7},{2,4},{3,5},{4,2},{5,3},{6,0},{7,1},{8,14},{9,15},{10,... | collective-permute-start | bytes 983048 | tf_op jit(solution)/shard_map/ppermute | solution.py:134
  40.5 4.8 %shard_map.104 = (f32[256,640]{1,0:T(8,128)S(1)}, bf16[256,640]{1,0:T(8,128)(2,1)S(1)}, bf16[256,640]{1,0:T(8,128)(2,1)S(1)}, bf16[256,640]{1,0:T(8,128)(2,1)S(1)}) custom-call(bf16[768,256]{1,0:T(8,128)(2,1)S(1)} %get-tuple-element.37.refs_0_, bf16[1920,640]{1,0:T(8,128)(2,1)S(1)} %get-tuple-element.38.refs_1_, ...), custom_call_target="tpu_custom_call" | custom-call | tf_op jit(solution)/shard_map/pallas_call | solution.py:145
  45.3 2.3 %collective-permute-done.14.refs_4_ = bf16[256,640]{1,0:T(8,128)(2,1)S(1)} collective-permute-done((bf16[256,640]{1,0:T(8,128)(2,1)S(1)}, bf16[256,640]{1,0:T(8,128)(2,1)S(1)}, u32[]{:S(2)}, u32[]{:S(2)}) %collective-permute-start.14) | collective-permute-done | bytes 327712 | tf_op jit(solution)/shard_map/ppermute | solution.py:134
  48.4 5.8 %collective-permute-done.15.refs_5_ = bf16[256,640]{1,0:T(8,128)(2,1)S(1)} collective-permute-done((bf16[256,640]{1,0:T(8,128)(2,1)S(1)}, bf16[256,640]{1,0:T(8,128)(2,1)S(1)}, u32[]{:S(2)}, u32[]{:S(2)}) %collective-permute-start.15) | collective-permute-done | bytes 327712 | tf_op jit(solution)/shard_map/ppermute | solution.py:134
  54.6 2.1 %shard_map.107 = (bf16[256,640]{1,0:T(8,128)(2,1)}, f32[2,640]{1,0:T(2,128)S(1)}) custom-call(bf16[256,640]{1,0:T(8,128)(2,1)S(1)} %bitcast.16, f32[2,640]{1,0:T(2,128)S(1)} %get-tuple-element.36.refs_3_.refs_1_, f32[2,640]{1,0:T(2,128)S(1)} %pad_maximum_fusion.refs_1_.refs_2_, f32[256,640]{1,0:T(8,128)S(1)} %get-tuple-element.42.refs_2_.refs_3_, ...), custom_call_target="tpu_custom_call" | custom-call | tf_op jit(solution)/shard_map/pallas_call | solution.py:145
  56.7 1.4 %collective-permute-start.20 = (f32[2,640]{1,0:T(2,128)S(1)}, f32[2,640]{1,0:T(2,128)S(1)}, u32[]{:S(2)}, u32[]{:S(2)}) collective-permute-start(f32[2,640]{1,0:T(2,128)S(1)} %get-tuple-element.60.refs_1_), channel_id=1, source_target_pairs={{0,2},{1,3},{2,0},{3,1},{4,6},{5,7},{6,4},{7,5},{8,10},{9,11},{10,... | collective-permute-start | bytes 15368 | tf_op jit(solution)/shard_map/ppermute | solution.py:134
  58.1 2.5 %collective-permute-done.20 = f32[2,640]{1,0:T(2,128)S(1)} collective-permute-done((f32[2,640]{1,0:T(2,128)S(1)}, f32[2,640]{1,0:T(2,128)S(1)}, u32[]{:S(2)}, u32[]{:S(2)}) %collective-permute-start.20) | collective-permute-done | bytes 5152 | tf_op jit(solution)/shard_map/ppermute | solution.py:134
  60.6 2.6 %collective-permute-start.17 = (bf16[256,640]{1,0:T(8,128)(2,1)S(1)}, bf16[256,640]{1,0:T(8,128)(2,1)S(1)}, u32[]{:S(2)}, u32[]{:S(2)}) collective-permute-start(bf16[256,640]{1,0:T(8,128)(2,1)S(1)} %shard_map.108), channel_id=1, source_target_pairs={{0,6},{1,7},{2,4},{3,5},{4,2},{5,3},{6,0},{7,1},{8,14},{9,15},{10,... | collective-permute-start | bytes 983048 | tf_op jit(solution)/shard_map/ppermute | solution.py:134
  63.3 4.1 %collective-permute-done.21 = f32[2,640]{1,0:T(2,128)S(1)} collective-permute-done((f32[2,640]{1,0:T(2,128)S(1)}, f32[2,640]{1,0:T(2,128)S(1)}, u32[]{:S(2)}, u32[]{:S(2)}) %collective-permute-start.21) | collective-permute-done | bytes 5152 | tf_op jit(solution)/shard_map/ppermute | solution.py:134
  68.8 1.4 %collective-permute-done.17.refs_3_ = bf16[256,640]{1,0:T(8,128)(2,1)S(1)} collective-permute-done((bf16[256,640]{1,0:T(8,128)(2,1)S(1)}, bf16[256,640]{1,0:T(8,128)(2,1)S(1)}, u32[]{:S(2)}, u32[]{:S(2)}) %collective-permute-start.17) | collective-permute-done | bytes 327712 | tf_op jit(solution)/shard_map/ppermute | solution.py:134
  70.2 1.1 %copy-done.5 = f32[256,640]{1,0:T(8,128)S(1)} copy-done((f32[256,640]{1,0:T(8,128)S(1)}, f32[256,640]{1,0:T(8,128)}, u32[]{:S(2)}) %copy-start.5) | copy-done | bytes 655384
  72.2 1.0 %copy-done = bf16[256,640]{1,0:T(8,128)(2,1)S(1)} copy-done((bf16[256,640]{1,0:T(8,128)(2,1)S(1)}, bf16[256,640]{1,0:T(8,128)(2,1)}, u32[]{:S(2)}) %copy-start) | copy-done | bytes 327704
  73.1 3.6 %conditional.1 = (f32[1,2,640]{2,1,0:T(2,128)S(1)}) conditional(s32[]{:T(128)} %bitcast.11, f32[2,640]{1,0:T(2,128)S(1)} %shard_map.112, f32[2,640]{1,0:T(2,128)S(1)} %shard_map.112), branch_computations={%region_0.1_spmd, %region_1.2_spmd} | conditional | flops 2560 | bytes 35888 | solution.py:468
  73.6 3.2 %collective-permute-done.1 = f32[2,640]{1,0:T(2,128)S(1)} collective-permute-done((f32[2,640]{1,0:T(2,128)S(1)}, f32[2,640]{1,0:T(2,128)S(1)}, u32[]{:S(2)}, u32[]{:S(2)}) %collective-permute-start.1) | collective-permute-done | bytes 5152 | tf_op jit(solution)/shard_map/cond/branch_1_fun/ppermute | solution.py:134
  76.8 3.2 %shard_map.110 = f32[720,640]{1,0:T(8,128)} custom-call(s32[1]{0:T(128)} %get-tuple-element.63.refs_0_, bf16[720,640]{1,0:T(8,128)(2,1)S(1)} %shard_map.103.refs_7_.refs_2_.refs_3_.refs_1_, bf16[720,640]{1,0:T(8,128)(2,1)} %collective-permute-done.18.refs_2_, bf16[720,640]{1,0:T(8,128)(2,1)S(1)} %collective-permute-done.19.refs_3_), custom_call_target="tpu_custom_call" | custom-call | tf_op jit(solution)/shard_map/pallas_call | solution.py:145
  (62 shorter events, 10.2 us)
Async XLA Ops:
  0.6 8.5 %collective-permute-start.2 = (bf16[720,640]{1,0:T(8,128)(2,1)}, bf16[720,640]{1,0:T(8,128)(2,1)S(1)}, u32[]{:S(2)}, u32[]{:S(2)}) collective-permute-start(bf16[720,640]{1,0:T(8,128)(2,1)} %bitcast.17), channel_id=1, source_target_pairs={{0,1},{1,0},{2,3},{3,2},{4,5},{5,4},{6,7},{7,6},{8,9},{9,8},{10,11... | collective-permute-start | bytes 2764808 | tf_op jit(solution)/shard_map/ppermute | solution.py:134
  1.1 11.4 %collective-permute-start.6 = (bf16[256,640]{1,0:T(8,128)(2,1)}, bf16[256,640]{1,0:T(8,128)(2,1)S(1)}, u32[]{:S(2)}, u32[]{:S(2)}) collective-permute-start(bf16[256,640]{1,0:T(8,128)(2,1)} %bitcast.19), channel_id=1, source_target_pairs={{0,4},{1,5},{2,6},{3,7},{4,0},{5,1},{6,2},{7,3},{8,12},{9,13},{10,... | collective-permute-start | bytes 983048 | tf_op jit(solution)/shard_map/ppermute | solution.py:134
  3.7 10.8 %collective-permute-start.5 = (bf16[256,640]{1,0:T(8,128)(2,1)}, bf16[256,640]{1,0:T(8,128)(2,1)S(1)}, u32[]{:S(2)}, u32[]{:S(2)}) collective-permute-start(bf16[256,640]{1,0:T(8,128)(2,1)} %bitcast.20), channel_id=1, source_target_pairs={{0,2},{1,3},{2,0},{3,1},{4,6},{5,7},{6,4},{7,5},{8,10},{9,11},{10,... | collective-permute-start | bytes 983048 | tf_op jit(solution)/shard_map/ppermute | solution.py:134
  5.9 1.0 %copy-start.1 = (bf16[1,16,16,640]{3,2,1,0:T(8,128)(2,1)S(1)}, bf16[1,16,16,640]{3,2,1,0:T(8,128)(2,1)}, u32[]{:S(2)}) copy-start(bf16[1,16,16,640]{3,2,1,0:T(8,128)(2,1)} %param.8) | copy-start | bytes 983044
  6.9 7.6 %copy-start.6 = (bf16[1,16,16,640]{3,2,1,0:T(8,128)(2,1)S(1)}, bf16[1,16,16,640]{3,2,1,0:T(8,128)(2,1)}, u32[]{:S(2)}) copy-start(bf16[1,16,16,640]{3,2,1,0:T(8,128)(2,1)} %param.9) | copy-start | bytes 983044
  8.4 13.1 %collective-permute-start.4 = (bf16[256,640]{1,0:T(8,128)(2,1)S(1)}, bf16[256,640]{1,0:T(8,128)(2,1)S(1)}, u32[]{:S(2)}, u32[]{:S(2)}) collective-permute-start(bf16[256,640]{1,0:T(8,128)(2,1)S(1)} %get-tuple-element.39.refs_1_.refs_2_), channel_id=1, source_target_pairs={{0,2},{1,3},{2,0},{3,1},{4,6},{5,7},{6,4},{7,5},{8,10},{9,11},{10,... | collective-permute-start | bytes 983048 | tf_op jit(solution)/shard_map/ppermute | solution.py:134
  9.0 12.5 %collective-permute-start.3 = (bf16[256,640]{1,0:T(8,128)(2,1)S(1)}, bf16[256,640]{1,0:T(8,128)(2,1)S(1)}, u32[]{:S(2)}, u32[]{:S(2)}) collective-permute-start(bf16[256,640]{1,0:T(8,128)(2,1)S(1)} %get-tuple-element.39.refs_1_.refs_2_), channel_id=1, source_target_pairs={{0,4},{1,5},{2,6},{3,7},{4,0},{5,1},{6,2},{7,3},{8,12},{9,13},{10,... | collective-permute-start | bytes 983048 | tf_op jit(solution)/shard_map/ppermute | solution.py:134
  9.2 1.2 %copy-start.3 = (bf16[1,720,640]{2,1,0:T(8,128)(2,1)S(1)}, bf16[1,720,640]{2,1,0:T(8,128)(2,1)}, u32[]{:S(2)}) copy-start(bf16[1,720,640]{2,1,0:T(8,128)(2,1)} %param.10) | copy-start | bytes 2764804
  15.7 10.5 %collective-permute-start.10 = (bf16[128,640]{1,0:T(8,128)(2,1)S(1)}, bf16[128,640]{1,0:T(8,128)(2,1)S(1)}, u32[]{:S(2)}, u32[]{:S(2)}) collective-permute-start(bf16[128,640]{1,0:T(8,128)(2,1)S(1)} %slice.18), channel_id=1, source_target_pairs={{0,4},{1,5},{2,6},{3,7},{4,0},{5,1},{6,2},{7,3},{8,12},{9,13},{10,... | collective-permute-start | bytes 491528 | tf_op jit(solution)/shard_map/ppermute | solution.py:134
  15.8 10.4 %collective-permute-start.9 = (bf16[128,640]{1,0:T(8,128)(2,1)S(1)}, bf16[128,640]{1,0:T(8,128)(2,1)S(1)}, u32[]{:S(2)}, u32[]{:S(2)}) collective-permute-start(bf16[128,640]{1,0:T(8,128)(2,1)S(1)} %slice.17), channel_id=1, source_target_pairs={{0,2},{1,3},{2,0},{3,1},{4,6},{5,7},{6,4},{7,5},{8,10},{9,11},{10,... | collective-permute-start | bytes 491528 | tf_op jit(solution)/shard_map/ppermute | solution.py:134
  21.6 6.2 %collective-permute-start.7 = (bf16[128,640]{1,0:T(8,128)(2,1)S(1)}, bf16[128,640]{1,0:T(8,128)(2,1)S(1)}, u32[]{:S(2)}, u32[]{:S(2)}) collective-permute-start(bf16[128,640]{1,0:T(8,128)(2,1)S(1)} %slice.15), channel_id=1, source_target_pairs={{0,2},{1,3},{2,0},{3,1},{4,6},{5,7},{6,4},{7,5},{8,10},{9,11},{10,... | collective-permute-start | bytes 491528 | tf_op jit(solution)/shard_map/ppermute | solution.py:134
  23.1 5.3 %collective-permute-start.8 = (bf16[128,640]{1,0:T(8,128)(2,1)S(1)}, bf16[128,640]{1,0:T(8,128)(2,1)S(1)}, u32[]{:S(2)}, u32[]{:S(2)}) collective-permute-start(bf16[128,640]{1,0:T(8,128)(2,1)S(1)} %slice.16), channel_id=1, source_target_pairs={{0,4},{1,5},{2,6},{3,7},{4,0},{5,1},{6,2},{7,3},{8,12},{9,13},{10,... | collective-permute-start | bytes 491528 | tf_op jit(solution)/shard_map/ppermute | solution.py:134
  30.0 2.5 %collective-permute-start.11 = (bf16[720,640]{1,0:T(8,128)(2,1)S(1)}, bf16[720,640]{1,0:T(8,128)(2,1)S(1)}, u32[]{:S(2)}, u32[]{:S(2)}) collective-permute-start(bf16[720,640]{1,0:T(8,128)(2,1)S(1)} %shard_map.102), channel_id=1, source_target_pairs={{0,1},{1,0},{2,3},{3,2},{4,5},{5,4},{6,7},{7,6},{8,9},{9,8},{10,11... | collective-permute-start | bytes 2764808 | tf_op jit(solution)/shard_map/ppermute | solution.py:134
  32.7 44.1 %collective-permute-start.19 = (bf16[720,640]{1,0:T(8,128)(2,1)S(1)}, bf16[720,640]{1,0:T(8,128)(2,1)S(1)}, u32[]{:S(2)}, u32[]{:S(2)}) collective-permute-start(bf16[720,640]{1,0:T(8,128)(2,1)S(1)} %shard_map.103.refs_7_.refs_2_.refs_3_.refs_1_), channel_id=1, source_target_pairs={{0,16},{8,24},{16,0},{24,8},{1,17},{9,25},{17,1},{25,9},{2,18},{10... | collective-permute-start | bytes 2764808 | tf_op jit(solution)/shard_map/ppermute | solution.py:134
  35.4 41.4 %collective-permute-start.18 = (bf16[720,640]{1,0:T(8,128)(2,1)S(1)}, bf16[720,640]{1,0:T(8,128)(2,1)}, u32[]{:S(2)}, u32[]{:S(2)}) collective-permute-start(bf16[720,640]{1,0:T(8,128)(2,1)S(1)} %shard_map.103.refs_7_.refs_2_.refs_3_.refs_1_), channel_id=1, source_target_pairs={{0,8},{8,0},{16,24},{24,16},{1,9},{9,1},{17,25},{25,17},{2,10},{10... | collective-permute-start | bytes 2764808 | tf_op jit(solution)/shard_map/ppermute | solution.py:134
  37.0 10.6 %collective-permute-start.14 = (bf16[256,640]{1,0:T(8,128)(2,1)S(1)}, bf16[256,640]{1,0:T(8,128)(2,1)S(1)}, u32[]{:S(2)}, u32[]{:S(2)}) collective-permute-start(bf16[256,640]{1,0:T(8,128)(2,1)S(1)} %get-tuple-element.57), channel_id=1, source_target_pairs={{0,2},{1,3},{2,0},{3,1},{4,6},{5,7},{6,4},{7,5},{8,10},{9,11},{10,... | collective-permute-start | bytes 983048 | tf_op jit(solution)/shard_map/ppermute | solution.py:134
  37.8 16.4 %collective-permute-start.15 = (bf16[256,640]{1,0:T(8,128)(2,1)S(1)}, bf16[256,640]{1,0:T(8,128)(2,1)S(1)}, u32[]{:S(2)}, u32[]{:S(2)}) collective-permute-start(bf16[256,640]{1,0:T(8,128)(2,1)S(1)} %get-tuple-element.58), channel_id=1, source_target_pairs={{0,4},{1,5},{2,6},{3,7},{4,0},{5,1},{6,2},{7,3},{8,12},{9,13},{10,... | collective-permute-start | bytes 983048 | tf_op jit(solution)/shard_map/ppermute | solution.py:134
  38.3 16.3 %collective-permute-start.16 = (bf16[256,640]{1,0:T(8,128)(2,1)S(1)}, bf16[256,640]{1,0:T(8,128)(2,1)S(1)}, u32[]{:S(2)}, u32[]{:S(2)}) collective-permute-start(bf16[256,640]{1,0:T(8,128)(2,1)S(1)} %get-tuple-element.59), channel_id=1, source_target_pairs={{0,6},{1,7},{2,4},{3,5},{4,2},{5,3},{6,0},{7,1},{8,14},{9,15},{10,... | collective-permute-start | bytes 983048 | tf_op jit(solution)/shard_map/ppermute | solution.py:134
  40.5 14.1 %copy-start.2 = (bf16[1,16,16,640]{3,2,1,0:T(8,128)(2,1)S(1)}, bf16[1,16,16,640]{3,2,1,0:T(8,128)(2,1)}, u32[]{:S(2)}) copy-start(bf16[1,16,16,640]{3,2,1,0:T(8,128)(2,1)} %param.8) | copy-start | bytes 983044
  45.3 8.9 %copy-start.4 = (f32[256,640]{1,0:T(8,128)}, f32[256,640]{1,0:T(8,128)S(1)}, u32[]{:S(2)}) copy-start(f32[256,640]{1,0:T(8,128)S(1)} %get-tuple-element.48.refs_0_) | copy-start | bytes 1966084
  45.3 22.1 %copy-start.8 = (s32[8]{0:T(128)S(1)}, s32[8]{0:T(128)}, u32[]{:S(2)}) copy-start(s32[8]{0:T(128)} %param.13) | copy-start | bytes 100
  47.6 15.6 %collective-permute-start.12 = (bf16[256,640]{1,0:T(8,128)(2,1)S(1)}, bf16[256,640]{1,0:T(8,128)(2,1)S(1)}, u32[]{:S(2)}, u32[]{:S(2)}) collective-permute-start(bf16[256,640]{1,0:T(8,128)(2,1)S(1)} %get-tuple-element.51), channel_id=1, source_target_pairs={{0,2},{1,3},{2,0},{3,1},{4,6},{5,7},{6,4},{7,5},{8,10},{9,11},{10,... | collective-permute-start | bytes 983048 | tf_op jit(solution)/shard_map/ppermute | solution.py:134
  54.2 9.0 %collective-permute-start.13 = (bf16[256,640]{1,0:T(8,128)(2,1)S(1)}, bf16[256,640]{1,0:T(8,128)(2,1)S(1)}, u32[]{:S(2)}, u32[]{:S(2)}) collective-permute-start(bf16[256,640]{1,0:T(8,128)(2,1)S(1)} %get-tuple-element.52), channel_id=1, source_target_pairs={{0,4},{1,5},{2,6},{3,7},{4,0},{5,1},{6,2},{7,3},{8,12},{9,13},{10,... | collective-permute-start | bytes 983048 | tf_op jit(solution)/shard_map/ppermute | solution.py:134
  56.7 3.9 %collective-permute-start.20 = (f32[2,640]{1,0:T(2,128)S(1)}, f32[2,640]{1,0:T(2,128)S(1)}, u32[]{:S(2)}, u32[]{:S(2)}) collective-permute-start(f32[2,640]{1,0:T(2,128)S(1)} %get-tuple-element.60.refs_1_), channel_id=1, source_target_pairs={{0,2},{1,3},{2,0},{3,1},{4,6},{5,7},{6,4},{7,5},{8,10},{9,11},{10,... | collective-permute-start | bytes 15368 | tf_op jit(solution)/shard_map/ppermute | solution.py:134
  60.6 9.6 %collective-permute-start.17 = (bf16[256,640]{1,0:T(8,128)(2,1)S(1)}, bf16[256,640]{1,0:T(8,128)(2,1)S(1)}, u32[]{:S(2)}, u32[]{:S(2)}) collective-permute-start(bf16[256,640]{1,0:T(8,128)(2,1)S(1)} %shard_map.108), channel_id=1, source_target_pairs={{0,6},{1,7},{2,4},{3,5},{4,2},{5,3},{6,0},{7,1},{8,14},{9,15},{10,... | collective-permute-start | bytes 983048 | tf_op jit(solution)/shard_map/ppermute | solution.py:134
  63.2 4.2 %collective-permute-start.21 = (f32[2,640]{1,0:T(2,128)S(1)}, f32[2,640]{1,0:T(2,128)S(1)}, u32[]{:S(2)}, u32[]{:S(2)}) collective-permute-start(f32[2,640]{1,0:T(2,128)S(1)} %shard_map.111), channel_id=1, source_target_pairs={{0,4},{1,5},{2,6},{3,7},{4,0},{5,1},{6,2},{7,3},{8,12},{9,13},{10,... | collective-permute-start | bytes 15368 | tf_op jit(solution)/shard_map/ppermute | solution.py:134
  67.4 1.3 %collective-permute-start.22 = (f32[2,640]{1,0:T(2,128)S(1)}, f32[2,640]{1,0:T(2,128)S(1)}, u32[]{:S(2)}, u32[]{:S(2)}) collective-permute-start(f32[2,640]{1,0:T(2,128)S(1)} %add.35), channel_id=1, source_target_pairs={{0,1},{1,0},{2,3},{3,2},{4,5},{5,4},{6,7},{7,6},{8,9},{9,8},{10,11... | collective-permute-start | bytes 15368 | tf_op jit(solution)/shard_map/ppermute | solution.py:134
  70.2 1.1 %copy-start.5 = (f32[256,640]{1,0:T(8,128)S(1)}, f32[256,640]{1,0:T(8,128)}, u32[]{:S(2)}) copy-start(f32[256,640]{1,0:T(8,128)} %copy-done.4) | copy-start | bytes 1966084
  72.2 1.0 %copy-start = (bf16[256,640]{1,0:T(8,128)(2,1)S(1)}, bf16[256,640]{1,0:T(8,128)(2,1)}, u32[]{:S(2)}) copy-start(bf16[256,640]{1,0:T(8,128)(2,1)} %shard_map.109.refs_1_) | copy-start | bytes 983044
  73.1 3.6 %collective-permute-start.1 = (f32[2,640]{1,0:T(2,128)S(1)}, f32[2,640]{1,0:T(2,128)S(1)}, u32[]{:S(2)}, u32[]{:S(2)}) collective-permute-start(f32[2,640]{1,0:T(2,128)S(1)} %param.1), channel_id=1, source_target_pairs={{0,8},{8,0},{16,24},{24,16},{1,9},{9,1},{17,25},{25,17},{2,10},{10... | collective-permute-start | bytes 15368 | tf_op jit(solution)/shard_map/cond/branch_1_fun/ppermute | solution.py:134
  76.8 3.2 %copy-start.7 = (f32[1,2,640]{2,1,0:T(2,128)}, f32[1,2,640]{2,1,0:T(2,128)S(1)}, u32[]{:S(2)}) copy-start(f32[1,2,640]{2,1,0:T(2,128)S(1)} %get-tuple-element.64) | copy-start | bytes 15364
where the time goes:
time: 81 us; the launch traced here: 80.2 us
  waiting for transfers between devices  25.1 us (31%)
  Pallas kernels  25 us (31%)
  starting transfers between devices  22.6 us (28%)
  local copies, waits for them, and re-layouts  4.97 us (6%)
  between operations  1.7 us (2%)
    ppermute x22, waiting for transfers between devices, swap(): return lax.ppermute(value, axis, pairs)  25.1 us
    pallas_call x13, Pallas kernels, call(): pl.pallas_call(body, out_shape=tuple(outs), in_specs=[untouched if index...  25 us
    ppermute x22, starting transfers between devices, swap(): return lax.ppermute(value, axis, pairs)  22.6 us
    unnamed x18, local copies, waits for them, and re-layouts  4.23 us
  transfers between devices with their start and end apart: 22, of which 13 were waited for; matrix products, arithmetic and copies ran while one was open for 2% of the time, Pallas kernels for 25%

commit v1 on v0

--- a/solution.py
+++ b/solution.py
@@ -125,7 +125,7 @@
 
 
 CORE, ACROSS, ALONG = 1, 2, 4
-VMEM_LIMIT = 12 * 1024 * 1024
+VMEM_LIMIT = 8 * 1024 * 1024
 F32, BF16 = jnp.float32, jnp.bfloat16
 
 

time: 81 us -> 81.4 us (level)
  waiting for transfers between devices: 25.1 us -> 26.1 us
    ppermute x22, waiting for transfers between devices: 25.1 us -> 26.1 us  [swap(): return lax.ppermute(value, axis, pairs)]
where the time goes in v1:
time: 81.4 us; the launch traced here: 81.1 us
  waiting for transfers between devices  26.1 us (32%)
  Pallas kernels  25 us (31%)
  starting transfers between devices  22.5 us (28%)
  local copies, waits for them, and re-layouts  4.97 us (6%)
  between operations  1.7 us (2%)
    ppermute x22, waiting for transfers between devices, swap(): return lax.ppermute(value, axis, pairs)  26.1 us
    pallas_call x13, Pallas kernels, call(): pl.pallas_call(body, out_shape=tuple(outs), in_specs=[untouched if index...  25 us
    ppermute x22, starting transfers between devices, swap(): return lax.ppermute(value, axis, pairs)  22.5 us
    unnamed x18, local copies, waits for them, and re-layouts  4.23 us
  transfers between devices with their start and end apart: 22, of which 13 were waited for; matrix products, arithmetic and copies ran while one was open for 2% of the time, Pallas kernels for 25%

profile of v1, /device:TPU:0, one launch (start us, length us, event | category | flops | bytes accessed | tf_op | source)
XLA Modules:
  0.0 81.1 jit_solution(7556808173631222135)
XLA Ops:
  1.1 2.6 %collective-permute-start.6 = (bf16[256,640]{1,0:T(8,128)(2,1)}, bf16[256,640]{1,0:T(8,128)(2,1)S(1)}, u32[]{:S(2)}, u32[]{:S(2)}) collective-permute-start(bf16[256,640]{1,0:T(8,128)(2,1)} %bitcast.19), channel_id=1, source_target_pairs={{0,4},{1,5},{2,6},{3,7},{4,0},{5,1},{6,2},{7,3},{8,12},{9,13},{10,... | collective-permute-start | bytes 983048 | tf_op jit(solution)/shard_map/ppermute | solution.py:134
  3.7 1.5 %collective-permute-start.5 = (bf16[256,640]{1,0:T(8,128)(2,1)}, bf16[256,640]{1,0:T(8,128)(2,1)S(1)}, u32[]{:S(2)}, u32[]{:S(2)}) collective-permute-start(bf16[256,640]{1,0:T(8,128)(2,1)} %bitcast.20), channel_id=1, source_target_pairs={{0,2},{1,3},{2,0},{3,1},{4,6},{5,7},{6,4},{7,5},{8,10},{9,11},{10,... | collective-permute-start | bytes 983048 | tf_op jit(solution)/shard_map/ppermute | solution.py:134
  6.9 1.5 %shard_map.93 = (bf16[256,640]{1,0:T(8,128)(2,1)S(1)}, f32[2,640]{1,0:T(2,128)S(1)}) custom-call(bf16[256,640]{1,0:T(8,128)(2,1)S(1)} %bitcast.15, f32[2,640]{1,0:T(2,128)S(1)} %pad_maximum_fusion.refs_1_.refs_2_), custom_call_target="tpu_custom_call" | custom-call | tf_op jit(solution)/shard_map/pallas_call | solution.py:145
  9.2 1.2 %copy-done.3 = bf16[1,720,640]{2,1,0:T(8,128)(2,1)S(1)} copy-done((bf16[1,720,640]{2,1,0:T(8,128)(2,1)S(1)}, bf16[1,720,640]{2,1,0:T(8,128)(2,1)}, u32[]{:S(2)}) %copy-start.3) | copy-done | bytes 921624
  10.3 1.9 %shard_map.94 = (bf16[1920,640]{1,0:T(8,128)(2,1)S(1)}, bf16[1920,640]{1,0:T(8,128)(2,1)S(1)}, bf16[768,256]{1,0:T(8,128)(2,1)S(1)}, bf16[768,256]{1,0:T(8,128)(2,1)S(1)}) custom-call(s32[3]{0:T(128)S(1)} %pad_add_fusion.refs_0_, bf16[720,640]{1,0:T(8,128)(2,1)S(1)} %bitcast.18, bf16[720,640]{1,0:T(8,128)(2,1)S(1)} %collective-permute-done.2.refs_2_, ...), custom_call_target="tpu_custom_call" | custom-call | tf_op jit(solution)/shard_map/pallas_call | solution.py:145
  12.5 2.0 %collective-permute-done.5.refs_2_.refs_0_ = bf16[256,640]{1,0:T(8,128)(2,1)S(1)} collective-permute-done((bf16[256,640]{1,0:T(8,128)(2,1)}, bf16[256,640]{1,0:T(8,128)(2,1)S(1)}, u32[]{:S(2)}, u32[]{:S(2)}) %collective-permute-start.5) | collective-permute-done | bytes 327712 | tf_op jit(solution)/shard_map/ppermute | solution.py:134
  14.5 1.1 %shard_map.95.refs_1_.refs_2_.refs_0_ = bf16[768,1920]{1,0:T(8,128)(2,1)S(1)} custom-call(bf16[768,256]{1,0:T(8,128)(2,1)S(1)} %get-tuple-element.41.refs_0_, bf16[256,640]{1,0:T(8,128)(2,1)S(1)} %bitcast.21, bf16[256,640]{1,0:T(8,128)(2,1)S(1)} %collective-permute-done.5.refs_2_.refs_0_, bf16[256,640]{1,0:T(8,128)(2,1)S(1)} %collective-permute-done.6.refs_3_.refs_1_), custom_call_target="tpu_custom_call" | custom-call | tf_op jit(solution)/shard_map/pallas_call | solution.py:145
  15.8 1.9 %collective-permute-start.9 = (bf16[128,640]{1,0:T(8,128)(2,1)S(1)}, bf16[128,640]{1,0:T(8,128)(2,1)S(1)}, u32[]{:S(2)}, u32[]{:S(2)}) collective-permute-start(bf16[128,640]{1,0:T(8,128)(2,1)S(1)} %slice.17), channel_id=1, source_target_pairs={{0,2},{1,3},{2,0},{3,1},{4,6},{5,7},{6,4},{7,5},{8,10},{9,11},{10,... | collective-permute-start | bytes 491528 | tf_op jit(solution)/shard_map/ppermute | solution.py:134
  17.7 2.6 %shard_map.96 = (f32[256,640]{1,0:T(8,128)S(1)}, bf16[256,640]{1,0:T(8,128)(2,1)S(1)}, bf16[256,640]{1,0:T(8,128)(2,1)S(1)}) custom-call(bf16[1920,640]{1,0:T(8,128)(2,1)S(1)} %get-tuple-element.40.refs_0_.refs_1_, bf16[768,1920]{1,0:T(8,128)(2,1)S(1)} %shard_map.95.refs_1_.refs_2_.refs_0_), custom_call_target="tpu_custom_call" | custom-call | tf_op jit(solution)/shard_map/pallas_call | solution.py:145
  20.3 1.2 %collective-permute-done.4.refs_1_ = bf16[256,640]{1,0:T(8,128)(2,1)S(1)} collective-permute-done((bf16[256,640]{1,0:T(8,128)(2,1)S(1)}, bf16[256,640]{1,0:T(8,128)(2,1)S(1)}, u32[]{:S(2)}, u32[]{:S(2)}) %collective-permute-start.4) | collective-permute-done | bytes 327712 | tf_op jit(solution)/shard_map/ppermute | solution.py:134
  21.6 1.6 %collective-permute-start.7 = (bf16[128,640]{1,0:T(8,128)(2,1)S(1)}, bf16[128,640]{1,0:T(8,128)(2,1)S(1)}, u32[]{:S(2)}, u32[]{:S(2)}) collective-permute-start(bf16[128,640]{1,0:T(8,128)(2,1)S(1)} %slice.15), channel_id=1, source_target_pairs={{0,2},{1,3},{2,0},{3,1},{4,6},{5,7},{6,4},{7,5},{8,10},{9,11},{10,... | collective-permute-start | bytes 491528 | tf_op jit(solution)/shard_map/ppermute | solution.py:134
  23.6 2.5 %shard_map.99.refs_3_.refs_5_.refs_4_ = f32[1920,640]{1,0:T(8,128)S(1)} custom-call(bf16[768,1920]{1,0:T(8,128)(2,1)S(1)} %shard_map.95.refs_1_.refs_2_.refs_0_, bf16[256,640]{1,0:T(8,128)(2,1)S(1)} %get-tuple-element.39.refs_1_.refs_2_, bf16[256,640]{1,0:T(8,128)(2,1)S(1)} %get-tuple-element.43.refs_2_.refs_3_, ...), custom_call_target="tpu_custom_call" | custom-call | tf_op jit(solution)/shard_map/pallas_call | solution.py:145
  26.6 1.1 %collective-permute-done.7.refs_2_.refs_1_.refs_5_ = bf16[128,640]{1,0:T(8,128)(2,1)S(1)} collective-permute-done((bf16[128,640]{1,0:T(8,128)(2,1)S(1)}, bf16[128,640]{1,0:T(8,128)(2,1)S(1)}, u32[]{:S(2)}, u32[]{:S(2)}) %collective-permute-start.7) | collective-permute-done | bytes 163872 | tf_op jit(solution)/shard_map/ppermute | solution.py:134
  28.5 1.5 %shard_map.102 = bf16[720,640]{1,0:T(8,128)(2,1)S(1)} custom-call(s32[3]{0:T(128)S(1)} %pad_add_fusion.refs_0_, bf16[128,640]{1,0:T(8,128)(2,1)S(1)} %collective-permute-done.7.refs_2_.refs_1_.refs_5_, bf16[128,640]{1,0:T(8,128)(2,1)S(1)} %collective-permute-done.8.refs_3_.refs_2_.refs_6_, bf16[256,1920]{1,0:T(8,128)(2,1)S(1)} %shard_map.100.refs_4_.refs_3_, ...), custom_call_target="tpu_custom_call" | custom-call | tf_op jit(solution)/shard_map/pallas_call | solution.py:145
  30.1 2.3 %shard_map.101 = (f32[720,640]{1,0:T(8,128)S(1)}, bf16[256,640]{1,0:T(8,128)(2,1)S(1)}) custom-call(s32[3]{0:T(128)S(1)} %pad_add_fusion.refs_0_, bf16[1920,640]{1,0:T(8,128)(2,1)S(1)} %get-tuple-element.40.refs_0_.refs_1_, bf16[128,640]{1,0:T(8,128)(2,1)S(1)} %collective-permute-done.7.refs_2_.refs_1_.refs_5_, ...), custom_call_target="tpu_custom_call" | custom-call | tf_op jit(solution)/shard_map/pallas_call | solution.py:145
  32.7 2.7 %collective-permute-start.19 = (bf16[720,640]{1,0:T(8,128)(2,1)S(1)}, bf16[720,640]{1,0:T(8,128)(2,1)S(1)}, u32[]{:S(2)}, u32[]{:S(2)}) collective-permute-start(bf16[720,640]{1,0:T(8,128)(2,1)S(1)} %shard_map.103.refs_7_.refs_2_.refs_3_.refs_1_), channel_id=1, source_target_pairs={{0,16},{8,24},{16,0},{24,8},{1,17},{9,25},{17,1},{25,9},{2,18},{10... | collective-permute-start | bytes 2764808 | tf_op jit(solution)/shard_map/ppermute | solution.py:134
  35.4 1.6 %collective-permute-start.18 = (bf16[720,640]{1,0:T(8,128)(2,1)S(1)}, bf16[720,640]{1,0:T(8,128)(2,1)}, u32[]{:S(2)}, u32[]{:S(2)}) collective-permute-start(bf16[720,640]{1,0:T(8,128)(2,1)S(1)} %shard_map.103.refs_7_.refs_2_.refs_3_.refs_1_), channel_id=1, source_target_pairs={{0,8},{8,0},{16,24},{24,16},{1,9},{9,1},{17,25},{25,17},{2,10},{10... | collective-permute-start | bytes 2764808 | tf_op jit(solution)/shard_map/ppermute | solution.py:134
  38.3 2.2 %collective-permute-start.16 = (bf16[256,640]{1,0:T(8,128)(2,1)S(1)}, bf16[256,640]{1,0:T(8,128)(2,1)S(1)}, u32[]{:S(2)}, u32[]{:S(2)}) collective-permute-start(bf16[256,640]{1,0:T(8,128)(2,1)S(1)} %get-tuple-element.59), channel_id=1, source_target_pairs={{0,6},{1,7},{2,4},{3,5},{4,2},{5,3},{6,0},{7,1},{8,14},{9,15},{10,... | collective-permute-start | bytes 983048 | tf_op jit(solution)/shard_map/ppermute | solution.py:134
  40.5 4.8 %shard_map.104 = (f32[256,640]{1,0:T(8,128)S(1)}, bf16[256,640]{1,0:T(8,128)(2,1)S(1)}, bf16[256,640]{1,0:T(8,128)(2,1)S(1)}, bf16[256,640]{1,0:T(8,128)(2,1)S(1)}) custom-call(bf16[768,256]{1,0:T(8,128)(2,1)S(1)} %get-tuple-element.37.refs_0_, bf16[1920,640]{1,0:T(8,128)(2,1)S(1)} %get-tuple-element.38.refs_1_, ...), custom_call_target="tpu_custom_call" | custom-call | tf_op jit(solution)/shard_map/pallas_call | solution.py:145
  45.3 2.3 %collective-permute-done.14.refs_4_ = bf16[256,640]{1,0:T(8,128)(2,1)S(1)} collective-permute-done((bf16[256,640]{1,0:T(8,128)(2,1)S(1)}, bf16[256,640]{1,0:T(8,128)(2,1)S(1)}, u32[]{:S(2)}, u32[]{:S(2)}) %collective-permute-start.14) | collective-permute-done | bytes 327712 | tf_op jit(solution)/shard_map/ppermute | solution.py:134
  48.4 5.8 %collective-permute-done.15.refs_5_ = bf16[256,640]{1,0:T(8,128)(2,1)S(1)} collective-permute-done((bf16[256,640]{1,0:T(8,128)(2,1)S(1)}, bf16[256,640]{1,0:T(8,128)(2,1)S(1)}, u32[]{:S(2)}, u32[]{:S(2)}) %collective-permute-start.15) | collective-permute-done | bytes 327712 | tf_op jit(solution)/shard_map/ppermute | solution.py:134
  54.6 2.1 %shard_map.107 = (bf16[256,640]{1,0:T(8,128)(2,1)}, f32[2,640]{1,0:T(2,128)S(1)}) custom-call(bf16[256,640]{1,0:T(8,128)(2,1)S(1)} %bitcast.16, f32[2,640]{1,0:T(2,128)S(1)} %get-tuple-element.36.refs_3_.refs_1_, f32[2,640]{1,0:T(2,128)S(1)} %pad_maximum_fusion.refs_1_.refs_2_, f32[256,640]{1,0:T(8,128)S(1)} %get-tuple-element.42.refs_2_.refs_3_, ...), custom_call_target="tpu_custom_call" | custom-call | tf_op jit(solution)/shard_map/pallas_call | solution.py:145
  56.7 1.4 %collective-permute-start.20 = (f32[2,640]{1,0:T(2,128)S(1)}, f32[2,640]{1,0:T(2,128)S(1)}, u32[]{:S(2)}, u32[]{:S(2)}) collective-permute-start(f32[2,640]{1,0:T(2,128)S(1)} %get-tuple-element.60.refs_1_), channel_id=1, source_target_pairs={{0,2},{1,3},{2,0},{3,1},{4,6},{5,7},{6,4},{7,5},{8,10},{9,11},{10,... | collective-permute-start | bytes 15368 | tf_op jit(solution)/shard_map/ppermute | solution.py:134
  58.1 2.5 %collective-permute-done.20 = f32[2,640]{1,0:T(2,128)S(1)} collective-permute-done((f32[2,640]{1,0:T(2,128)S(1)}, f32[2,640]{1,0:T(2,128)S(1)}, u32[]{:S(2)}, u32[]{:S(2)}) %collective-permute-start.20) | collective-permute-done | bytes 5152 | tf_op jit(solution)/shard_map/ppermute | solution.py:134
  60.6 2.6 %collective-permute-start.17 = (bf16[256,640]{1,0:T(8,128)(2,1)S(1)}, bf16[256,640]{1,0:T(8,128)(2,1)S(1)}, u32[]{:S(2)}, u32[]{:S(2)}) collective-permute-start(bf16[256,640]{1,0:T(8,128)(2,1)S(1)} %shard_map.108), channel_id=1, source_target_pairs={{0,6},{1,7},{2,4},{3,5},{4,2},{5,3},{6,0},{7,1},{8,14},{9,15},{10,... | collective-permute-start | bytes 983048 | tf_op jit(solution)/shard_map/ppermute | solution.py:134
  63.3 4.1 %collective-permute-done.21 = f32[2,640]{1,0:T(2,128)S(1)} collective-permute-done((f32[2,640]{1,0:T(2,128)S(1)}, f32[2,640]{1,0:T(2,128)S(1)}, u32[]{:S(2)}, u32[]{:S(2)}) %collective-permute-start.21) | collective-permute-done | bytes 5152 | tf_op jit(solution)/shard_map/ppermute | solution.py:134
  68.8 1.4 %collective-permute-done.17.refs_3_ = bf16[256,640]{1,0:T(8,128)(2,1)S(1)} collective-permute-done((bf16[256,640]{1,0:T(8,128)(2,1)S(1)}, bf16[256,640]{1,0:T(8,128)(2,1)S(1)}, u32[]{:S(2)}, u32[]{:S(2)}) %collective-permute-start.17) | collective-permute-done | bytes 327712 | tf_op jit(solution)/shard_map/ppermute | solution.py:134
  70.2 1.1 %copy-done.5 = f32[256,640]{1,0:T(8,128)S(1)} copy-done((f32[256,640]{1,0:T(8,128)S(1)}, f32[256,640]{1,0:T(8,128)}, u32[]{:S(2)}) %copy-start.5) | copy-done | bytes 655384
  72.2 1.0 %copy-done = bf16[256,640]{1,0:T(8,128)(2,1)S(1)} copy-done((bf16[256,640]{1,0:T(8,128)(2,1)S(1)}, bf16[256,640]{1,0:T(8,128)(2,1)}, u32[]{:S(2)}) %copy-start) | copy-done | bytes 327704
  73.1 4.5 %conditional.1 = (f32[1,2,640]{2,1,0:T(2,128)S(1)}) conditional(s32[]{:T(128)} %bitcast.11, f32[2,640]{1,0:T(2,128)S(1)} %shard_map.112, f32[2,640]{1,0:T(2,128)S(1)} %shard_map.112), branch_computations={%region_0.1_spmd, %region_1.2_spmd} | conditional | flops 2560 | bytes 35888 | solution.py:468
  73.5 4.1 %collective-permute-done = f32[2,640]{1,0:T(2,128)S(1)} collective-permute-done((f32[2,640]{1,0:T(2,128)S(1)}, f32[2,640]{1,0:T(2,128)S(1)}, u32[]{:S(2)}, u32[]{:S(2)}) %collective-permute-start) | collective-permute-done | bytes 5152 | tf_op jit(solution)/shard_map/cond/branch_0_fun/ppermute | solution.py:134
  77.7 3.2 %shard_map.110 = f32[720,640]{1,0:T(8,128)} custom-call(s32[1]{0:T(128)} %get-tuple-element.63.refs_0_, bf16[720,640]{1,0:T(8,128)(2,1)S(1)} %shard_map.103.refs_7_.refs_2_.refs_3_.refs_1_, bf16[720,640]{1,0:T(8,128)(2,1)} %collective-permute-done.18.refs_2_, bf16[720,640]{1,0:T(8,128)(2,1)S(1)} %collective-permute-done.19.refs_3_), custom_call_target="tpu_custom_call" | custom-call | tf_op jit(solution)/shard_map/pallas_call | solution.py:145
  (62 shorter events, 10.1 us)
Async XLA Ops:
  0.6 8.5 %collective-permute-start.2 = (bf16[720,640]{1,0:T(8,128)(2,1)}, bf16[720,640]{1,0:T(8,128)(2,1)S(1)}, u32[]{:S(2)}, u32[]{:S(2)}) collective-permute-start(bf16[720,640]{1,0:T(8,128)(2,1)} %bitcast.17), channel_id=1, source_target_pairs={{0,1},{1,0},{2,3},{3,2},{4,5},{5,4},{6,7},{7,6},{8,9},{9,8},{10,11... | collective-permute-start | bytes 2764808 | tf_op jit(solution)/shard_map/ppermute | solution.py:134
  1.1 11.4 %collective-permute-start.6 = (bf16[256,640]{1,0:T(8,128)(2,1)}, bf16[256,640]{1,0:T(8,128)(2,1)S(1)}, u32[]{:S(2)}, u32[]{:S(2)}) collective-permute-start(bf16[256,640]{1,0:T(8,128)(2,1)} %bitcast.19), channel_id=1, source_target_pairs={{0,4},{1,5},{2,6},{3,7},{4,0},{5,1},{6,2},{7,3},{8,12},{9,13},{10,... | collective-permute-start | bytes 983048 | tf_op jit(solution)/shard_map/ppermute | solution.py:134
  3.7 10.8 %collective-permute-start.5 = (bf16[256,640]{1,0:T(8,128)(2,1)}, bf16[256,640]{1,0:T(8,128)(2,1)S(1)}, u32[]{:S(2)}, u32[]{:S(2)}) collective-permute-start(bf16[256,640]{1,0:T(8,128)(2,1)} %bitcast.20), channel_id=1, source_target_pairs={{0,2},{1,3},{2,0},{3,1},{4,6},{5,7},{6,4},{7,5},{8,10},{9,11},{10,... | collective-permute-start | bytes 983048 | tf_op jit(solution)/shard_map/ppermute | solution.py:134
  5.9 1.0 %copy-start.1 = (bf16[1,16,16,640]{3,2,1,0:T(8,128)(2,1)S(1)}, bf16[1,16,16,640]{3,2,1,0:T(8,128)(2,1)}, u32[]{:S(2)}) copy-start(bf16[1,16,16,640]{3,2,1,0:T(8,128)(2,1)} %param.8) | copy-start | bytes 983044
  6.9 7.6 %copy-start.6 = (bf16[1,16,16,640]{3,2,1,0:T(8,128)(2,1)S(1)}, bf16[1,16,16,640]{3,2,1,0:T(8,128)(2,1)}, u32[]{:S(2)}) copy-start(bf16[1,16,16,640]{3,2,1,0:T(8,128)(2,1)} %param.9) | copy-start | bytes 983044
  8.4 13.1 %collective-permute-start.4 = (bf16[256,640]{1,0:T(8,128)(2,1)S(1)}, bf16[256,640]{1,0:T(8,128)(2,1)S(1)}, u32[]{:S(2)}, u32[]{:S(2)}) collective-permute-start(bf16[256,640]{1,0:T(8,128)(2,1)S(1)} %get-tuple-element.39.refs_1_.refs_2_), channel_id=1, source_target_pairs={{0,2},{1,3},{2,0},{3,1},{4,6},{5,7},{6,4},{7,5},{8,10},{9,11},{10,... | collective-permute-start | bytes 983048 | tf_op jit(solution)/shard_map/ppermute | solution.py:134
  9.0 12.5 %collective-permute-start.3 = (bf16[256,640]{1,0:T(8,128)(2,1)S(1)}, bf16[256,640]{1,0:T(8,128)(2,1)S(1)}, u32[]{:S(2)}, u32[]{:S(2)}) collective-permute-start(bf16[256,640]{1,0:T(8,128)(2,1)S(1)} %get-tuple-element.39.refs_1_.refs_2_), channel_id=1, source_target_pairs={{0,4},{1,5},{2,6},{3,7},{4,0},{5,1},{6,2},{7,3},{8,12},{9,13},{10,... | collective-permute-start | bytes 983048 | tf_op jit(solution)/shard_map/ppermute | solution.py:134
  9.2 1.2 %copy-start.3 = (bf16[1,720,640]{2,1,0:T(8,128)(2,1)S(1)}, bf16[1,720,640]{2,1,0:T(8,128)(2,1)}, u32[]{:S(2)}) copy-start(bf16[1,720,640]{2,1,0:T(8,128)(2,1)} %param.10) | copy-start | bytes 2764804
  15.7 10.5 %collective-permute-start.10 = (bf16[128,640]{1,0:T(8,128)(2,1)S(1)}, bf16[128,640]{1,0:T(8,128)(2,1)S(1)}, u32[]{:S(2)}, u32[]{:S(2)}) collective-permute-start(bf16[128,640]{1,0:T(8,128)(2,1)S(1)} %slice.18), channel_id=1, source_target_pairs={{0,4},{1,5},{2,6},{3,7},{4,0},{5,1},{6,2},{7,3},{8,12},{9,13},{10,... | collective-permute-start | bytes 491528 | tf_op jit(solution)/shard_map/ppermute | solution.py:134
  15.8 10.4 %collective-permute-start.9 = (bf16[128,640]{1,0:T(8,128)(2,1)S(1)}, bf16[128,640]{1,0:T(8,128)(2,1)S(1)}, u32[]{:S(2)}, u32[]{:S(2)}) collective-permute-start(bf16[128,640]{1,0:T(8,128)(2,1)S(1)} %slice.17), channel_id=1, source_target_pairs={{0,2},{1,3},{2,0},{3,1},{4,6},{5,7},{6,4},{7,5},{8,10},{9,11},{10,... | collective-permute-start | bytes 491528 | tf_op jit(solution)/shard_map/ppermute | solution.py:134
  21.6 6.2 %collective-permute-start.7 = (bf16[128,640]{1,0:T(8,128)(2,1)S(1)}, bf16[128,640]{1,0:T(8,128)(2,1)S(1)}, u32[]{:S(2)}, u32[]{:S(2)}) collective-permute-start(bf16[128,640]{1,0:T(8,128)(2,1)S(1)} %slice.15), channel_id=1, source_target_pairs={{0,2},{1,3},{2,0},{3,1},{4,6},{5,7},{6,4},{7,5},{8,10},{9,11},{10,... | collective-permute-start | bytes 491528 | tf_op jit(solution)/shard_map/ppermute | solution.py:134
  23.1 5.3 %collective-permute-start.8 = (bf16[128,640]{1,0:T(8,128)(2,1)S(1)}, bf16[128,640]{1,0:T(8,128)(2,1)S(1)}, u32[]{:S(2)}, u32[]{:S(2)}) collective-permute-start(bf16[128,640]{1,0:T(8,128)(2,1)S(1)} %slice.16), channel_id=1, source_target_pairs={{0,4},{1,5},{2,6},{3,7},{4,0},{5,1},{6,2},{7,3},{8,12},{9,13},{10,... | collective-permute-start | bytes 491528 | tf_op jit(solution)/shard_map/ppermute | solution.py:134
  30.0 2.5 %collective-permute-start.11 = (bf16[720,640]{1,0:T(8,128)(2,1)S(1)}, bf16[720,640]{1,0:T(8,128)(2,1)S(1)}, u32[]{:S(2)}, u32[]{:S(2)}) collective-permute-start(bf16[720,640]{1,0:T(8,128)(2,1)S(1)} %shard_map.102), channel_id=1, source_target_pairs={{0,1},{1,0},{2,3},{3,2},{4,5},{5,4},{6,7},{7,6},{8,9},{9,8},{10,11... | collective-permute-start | bytes 2764808 | tf_op jit(solution)/shard_map/ppermute | solution.py:134
  32.7 45.0 %collective-permute-start.19 = (bf16[720,640]{1,0:T(8,128)(2,1)S(1)}, bf16[720,640]{1,0:T(8,128)(2,1)S(1)}, u32[]{:S(2)}, u32[]{:S(2)}) collective-permute-start(bf16[720,640]{1,0:T(8,128)(2,1)S(1)} %shard_map.103.refs_7_.refs_2_.refs_3_.refs_1_), channel_id=1, source_target_pairs={{0,16},{8,24},{16,0},{24,8},{1,17},{9,25},{17,1},{25,9},{2,18},{10... | collective-permute-start | bytes 2764808 | tf_op jit(solution)/shard_map/ppermute | solution.py:134
  35.4 42.3 %collective-permute-start.18 = (bf16[720,640]{1,0:T(8,128)(2,1)S(1)}, bf16[720,640]{1,0:T(8,128)(2,1)}, u32[]{:S(2)}, u32[]{:S(2)}) collective-permute-start(bf16[720,640]{1,0:T(8,128)(2,1)S(1)} %shard_map.103.refs_7_.refs_2_.refs_3_.refs_1_), channel_id=1, source_target_pairs={{0,8},{8,0},{16,24},{24,16},{1,9},{9,1},{17,25},{25,17},{2,10},{10... | collective-permute-start | bytes 2764808 | tf_op jit(solution)/shard_map/ppermute | solution.py:134
  37.0 10.6 %collective-permute-start.14 = (bf16[256,640]{1,0:T(8,128)(2,1)S(1)}, bf16[256,640]{1,0:T(8,128)(2,1)S(1)}, u32[]{:S(2)}, u32[]{:S(2)}) collective-permute-start(bf16[256,640]{1,0:T(8,128)(2,1)S(1)} %get-tuple-element.57), channel_id=1, source_target_pairs={{0,2},{1,3},{2,0},{3,1},{4,6},{5,7},{6,4},{7,5},{8,10},{9,11},{10,... | collective-permute-start | bytes 983048 | tf_op jit(solution)/shard_map/ppermute | solution.py:134
  37.8 16.4 %collective-permute-start.15 = (bf16[256,640]{1,0:T(8,128)(2,1)S(1)}, bf16[256,640]{1,0:T(8,128)(2,1)S(1)}, u32[]{:S(2)}, u32[]{:S(2)}) collective-permute-start(bf16[256,640]{1,0:T(8,128)(2,1)S(1)} %get-tuple-element.58), channel_id=1, source_target_pairs={{0,4},{1,5},{2,6},{3,7},{4,0},{5,1},{6,2},{7,3},{8,12},{9,13},{10,... | collective-permute-start | bytes 983048 | tf_op jit(solution)/shard_map/ppermute | solution.py:134
  38.3 16.3 %collective-permute-start.16 = (bf16[256,640]{1,0:T(8,128)(2,1)S(1)}, bf16[256,640]{1,0:T(8,128)(2,1)S(1)}, u32[]{:S(2)}, u32[]{:S(2)}) collective-permute-start(bf16[256,640]{1,0:T(8,128)(2,1)S(1)} %get-tuple-element.59), channel_id=1, source_target_pairs={{0,6},{1,7},{2,4},{3,5},{4,2},{5,3},{6,0},{7,1},{8,14},{9,15},{10,... | collective-permute-start | bytes 983048 | tf_op jit(solution)/shard_map/ppermute | solution.py:134
  40.5 14.1 %copy-start.2 = (bf16[1,16,16,640]{3,2,1,0:T(8,128)(2,1)S(1)}, bf16[1,16,16,640]{3,2,1,0:T(8,128)(2,1)}, u32[]{:S(2)}) copy-start(bf16[1,16,16,640]{3,2,1,0:T(8,128)(2,1)} %param.8) | copy-start | bytes 983044
  45.3 8.9 %copy-start.4 = (f32[256,640]{1,0:T(8,128)}, f32[256,640]{1,0:T(8,128)S(1)}, u32[]{:S(2)}) copy-start(f32[256,640]{1,0:T(8,128)S(1)} %get-tuple-element.48.refs_0_) | copy-start | bytes 1966084
  45.3 22.1 %copy-start.8 = (s32[8]{0:T(128)S(1)}, s32[8]{0:T(128)}, u32[]{:S(2)}) copy-start(s32[8]{0:T(128)} %param.13) | copy-start | bytes 100
  47.6 15.6 %collective-permute-start.12 = (bf16[256,640]{1,0:T(8,128)(2,1)S(1)}, bf16[256,640]{1,0:T(8,128)(2,1)S(1)}, u32[]{:S(2)}, u32[]{:S(2)}) collective-permute-start(bf16[256,640]{1,0:T(8,128)(2,1)S(1)} %get-tuple-element.51), channel_id=1, source_target_pairs={{0,2},{1,3},{2,0},{3,1},{4,6},{5,7},{6,4},{7,5},{8,10},{9,11},{10,... | collective-permute-start | bytes 983048 | tf_op jit(solution)/shard_map/ppermute | solution.py:134
  54.2 9.0 %collective-permute-start.13 = (bf16[256,640]{1,0:T(8,128)(2,1)S(1)}, bf16[256,640]{1,0:T(8,128)(2,1)S(1)}, u32[]{:S(2)}, u32[]{:S(2)}) collective-permute-start(bf16[256,640]{1,0:T(8,128)(2,1)S(1)} %get-tuple-element.52), channel_id=1, source_target_pairs={{0,4},{1,5},{2,6},{3,7},{4,0},{5,1},{6,2},{7,3},{8,12},{9,13},{10,... | collective-permute-start | bytes 983048 | tf_op jit(solution)/shard_map/ppermute | solution.py:134
  56.7 3.9 %collective-permute-start.20 = (f32[2,640]{1,0:T(2,128)S(1)}, f32[2,640]{1,0:T(2,128)S(1)}, u32[]{:S(2)}, u32[]{:S(2)}) collective-permute-start(f32[2,640]{1,0:T(2,128)S(1)} %get-tuple-element.60.refs_1_), channel_id=1, source_target_pairs={{0,2},{1,3},{2,0},{3,1},{4,6},{5,7},{6,4},{7,5},{8,10},{9,11},{10,... | collective-permute-start | bytes 15368 | tf_op jit(solution)/shard_map/ppermute | solution.py:134
  60.6 9.6 %collective-permute-start.17 = (bf16[256,640]{1,0:T(8,128)(2,1)S(1)}, bf16[256,640]{1,0:T(8,128)(2,1)S(1)}, u32[]{:S(2)}, u32[]{:S(2)}) collective-permute-start(bf16[256,640]{1,0:T(8,128)(2,1)S(1)} %shard_map.108), channel_id=1, source_target_pairs={{0,6},{1,7},{2,4},{3,5},{4,2},{5,3},{6,0},{7,1},{8,14},{9,15},{10,... | collective-permute-start | bytes 983048 | tf_op jit(solution)/shard_map/ppermute | solution.py:134
  63.2 4.2 %collective-permute-start.21 = (f32[2,640]{1,0:T(2,128)S(1)}, f32[2,640]{1,0:T(2,128)S(1)}, u32[]{:S(2)}, u32[]{:S(2)}) collective-permute-start(f32[2,640]{1,0:T(2,128)S(1)} %shard_map.111), channel_id=1, source_target_pairs={{0,4},{1,5},{2,6},{3,7},{4,0},{5,1},{6,2},{7,3},{8,12},{9,13},{10,... | collective-permute-start | bytes 15368 | tf_op jit(solution)/shard_map/ppermute | solution.py:134
  67.4 1.3 %collective-permute-start.22 = (f32[2,640]{1,0:T(2,128)S(1)}, f32[2,640]{1,0:T(2,128)S(1)}, u32[]{:S(2)}, u32[]{:S(2)}) collective-permute-start(f32[2,640]{1,0:T(2,128)S(1)} %add.35), channel_id=1, source_target_pairs={{0,1},{1,0},{2,3},{3,2},{4,5},{5,4},{6,7},{7,6},{8,9},{9,8},{10,11... | collective-permute-start | bytes 15368 | tf_op jit(solution)/shard_map/ppermute | solution.py:134
  70.2 1.1 %copy-start.5 = (f32[256,640]{1,0:T(8,128)S(1)}, f32[256,640]{1,0:T(8,128)}, u32[]{:S(2)}) copy-start(f32[256,640]{1,0:T(8,128)} %copy-done.4) | copy-start | bytes 1966084
  72.2 1.0 %copy-start = (bf16[256,640]{1,0:T(8,128)(2,1)S(1)}, bf16[256,640]{1,0:T(8,128)(2,1)}, u32[]{:S(2)}) copy-start(bf16[256,640]{1,0:T(8,128)(2,1)} %shard_map.109.refs_1_) | copy-start | bytes 983044
  73.1 4.5 %collective-permute-start = (f32[2,640]{1,0:T(2,128)S(1)}, f32[2,640]{1,0:T(2,128)S(1)}, u32[]{:S(2)}, u32[]{:S(2)}) collective-permute-start(f32[2,640]{1,0:T(2,128)S(1)} %param), channel_id=1, source_target_pairs={{0,16},{8,24},{16,0},{24,8},{1,17},{9,25},{17,1},{25,9},{2,18},{10... | collective-permute-start | bytes 15368 | tf_op jit(solution)/shard_map/cond/branch_0_fun/ppermute | solution.py:134
  77.7 3.2 %copy-start.7 = (f32[1,2,640]{2,1,0:T(2,128)}, f32[1,2,640]{2,1,0:T(2,128)S(1)}, u32[]{:S(2)}) copy-start(f32[1,2,640]{2,1,0:T(2,128)S(1)} %get-tuple-element.64) | copy-start | bytes 15364

commit v2 on v0

--- a/solution.py
+++ b/solution.py
@@ -325,15 +325,26 @@
     narrow[...] = (keep[...] + got[...].astype(F32)).astype(BF16)
 
 
-def pair_kernel(chunks, bit, own, pair1, pair2, mean, made, leave):
+def pair_kernel(chunks, bit, own, pair1, pair2, mean, made, got, arrive, leave):
     size = own.shape[0] // chunks
+    parts = [pl.ds(index * size, size) for index in range(chunks)]
+
+    def fetch(index):
+        rows = parts[index]
+        return pltpu.make_async_copy(pair1.at[rows], got.at[rows], arrive.at[index])
+
+    @pl.when(bit[0] == 0)
+    def _():
+        for index in range(chunks):
+            fetch(index).start()
+
     stores = []
-    for index in range(chunks):
-        rows = pl.ds(index * size, size)
+    for index, rows in enumerate(parts):
 
         @pl.when(bit[0] == 0)
         def _():
-            made[rows, :] = 0.5 * (own[rows, :].astype(F32) + pair1[rows, :].astype(F32))
+            fetch(index).wait()
+            made[rows, :] = 0.5 * (own[rows, :].astype(F32) + got[rows, :].astype(F32))
 
         @pl.when(bit[0] != 0)
         def _():
@@ -343,6 +354,10 @@
         stores[-1].start()
     for store in stores:
         store.wait()
+
+
+def copy_kernel(source, target):
+    target[...] = source[...]
 
 
 def back_kernel(groups, factor, latent, stats, params, g0, g1, g2, g3, grad, terms):
@@ -473,11 +488,17 @@
     )
     shard_bit = lax.dynamic_slice_in_dim(partner_bit, place, 1)
     (weight_avg,) = call(
-        functools.partial(pair_kernel, 5),
+        functools.partial(pair_kernel, 9),
         [shaped((rows, chans), F32)],
         [shard_bit, narrow, pair1, pair2],
-        [pltpu.VMEM((rows, chans), F32), pltpu.SemaphoreType.DMA((5,))],
+        [
+            pltpu.VMEM((rows, chans), F32),
+            pltpu.VMEM((rows, chans), BF16),
+            pltpu.SemaphoreType.DMA((9,)),
+            pltpu.SemaphoreType.DMA((9,)),
+        ],
         copies_out=True,
+        outside=(2,),
     )
     shape = (1, side, side, chans)
     return (block_out.reshape(shape), input_grad.reshape(shape), weight_avg[None], norm_avg[None])

time: 81 us -> 80.3 us (level)
  no operation moved by 1% of the time
where the time goes in v2:
time: 80.3 us; the launch traced here: 80 us
  waiting for transfers between devices  25.1 us (31%)
  Pallas kernels  24.8 us (31%)
  starting transfers between devices  22.6 us (28%)
  local copies, waits for them, and re-layouts  4.97 us (6%)
  between operations  1.7 us (2%)
    ppermute x22, waiting for transfers between devices, swap(): return lax.ppermute(value, axis, pairs)  25.1 us
    pallas_call x13, Pallas kernels, call(): pl.pallas_call(body, out_shape=tuple(outs), in_specs=[untouched if index...  24.8 us
    ppermute x22, starting transfers between devices, swap(): return lax.ppermute(value, axis, pairs)  22.6 us
    unnamed x18, local copies, waits for them, and re-layouts  4.23 us
  transfers between devices with their start and end apart: 22, of which 13 were waited for; matrix products, arithmetic and copies ran while one was open for 2% of the time, Pallas kernels for 25%

profile of v2, /device:TPU:0, one launch (start us, length us, event | category | flops | bytes accessed | tf_op | source)
XLA Modules:
  0.0 80.0 jit_solution(5263138012639050980)
XLA Ops:
  1.1 2.6 %collective-permute-start.6 = (bf16[256,640]{1,0:T(8,128)(2,1)}, bf16[256,640]{1,0:T(8,128)(2,1)S(1)}, u32[]{:S(2)}, u32[]{:S(2)}) collective-permute-start(bf16[256,640]{1,0:T(8,128)(2,1)} %bitcast.19), channel_id=1, source_target_pairs={{0,4},{1,5},{2,6},{3,7},{4,0},{5,1},{6,2},{7,3},{8,12},{9,13},{10,... | collective-permute-start | bytes 983048 | tf_op jit(solution)/shard_map/ppermute | solution.py:134
  3.7 1.5 %collective-permute-start.5 = (bf16[256,640]{1,0:T(8,128)(2,1)}, bf16[256,640]{1,0:T(8,128)(2,1)S(1)}, u32[]{:S(2)}, u32[]{:S(2)}) collective-permute-start(bf16[256,640]{1,0:T(8,128)(2,1)} %bitcast.20), channel_id=1, source_target_pairs={{0,2},{1,3},{2,0},{3,1},{4,6},{5,7},{6,4},{7,5},{8,10},{9,11},{10,... | collective-permute-start | bytes 983048 | tf_op jit(solution)/shard_map/ppermute | solution.py:134
  6.9 1.5 %shard_map.93 = (bf16[256,640]{1,0:T(8,128)(2,1)S(1)}, f32[2,640]{1,0:T(2,128)S(1)}) custom-call(bf16[256,640]{1,0:T(8,128)(2,1)S(1)} %bitcast.15, f32[2,640]{1,0:T(2,128)S(1)} %pad_maximum_fusion.refs_1_.refs_2_), custom_call_target="tpu_custom_call" | custom-call | tf_op jit(solution)/shard_map/pallas_call | solution.py:145
  9.2 1.2 %copy-done.3 = bf16[1,720,640]{2,1,0:T(8,128)(2,1)S(1)} copy-done((bf16[1,720,640]{2,1,0:T(8,128)(2,1)S(1)}, bf16[1,720,640]{2,1,0:T(8,128)(2,1)}, u32[]{:S(2)}) %copy-start.3) | copy-done | bytes 921624
  10.3 1.9 %shard_map.94 = (bf16[1920,640]{1,0:T(8,128)(2,1)S(1)}, bf16[1920,640]{1,0:T(8,128)(2,1)S(1)}, bf16[768,256]{1,0:T(8,128)(2,1)S(1)}, bf16[768,256]{1,0:T(8,128)(2,1)S(1)}) custom-call(s32[3]{0:T(128)S(1)} %pad_add_fusion.refs_0_, bf16[720,640]{1,0:T(8,128)(2,1)S(1)} %bitcast.18, bf16[720,640]{1,0:T(8,128)(2,1)S(1)} %collective-permute-done.2.refs_2_, ...), custom_call_target="tpu_custom_call" | custom-call | tf_op jit(solution)/shard_map/pallas_call | solution.py:145
  12.5 2.0 %collective-permute-done.5.refs_2_.refs_0_ = bf16[256,640]{1,0:T(8,128)(2,1)S(1)} collective-permute-done((bf16[256,640]{1,0:T(8,128)(2,1)}, bf16[256,640]{1,0:T(8,128)(2,1)S(1)}, u32[]{:S(2)}, u32[]{:S(2)}) %collective-permute-start.5) | collective-permute-done | bytes 327712 | tf_op jit(solution)/shard_map/ppermute | solution.py:134
  14.5 1.1 %shard_map.95.refs_1_.refs_2_.refs_0_ = bf16[768,1920]{1,0:T(8,128)(2,1)S(1)} custom-call(bf16[768,256]{1,0:T(8,128)(2,1)S(1)} %get-tuple-element.41.refs_0_, bf16[256,640]{1,0:T(8,128)(2,1)S(1)} %bitcast.21, bf16[256,640]{1,0:T(8,128)(2,1)S(1)} %collective-permute-done.5.refs_2_.refs_0_, bf16[256,640]{1,0:T(8,128)(2,1)S(1)} %collective-permute-done.6.refs_3_.refs_1_), custom_call_target="tpu_custom_call" | custom-call | tf_op jit(solution)/shard_map/pallas_call | solution.py:145
  15.8 1.9 %collective-permute-start.9 = (bf16[128,640]{1,0:T(8,128)(2,1)S(1)}, bf16[128,640]{1,0:T(8,128)(2,1)S(1)}, u32[]{:S(2)}, u32[]{:S(2)}) collective-permute-start(bf16[128,640]{1,0:T(8,128)(2,1)S(1)} %slice.17), channel_id=1, source_target_pairs={{0,2},{1,3},{2,0},{3,1},{4,6},{5,7},{6,4},{7,5},{8,10},{9,11},{10,... | collective-permute-start | bytes 491528 | tf_op jit(solution)/shard_map/ppermute | solution.py:134
  17.7 2.6 %shard_map.96 = (f32[256,640]{1,0:T(8,128)S(1)}, bf16[256,640]{1,0:T(8,128)(2,1)S(1)}, bf16[256,640]{1,0:T(8,128)(2,1)S(1)}) custom-call(bf16[1920,640]{1,0:T(8,128)(2,1)S(1)} %get-tuple-element.40.refs_0_.refs_1_, bf16[768,1920]{1,0:T(8,128)(2,1)S(1)} %shard_map.95.refs_1_.refs_2_.refs_0_), custom_call_target="tpu_custom_call" | custom-call | tf_op jit(solution)/shard_map/pallas_call | solution.py:145
  20.3 1.2 %collective-permute-done.4.refs_1_ = bf16[256,640]{1,0:T(8,128)(2,1)S(1)} collective-permute-done((bf16[256,640]{1,0:T(8,128)(2,1)S(1)}, bf16[256,640]{1,0:T(8,128)(2,1)S(1)}, u32[]{:S(2)}, u32[]{:S(2)}) %collective-permute-start.4) | collective-permute-done | bytes 327712 | tf_op jit(solution)/shard_map/ppermute | solution.py:134
  21.6 1.6 %collective-permute-start.7 = (bf16[128,640]{1,0:T(8,128)(2,1)S(1)}, bf16[128,640]{1,0:T(8,128)(2,1)S(1)}, u32[]{:S(2)}, u32[]{:S(2)}) collective-permute-start(bf16[128,640]{1,0:T(8,128)(2,1)S(1)} %slice.15), channel_id=1, source_target_pairs={{0,2},{1,3},{2,0},{3,1},{4,6},{5,7},{6,4},{7,5},{8,10},{9,11},{10,... | collective-permute-start | bytes 491528 | tf_op jit(solution)/shard_map/ppermute | solution.py:134
  23.6 2.5 %shard_map.99.refs_3_.refs_5_.refs_4_ = f32[1920,640]{1,0:T(8,128)S(1)} custom-call(bf16[768,1920]{1,0:T(8,128)(2,1)S(1)} %shard_map.95.refs_1_.refs_2_.refs_0_, bf16[256,640]{1,0:T(8,128)(2,1)S(1)} %get-tuple-element.39.refs_1_.refs_2_, bf16[256,640]{1,0:T(8,128)(2,1)S(1)} %get-tuple-element.43.refs_2_.refs_3_, ...), custom_call_target="tpu_custom_call" | custom-call | tf_op jit(solution)/shard_map/pallas_call | solution.py:145
  26.6 1.1 %collective-permute-done.7.refs_2_.refs_1_.refs_5_ = bf16[128,640]{1,0:T(8,128)(2,1)S(1)} collective-permute-done((bf16[128,640]{1,0:T(8,128)(2,1)S(1)}, bf16[128,640]{1,0:T(8,128)(2,1)S(1)}, u32[]{:S(2)}, u32[]{:S(2)}) %collective-permute-start.7) | collective-permute-done | bytes 163872 | tf_op jit(solution)/shard_map/ppermute | solution.py:134
  28.5 1.5 %shard_map.102 = bf16[720,640]{1,0:T(8,128)(2,1)S(1)} custom-call(s32[3]{0:T(128)S(1)} %pad_add_fusion.refs_0_, bf16[128,640]{1,0:T(8,128)(2,1)S(1)} %collective-permute-done.7.refs_2_.refs_1_.refs_5_, bf16[128,640]{1,0:T(8,128)(2,1)S(1)} %collective-permute-done.8.refs_3_.refs_2_.refs_6_, bf16[256,1920]{1,0:T(8,128)(2,1)S(1)} %shard_map.100.refs_4_.refs_3_, ...), custom_call_target="tpu_custom_call" | custom-call | tf_op jit(solution)/shard_map/pallas_call | solution.py:145
  30.1 2.3 %shard_map.101 = (f32[720,640]{1,0:T(8,128)S(1)}, bf16[256,640]{1,0:T(8,128)(2,1)S(1)}) custom-call(s32[3]{0:T(128)S(1)} %pad_add_fusion.refs_0_, bf16[1920,640]{1,0:T(8,128)(2,1)S(1)} %get-tuple-element.40.refs_0_.refs_1_, bf16[128,640]{1,0:T(8,128)(2,1)S(1)} %collective-permute-done.7.refs_2_.refs_1_.refs_5_, ...), custom_call_target="tpu_custom_call" | custom-call | tf_op jit(solution)/shard_map/pallas_call | solution.py:145
  32.7 2.7 %collective-permute-start.19 = (bf16[720,640]{1,0:T(8,128)(2,1)S(1)}, bf16[720,640]{1,0:T(8,128)(2,1)S(1)}, u32[]{:S(2)}, u32[]{:S(2)}) collective-permute-start(bf16[720,640]{1,0:T(8,128)(2,1)S(1)} %shard_map.103.refs_7_.refs_2_.refs_3_.refs_1_), channel_id=1, source_target_pairs={{0,16},{8,24},{16,0},{24,8},{1,17},{9,25},{17,1},{25,9},{2,18},{10... | collective-permute-start | bytes 2764808 | tf_op jit(solution)/shard_map/ppermute | solution.py:134
  35.4 1.6 %collective-permute-start.18 = (bf16[720,640]{1,0:T(8,128)(2,1)S(1)}, bf16[720,640]{1,0:T(8,128)(2,1)}, u32[]{:S(2)}, u32[]{:S(2)}) collective-permute-start(bf16[720,640]{1,0:T(8,128)(2,1)S(1)} %shard_map.103.refs_7_.refs_2_.refs_3_.refs_1_), channel_id=1, source_target_pairs={{0,8},{8,0},{16,24},{24,16},{1,9},{9,1},{17,25},{25,17},{2,10},{10... | collective-permute-start | bytes 2764808 | tf_op jit(solution)/shard_map/ppermute | solution.py:134
  38.3 2.2 %collective-permute-start.16 = (bf16[256,640]{1,0:T(8,128)(2,1)S(1)}, bf16[256,640]{1,0:T(8,128)(2,1)S(1)}, u32[]{:S(2)}, u32[]{:S(2)}) collective-permute-start(bf16[256,640]{1,0:T(8,128)(2,1)S(1)} %get-tuple-element.59), channel_id=1, source_target_pairs={{0,6},{1,7},{2,4},{3,5},{4,2},{5,3},{6,0},{7,1},{8,14},{9,15},{10,... | collective-permute-start | bytes 983048 | tf_op jit(solution)/shard_map/ppermute | solution.py:134
  40.5 4.8 %shard_map.104 = (f32[256,640]{1,0:T(8,128)S(1)}, bf16[256,640]{1,0:T(8,128)(2,1)S(1)}, bf16[256,640]{1,0:T(8,128)(2,1)S(1)}, bf16[256,640]{1,0:T(8,128)(2,1)S(1)}) custom-call(bf16[768,256]{1,0:T(8,128)(2,1)S(1)} %get-tuple-element.37.refs_0_, bf16[1920,640]{1,0:T(8,128)(2,1)S(1)} %get-tuple-element.38.refs_1_, ...), custom_call_target="tpu_custom_call" | custom-call | tf_op jit(solution)/shard_map/pallas_call | solution.py:145
  45.3 2.3 %collective-permute-done.14.refs_4_ = bf16[256,640]{1,0:T(8,128)(2,1)S(1)} collective-permute-done((bf16[256,640]{1,0:T(8,128)(2,1)S(1)}, bf16[256,640]{1,0:T(8,128)(2,1)S(1)}, u32[]{:S(2)}, u32[]{:S(2)}) %collective-permute-start.14) | collective-permute-done | bytes 327712 | tf_op jit(solution)/shard_map/ppermute | solution.py:134
  48.4 5.8 %collective-permute-done.15.refs_5_ = bf16[256,640]{1,0:T(8,128)(2,1)S(1)} collective-permute-done((bf16[256,640]{1,0:T(8,128)(2,1)S(1)}, bf16[256,640]{1,0:T(8,128)(2,1)S(1)}, u32[]{:S(2)}, u32[]{:S(2)}) %collective-permute-start.15) | collective-permute-done | bytes 327712 | tf_op jit(solution)/shard_map/ppermute | solution.py:134
  54.6 2.1 %shard_map.107 = (bf16[256,640]{1,0:T(8,128)(2,1)}, f32[2,640]{1,0:T(2,128)S(1)}) custom-call(bf16[256,640]{1,0:T(8,128)(2,1)S(1)} %bitcast.16, f32[2,640]{1,0:T(2,128)S(1)} %get-tuple-element.36.refs_3_.refs_1_, f32[2,640]{1,0:T(2,128)S(1)} %pad_maximum_fusion.refs_1_.refs_2_, f32[256,640]{1,0:T(8,128)S(1)} %get-tuple-element.42.refs_2_.refs_3_, ...), custom_call_target="tpu_custom_call" | custom-call | tf_op jit(solution)/shard_map/pallas_call | solution.py:145
  56.7 1.4 %collective-permute-start.20 = (f32[2,640]{1,0:T(2,128)S(1)}, f32[2,640]{1,0:T(2,128)S(1)}, u32[]{:S(2)}, u32[]{:S(2)}) collective-permute-start(f32[2,640]{1,0:T(2,128)S(1)} %get-tuple-element.60.refs_1_), channel_id=1, source_target_pairs={{0,2},{1,3},{2,0},{3,1},{4,6},{5,7},{6,4},{7,5},{8,10},{9,11},{10,... | collective-permute-start | bytes 15368 | tf_op jit(solution)/shard_map/ppermute | solution.py:134
  58.1 2.5 %collective-permute-done.20 = f32[2,640]{1,0:T(2,128)S(1)} collective-permute-done((f32[2,640]{1,0:T(2,128)S(1)}, f32[2,640]{1,0:T(2,128)S(1)}, u32[]{:S(2)}, u32[]{:S(2)}) %collective-permute-start.20) | collective-permute-done | bytes 5152 | tf_op jit(solution)/shard_map/ppermute | solution.py:134
  60.6 2.6 %collective-permute-start.17 = (bf16[256,640]{1,0:T(8,128)(2,1)S(1)}, bf16[256,640]{1,0:T(8,128)(2,1)S(1)}, u32[]{:S(2)}, u32[]{:S(2)}) collective-permute-start(bf16[256,640]{1,0:T(8,128)(2,1)S(1)} %shard_map.108), channel_id=1, source_target_pairs={{0,6},{1,7},{2,4},{3,5},{4,2},{5,3},{6,0},{7,1},{8,14},{9,15},{10,... | collective-permute-start | bytes 983048 | tf_op jit(solution)/shard_map/ppermute | solution.py:134
  63.3 4.1 %collective-permute-done.21 = f32[2,640]{1,0:T(2,128)S(1)} collective-permute-done((f32[2,640]{1,0:T(2,128)S(1)}, f32[2,640]{1,0:T(2,128)S(1)}, u32[]{:S(2)}, u32[]{:S(2)}) %collective-permute-start.21) | collective-permute-done | bytes 5152 | tf_op jit(solution)/shard_map/ppermute | solution.py:134
  68.8 1.4 %collective-permute-done.17.refs_3_ = bf16[256,640]{1,0:T(8,128)(2,1)S(1)} collective-permute-done((bf16[256,640]{1,0:T(8,128)(2,1)S(1)}, bf16[256,640]{1,0:T(8,128)(2,1)S(1)}, u32[]{:S(2)}, u32[]{:S(2)}) %collective-permute-start.17) | collective-permute-done | bytes 327712 | tf_op jit(solution)/shard_map/ppermute | solution.py:134
  70.2 1.1 %copy-done.5 = f32[256,640]{1,0:T(8,128)S(1)} copy-done((f32[256,640]{1,0:T(8,128)S(1)}, f32[256,640]{1,0:T(8,128)}, u32[]{:S(2)}) %copy-start.5) | copy-done | bytes 655384
  72.2 1.0 %copy-done = bf16[256,640]{1,0:T(8,128)(2,1)S(1)} copy-done((bf16[256,640]{1,0:T(8,128)(2,1)S(1)}, bf16[256,640]{1,0:T(8,128)(2,1)}, u32[]{:S(2)}) %copy-start) | copy-done | bytes 327704
  73.1 3.6 %conditional.1 = (f32[1,2,640]{2,1,0:T(2,128)S(1)}) conditional(s32[]{:T(128)} %bitcast.11, f32[2,640]{1,0:T(2,128)S(1)} %shard_map.112, f32[2,640]{1,0:T(2,128)S(1)} %shard_map.112), branch_computations={%region_0.1_spmd, %region_1.2_spmd} | conditional | flops 2560 | bytes 35888 | solution.py:483
  73.6 3.2 %collective-permute-done.1 = f32[2,640]{1,0:T(2,128)S(1)} collective-permute-done((f32[2,640]{1,0:T(2,128)S(1)}, f32[2,640]{1,0:T(2,128)S(1)}, u32[]{:S(2)}, u32[]{:S(2)}) %collective-permute-start.1) | collective-permute-done | bytes 5152 | tf_op jit(solution)/shard_map/cond/branch_1_fun/ppermute | solution.py:134
  76.8 3.0 %shard_map.110 = f32[720,640]{1,0:T(8,128)} custom-call(s32[1]{0:T(128)} %get-tuple-element.63.refs_0_, bf16[720,640]{1,0:T(8,128)(2,1)S(1)} %shard_map.103.refs_7_.refs_2_.refs_3_.refs_1_, bf16[720,640]{1,0:T(8,128)(2,1)} %collective-permute-done.18.refs_2_, bf16[720,640]{1,0:T(8,128)(2,1)S(1)} %collective-permute-done.19.refs_3_), custom_call_target="tpu_custom_call" | custom-call | tf_op jit(solution)/shard_map/pallas_call | solution.py:145
  (62 shorter events, 10.2 us)
Async XLA Ops:
  0.6 8.5 %collective-permute-start.2 = (bf16[720,640]{1,0:T(8,128)(2,1)}, bf16[720,640]{1,0:T(8,128)(2,1)S(1)}, u32[]{:S(2)}, u32[]{:S(2)}) collective-permute-start(bf16[720,640]{1,0:T(8,128)(2,1)} %bitcast.17), channel_id=1, source_target_pairs={{0,1},{1,0},{2,3},{3,2},{4,5},{5,4},{6,7},{7,6},{8,9},{9,8},{10,11... | collective-permute-start | bytes 2764808 | tf_op jit(solution)/shard_map/ppermute | solution.py:134
  1.1 11.4 %collective-permute-start.6 = (bf16[256,640]{1,0:T(8,128)(2,1)}, bf16[256,640]{1,0:T(8,128)(2,1)S(1)}, u32[]{:S(2)}, u32[]{:S(2)}) collective-permute-start(bf16[256,640]{1,0:T(8,128)(2,1)} %bitcast.19), channel_id=1, source_target_pairs={{0,4},{1,5},{2,6},{3,7},{4,0},{5,1},{6,2},{7,3},{8,12},{9,13},{10,... | collective-permute-start | bytes 983048 | tf_op jit(solution)/shard_map/ppermute | solution.py:134
  3.7 10.8 %collective-permute-start.5 = (bf16[256,640]{1,0:T(8,128)(2,1)}, bf16[256,640]{1,0:T(8,128)(2,1)S(1)}, u32[]{:S(2)}, u32[]{:S(2)}) collective-permute-start(bf16[256,640]{1,0:T(8,128)(2,1)} %bitcast.20), channel_id=1, source_target_pairs={{0,2},{1,3},{2,0},{3,1},{4,6},{5,7},{6,4},{7,5},{8,10},{9,11},{10,... | collective-permute-start | bytes 983048 | tf_op jit(solution)/shard_map/ppermute | solution.py:134
  5.9 1.0 %copy-start.1 = (bf16[1,16,16,640]{3,2,1,0:T(8,128)(2,1)S(1)}, bf16[1,16,16,640]{3,2,1,0:T(8,128)(2,1)}, u32[]{:S(2)}) copy-start(bf16[1,16,16,640]{3,2,1,0:T(8,128)(2,1)} %param.8) | copy-start | bytes 983044
  6.9 7.6 %copy-start.6 = (bf16[1,16,16,640]{3,2,1,0:T(8,128)(2,1)S(1)}, bf16[1,16,16,640]{3,2,1,0:T(8,128)(2,1)}, u32[]{:S(2)}) copy-start(bf16[1,16,16,640]{3,2,1,0:T(8,128)(2,1)} %param.9) | copy-start | bytes 983044
  8.4 13.1 %collective-permute-start.4 = (bf16[256,640]{1,0:T(8,128)(2,1)S(1)}, bf16[256,640]{1,0:T(8,128)(2,1)S(1)}, u32[]{:S(2)}, u32[]{:S(2)}) collective-permute-start(bf16[256,640]{1,0:T(8,128)(2,1)S(1)} %get-tuple-element.39.refs_1_.refs_2_), channel_id=1, source_target_pairs={{0,2},{1,3},{2,0},{3,1},{4,6},{5,7},{6,4},{7,5},{8,10},{9,11},{10,... | collective-permute-start | bytes 983048 | tf_op jit(solution)/shard_map/ppermute | solution.py:134
  9.0 12.5 %collective-permute-start.3 = (bf16[256,640]{1,0:T(8,128)(2,1)S(1)}, bf16[256,640]{1,0:T(8,128)(2,1)S(1)}, u32[]{:S(2)}, u32[]{:S(2)}) collective-permute-start(bf16[256,640]{1,0:T(8,128)(2,1)S(1)} %get-tuple-element.39.refs_1_.refs_2_), channel_id=1, source_target_pairs={{0,4},{1,5},{2,6},{3,7},{4,0},{5,1},{6,2},{7,3},{8,12},{9,13},{10,... | collective-permute-start | bytes 983048 | tf_op jit(solution)/shard_map/ppermute | solution.py:134
  9.2 1.2 %copy-start.3 = (bf16[1,720,640]{2,1,0:T(8,128)(2,1)S(1)}, bf16[1,720,640]{2,1,0:T(8,128)(2,1)}, u32[]{:S(2)}) copy-start(bf16[1,720,640]{2,1,0:T(8,128)(2,1)} %param.10) | copy-start | bytes 2764804
  15.7 10.5 %collective-permute-start.10 = (bf16[128,640]{1,0:T(8,128)(2,1)S(1)}, bf16[128,640]{1,0:T(8,128)(2,1)S(1)}, u32[]{:S(2)}, u32[]{:S(2)}) collective-permute-start(bf16[128,640]{1,0:T(8,128)(2,1)S(1)} %slice.18), channel_id=1, source_target_pairs={{0,4},{1,5},{2,6},{3,7},{4,0},{5,1},{6,2},{7,3},{8,12},{9,13},{10,... | collective-permute-start | bytes 491528 | tf_op jit(solution)/shard_map/ppermute | solution.py:134
  15.8 10.4 %collective-permute-start.9 = (bf16[128,640]{1,0:T(8,128)(2,1)S(1)}, bf16[128,640]{1,0:T(8,128)(2,1)S(1)}, u32[]{:S(2)}, u32[]{:S(2)}) collective-permute-start(bf16[128,640]{1,0:T(8,128)(2,1)S(1)} %slice.17), channel_id=1, source_target_pairs={{0,2},{1,3},{2,0},{3,1},{4,6},{5,7},{6,4},{7,5},{8,10},{9,11},{10,... | collective-permute-start | bytes 491528 | tf_op jit(solution)/shard_map/ppermute | solution.py:134
  21.6 6.2 %collective-permute-start.7 = (bf16[128,640]{1,0:T(8,128)(2,1)S(1)}, bf16[128,640]{1,0:T(8,128)(2,1)S(1)}, u32[]{:S(2)}, u32[]{:S(2)}) collective-permute-start(bf16[128,640]{1,0:T(8,128)(2,1)S(1)} %slice.15), channel_id=1, source_target_pairs={{0,2},{1,3},{2,0},{3,1},{4,6},{5,7},{6,4},{7,5},{8,10},{9,11},{10,... | collective-permute-start | bytes 491528 | tf_op jit(solution)/shard_map/ppermute | solution.py:134
  23.1 5.3 %collective-permute-start.8 = (bf16[128,640]{1,0:T(8,128)(2,1)S(1)}, bf16[128,640]{1,0:T(8,128)(2,1)S(1)}, u32[]{:S(2)}, u32[]{:S(2)}) collective-permute-start(bf16[128,640]{1,0:T(8,128)(2,1)S(1)} %slice.16), channel_id=1, source_target_pairs={{0,4},{1,5},{2,6},{3,7},{4,0},{5,1},{6,2},{7,3},{8,12},{9,13},{10,... | collective-permute-start | bytes 491528 | tf_op jit(solution)/shard_map/ppermute | solution.py:134
  30.0 2.5 %collective-permute-start.11 = (bf16[720,640]{1,0:T(8,128)(2,1)S(1)}, bf16[720,640]{1,0:T(8,128)(2,1)S(1)}, u32[]{:S(2)}, u32[]{:S(2)}) collective-permute-start(bf16[720,640]{1,0:T(8,128)(2,1)S(1)} %shard_map.102), channel_id=1, source_target_pairs={{0,1},{1,0},{2,3},{3,2},{4,5},{5,4},{6,7},{7,6},{8,9},{9,8},{10,11... | collective-permute-start | bytes 2764808 | tf_op jit(solution)/shard_map/ppermute | solution.py:134
  32.7 44.1 %collective-permute-start.19 = (bf16[720,640]{1,0:T(8,128)(2,1)S(1)}, bf16[720,640]{1,0:T(8,128)(2,1)S(1)}, u32[]{:S(2)}, u32[]{:S(2)}) collective-permute-start(bf16[720,640]{1,0:T(8,128)(2,1)S(1)} %shard_map.103.refs_7_.refs_2_.refs_3_.refs_1_), channel_id=1, source_target_pairs={{0,16},{8,24},{16,0},{24,8},{1,17},{9,25},{17,1},{25,9},{2,18},{10... | collective-permute-start | bytes 2764808 | tf_op jit(solution)/shard_map/ppermute | solution.py:134
  35.4 41.4 %collective-permute-start.18 = (bf16[720,640]{1,0:T(8,128)(2,1)S(1)}, bf16[720,640]{1,0:T(8,128)(2,1)}, u32[]{:S(2)}, u32[]{:S(2)}) collective-permute-start(bf16[720,640]{1,0:T(8,128)(2,1)S(1)} %shard_map.103.refs_7_.refs_2_.refs_3_.refs_1_), channel_id=1, source_target_pairs={{0,8},{8,0},{16,24},{24,16},{1,9},{9,1},{17,25},{25,17},{2,10},{10... | collective-permute-start | bytes 2764808 | tf_op jit(solution)/shard_map/ppermute | solution.py:134
  37.0 10.6 %collective-permute-start.14 = (bf16[256,640]{1,0:T(8,128)(2,1)S(1)}, bf16[256,640]{1,0:T(8,128)(2,1)S(1)}, u32[]{:S(2)}, u32[]{:S(2)}) collective-permute-start(bf16[256,640]{1,0:T(8,128)(2,1)S(1)} %get-tuple-element.57), channel_id=1, source_target_pairs={{0,2},{1,3},{2,0},{3,1},{4,6},{5,7},{6,4},{7,5},{8,10},{9,11},{10,... | collective-permute-start | bytes 983048 | tf_op jit(solution)/shard_map/ppermute | solution.py:134
  37.8 16.4 %collective-permute-start.15 = (bf16[256,640]{1,0:T(8,128)(2,1)S(1)}, bf16[256,640]{1,0:T(8,128)(2,1)S(1)}, u32[]{:S(2)}, u32[]{:S(2)}) collective-permute-start(bf16[256,640]{1,0:T(8,128)(2,1)S(1)} %get-tuple-element.58), channel_id=1, source_target_pairs={{0,4},{1,5},{2,6},{3,7},{4,0},{5,1},{6,2},{7,3},{8,12},{9,13},{10,... | collective-permute-start | bytes 983048 | tf_op jit(solution)/shard_map/ppermute | solution.py:134
  38.3 16.3 %collective-permute-start.16 = (bf16[256,640]{1,0:T(8,128)(2,1)S(1)}, bf16[256,640]{1,0:T(8,128)(2,1)S(1)}, u32[]{:S(2)}, u32[]{:S(2)}) collective-permute-start(bf16[256,640]{1,0:T(8,128)(2,1)S(1)} %get-tuple-element.59), channel_id=1, source_target_pairs={{0,6},{1,7},{2,4},{3,5},{4,2},{5,3},{6,0},{7,1},{8,14},{9,15},{10,... | collective-permute-start | bytes 983048 | tf_op jit(solution)/shard_map/ppermute | solution.py:134
  40.5 14.1 %copy-start.2 = (bf16[1,16,16,640]{3,2,1,0:T(8,128)(2,1)S(1)}, bf16[1,16,16,640]{3,2,1,0:T(8,128)(2,1)}, u32[]{:S(2)}) copy-start(bf16[1,16,16,640]{3,2,1,0:T(8,128)(2,1)} %param.8) | copy-start | bytes 983044
  45.3 8.9 %copy-start.4 = (f32[256,640]{1,0:T(8,128)}, f32[256,640]{1,0:T(8,128)S(1)}, u32[]{:S(2)}) copy-start(f32[256,640]{1,0:T(8,128)S(1)} %get-tuple-element.48.refs_0_) | copy-start | bytes 1966084
  45.3 22.1 %copy-start.8 = (s32[8]{0:T(128)S(1)}, s32[8]{0:T(128)}, u32[]{:S(2)}) copy-start(s32[8]{0:T(128)} %param.13) | copy-start | bytes 100
  47.6 15.6 %collective-permute-start.12 = (bf16[256,640]{1,0:T(8,128)(2,1)S(1)}, bf16[256,640]{1,0:T(8,128)(2,1)S(1)}, u32[]{:S(2)}, u32[]{:S(2)}) collective-permute-start(bf16[256,640]{1,0:T(8,128)(2,1)S(1)} %get-tuple-element.51), channel_id=1, source_target_pairs={{0,2},{1,3},{2,0},{3,1},{4,6},{5,7},{6,4},{7,5},{8,10},{9,11},{10,... | collective-permute-start | bytes 983048 | tf_op jit(solution)/shard_map/ppermute | solution.py:134
  54.2 9.0 %collective-permute-start.13 = (bf16[256,640]{1,0:T(8,128)(2,1)S(1)}, bf16[256,640]{1,0:T(8,128)(2,1)S(1)}, u32[]{:S(2)}, u32[]{:S(2)}) collective-permute-start(bf16[256,640]{1,0:T(8,128)(2,1)S(1)} %get-tuple-element.52), channel_id=1, source_target_pairs={{0,4},{1,5},{2,6},{3,7},{4,0},{5,1},{6,2},{7,3},{8,12},{9,13},{10,... | collective-permute-start | bytes 983048 | tf_op jit(solution)/shard_map/ppermute | solution.py:134
  56.7 3.9 %collective-permute-start.20 = (f32[2,640]{1,0:T(2,128)S(1)}, f32[2,640]{1,0:T(2,128)S(1)}, u32[]{:S(2)}, u32[]{:S(2)}) collective-permute-start(f32[2,640]{1,0:T(2,128)S(1)} %get-tuple-element.60.refs_1_), channel_id=1, source_target_pairs={{0,2},{1,3},{2,0},{3,1},{4,6},{5,7},{6,4},{7,5},{8,10},{9,11},{10,... | collective-permute-start | bytes 15368 | tf_op jit(solution)/shard_map/ppermute | solution.py:134
  60.6 9.6 %collective-permute-start.17 = (bf16[256,640]{1,0:T(8,128)(2,1)S(1)}, bf16[256,640]{1,0:T(8,128)(2,1)S(1)}, u32[]{:S(2)}, u32[]{:S(2)}) collective-permute-start(bf16[256,640]{1,0:T(8,128)(2,1)S(1)} %shard_map.108), channel_id=1, source_target_pairs={{0,6},{1,7},{2,4},{3,5},{4,2},{5,3},{6,0},{7,1},{8,14},{9,15},{10,... | collective-permute-start | bytes 983048 | tf_op jit(solution)/shard_map/ppermute | solution.py:134
  63.2 4.2 %collective-permute-start.21 = (f32[2,640]{1,0:T(2,128)S(1)}, f32[2,640]{1,0:T(2,128)S(1)}, u32[]{:S(2)}, u32[]{:S(2)}) collective-permute-start(f32[2,640]{1,0:T(2,128)S(1)} %shard_map.111), channel_id=1, source_target_pairs={{0,4},{1,5},{2,6},{3,7},{4,0},{5,1},{6,2},{7,3},{8,12},{9,13},{10,... | collective-permute-start | bytes 15368 | tf_op jit(solution)/shard_map/ppermute | solution.py:134
  67.4 1.3 %collective-permute-start.22 = (f32[2,640]{1,0:T(2,128)S(1)}, f32[2,640]{1,0:T(2,128)S(1)}, u32[]{:S(2)}, u32[]{:S(2)}) collective-permute-start(f32[2,640]{1,0:T(2,128)S(1)} %add.35), channel_id=1, source_target_pairs={{0,1},{1,0},{2,3},{3,2},{4,5},{5,4},{6,7},{7,6},{8,9},{9,8},{10,11... | collective-permute-start | bytes 15368 | tf_op jit(solution)/shard_map/ppermute | solution.py:134
  70.2 1.1 %copy-start.5 = (f32[256,640]{1,0:T(8,128)S(1)}, f32[256,640]{1,0:T(8,128)}, u32[]{:S(2)}) copy-start(f32[256,640]{1,0:T(8,128)} %copy-done.4) | copy-start | bytes 1966084
  72.2 1.0 %copy-start = (bf16[256,640]{1,0:T(8,128)(2,1)S(1)}, bf16[256,640]{1,0:T(8,128)(2,1)}, u32[]{:S(2)}) copy-start(bf16[256,640]{1,0:T(8,128)(2,1)} %shard_map.109.refs_1_) | copy-start | bytes 983044
  73.1 3.6 %collective-permute-start.1 = (f32[2,640]{1,0:T(2,128)S(1)}, f32[2,640]{1,0:T(2,128)S(1)}, u32[]{:S(2)}, u32[]{:S(2)}) collective-permute-start(f32[2,640]{1,0:T(2,128)S(1)} %param.1), channel_id=1, source_target_pairs={{0,8},{8,0},{16,24},{24,16},{1,9},{9,1},{17,25},{25,17},{2,10},{10... | collective-permute-start | bytes 15368 | tf_op jit(solution)/shard_map/cond/branch_1_fun/ppermute | solution.py:134
  76.8 3.0 %copy-start.7 = (f32[1,2,640]{2,1,0:T(2,128)}, f32[1,2,640]{2,1,0:T(2,128)S(1)}, u32[]{:S(2)}) copy-start(f32[1,2,640]{2,1,0:T(2,128)S(1)} %get-tuple-element.64) | copy-start | bytes 15364

commit v3 on v2

--- a/solution.py
+++ b/solution.py
@@ -488,14 +488,14 @@
     )
     shard_bit = lax.dynamic_slice_in_dim(partner_bit, place, 1)
     (weight_avg,) = call(
-        functools.partial(pair_kernel, 9),
+        functools.partial(pair_kernel, 3),
         [shaped((rows, chans), F32)],
         [shard_bit, narrow, pair1, pair2],
         [
             pltpu.VMEM((rows, chans), F32),
             pltpu.VMEM((rows, chans), BF16),
-            pltpu.SemaphoreType.DMA((9,)),
-            pltpu.SemaphoreType.DMA((9,)),
+            pltpu.SemaphoreType.DMA((3,)),
+            pltpu.SemaphoreType.DMA((3,)),
         ],
         copies_out=True,
         outside=(2,),

time: 80.3 us -> 80.3 us (level)
  no operation moved by 1% of the time
where the time goes in v3:
time: 80.3 us; the launch traced here: 80 us
  waiting for transfers between devices  25.1 us (31%)
  Pallas kernels  24.8 us (31%)
  starting transfers between devices  22.6 us (28%)
  local copies, waits for them, and re-layouts  4.97 us (6%)
  between operations  1.7 us (2%)
    ppermute x22, waiting for transfers between devices, swap(): return lax.ppermute(value, axis, pairs)  25.1 us
    pallas_call x13, Pallas kernels, call(): pl.pallas_call(body, out_shape=tuple(outs), in_specs=[untouched if index...  24.8 us
    ppermute x22, starting transfers between devices, swap(): return lax.ppermute(value, axis, pairs)  22.6 us
    unnamed x18, local copies, waits for them, and re-layouts  4.23 us
  transfers between devices with their start and end apart: 22, of which 13 were waited for; matrix products, arithmetic and copies ran while one was open for 2% of the time, Pallas kernels for 25%

profile of v3, /device:TPU:0, one launch (start us, length us, event | category | flops | bytes accessed | tf_op | source)
XLA Modules:
  0.0 80.0 jit_solution(11396774162231873728)
XLA Ops:
  1.1 2.6 %collective-permute-start.6 = (bf16[256,640]{1,0:T(8,128)(2,1)}, bf16[256,640]{1,0:T(8,128)(2,1)S(1)}, u32[]{:S(2)}, u32[]{:S(2)}) collective-permute-start(bf16[256,640]{1,0:T(8,128)(2,1)} %bitcast.19), channel_id=1, source_target_pairs={{0,4},{1,5},{2,6},{3,7},{4,0},{5,1},{6,2},{7,3},{8,12},{9,13},{10,... | collective-permute-start | bytes 983048 | tf_op jit(solution)/shard_map/ppermute | solution.py:134
  3.7 1.5 %collective-permute-start.5 = (bf16[256,640]{1,0:T(8,128)(2,1)}, bf16[256,640]{1,0:T(8,128)(2,1)S(1)}, u32[]{:S(2)}, u32[]{:S(2)}) collective-permute-start(bf16[256,640]{1,0:T(8,128)(2,1)} %bitcast.20), channel_id=1, source_target_pairs={{0,2},{1,3},{2,0},{3,1},{4,6},{5,7},{6,4},{7,5},{8,10},{9,11},{10,... | collective-permute-start | bytes 983048 | tf_op jit(solution)/shard_map/ppermute | solution.py:134
  6.9 1.5 %shard_map.93 = (bf16[256,640]{1,0:T(8,128)(2,1)S(1)}, f32[2,640]{1,0:T(2,128)S(1)}) custom-call(bf16[256,640]{1,0:T(8,128)(2,1)S(1)} %bitcast.15, f32[2,640]{1,0:T(2,128)S(1)} %pad_maximum_fusion.refs_1_.refs_2_), custom_call_target="tpu_custom_call" | custom-call | tf_op jit(solution)/shard_map/pallas_call | solution.py:145
  9.2 1.2 %copy-done.3 = bf16[1,720,640]{2,1,0:T(8,128)(2,1)S(1)} copy-done((bf16[1,720,640]{2,1,0:T(8,128)(2,1)S(1)}, bf16[1,720,640]{2,1,0:T(8,128)(2,1)}, u32[]{:S(2)}) %copy-start.3) | copy-done | bytes 921624
  10.3 1.9 %shard_map.94 = (bf16[1920,640]{1,0:T(8,128)(2,1)S(1)}, bf16[1920,640]{1,0:T(8,128)(2,1)S(1)}, bf16[768,256]{1,0:T(8,128)(2,1)S(1)}, bf16[768,256]{1,0:T(8,128)(2,1)S(1)}) custom-call(s32[3]{0:T(128)S(1)} %pad_add_fusion.refs_0_, bf16[720,640]{1,0:T(8,128)(2,1)S(1)} %bitcast.18, bf16[720,640]{1,0:T(8,128)(2,1)S(1)} %collective-permute-done.2.refs_2_, ...), custom_call_target="tpu_custom_call" | custom-call | tf_op jit(solution)/shard_map/pallas_call | solution.py:145
  12.5 2.0 %collective-permute-done.5.refs_2_.refs_0_ = bf16[256,640]{1,0:T(8,128)(2,1)S(1)} collective-permute-done((bf16[256,640]{1,0:T(8,128)(2,1)}, bf16[256,640]{1,0:T(8,128)(2,1)S(1)}, u32[]{:S(2)}, u32[]{:S(2)}) %collective-permute-start.5) | collective-permute-done | bytes 327712 | tf_op jit(solution)/shard_map/ppermute | solution.py:134
  14.5 1.1 %shard_map.95.refs_1_.refs_2_.refs_0_ = bf16[768,1920]{1,0:T(8,128)(2,1)S(1)} custom-call(bf16[768,256]{1,0:T(8,128)(2,1)S(1)} %get-tuple-element.41.refs_0_, bf16[256,640]{1,0:T(8,128)(2,1)S(1)} %bitcast.21, bf16[256,640]{1,0:T(8,128)(2,1)S(1)} %collective-permute-done.5.refs_2_.refs_0_, bf16[256,640]{1,0:T(8,128)(2,1)S(1)} %collective-permute-done.6.refs_3_.refs_1_), custom_call_target="tpu_custom_call" | custom-call | tf_op jit(solution)/shard_map/pallas_call | solution.py:145
  15.8 1.9 %collective-permute-start.9 = (bf16[128,640]{1,0:T(8,128)(2,1)S(1)}, bf16[128,640]{1,0:T(8,128)(2,1)S(1)}, u32[]{:S(2)}, u32[]{:S(2)}) collective-permute-start(bf16[128,640]{1,0:T(8,128)(2,1)S(1)} %slice.17), channel_id=1, source_target_pairs={{0,2},{1,3},{2,0},{3,1},{4,6},{5,7},{6,4},{7,5},{8,10},{9,11},{10,... | collective-permute-start | bytes 491528 | tf_op jit(solution)/shard_map/ppermute | solution.py:134
  17.7 2.6 %shard_map.96 = (f32[256,640]{1,0:T(8,128)S(1)}, bf16[256,640]{1,0:T(8,128)(2,1)S(1)}, bf16[256,640]{1,0:T(8,128)(2,1)S(1)}) custom-call(bf16[1920,640]{1,0:T(8,128)(2,1)S(1)} %get-tuple-element.40.refs_0_.refs_1_, bf16[768,1920]{1,0:T(8,128)(2,1)S(1)} %shard_map.95.refs_1_.refs_2_.refs_0_), custom_call_target="tpu_custom_call" | custom-call | tf_op jit(solution)/shard_map/pallas_call | solution.py:145
  20.3 1.2 %collective-permute-done.4.refs_1_ = bf16[256,640]{1,0:T(8,128)(2,1)S(1)} collective-permute-done((bf16[256,640]{1,0:T(8,128)(2,1)S(1)}, bf16[256,640]{1,0:T(8,128)(2,1)S(1)}, u32[]{:S(2)}, u32[]{:S(2)}) %collective-permute-start.4) | collective-permute-done | bytes 327712 | tf_op jit(solution)/shard_map/ppermute | solution.py:134
  21.6 1.6 %collective-permute-start.7 = (bf16[128,640]{1,0:T(8,128)(2,1)S(1)}, bf16[128,640]{1,0:T(8,128)(2,1)S(1)}, u32[]{:S(2)}, u32[]{:S(2)}) collective-permute-start(bf16[128,640]{1,0:T(8,128)(2,1)S(1)} %slice.15), channel_id=1, source_target_pairs={{0,2},{1,3},{2,0},{3,1},{4,6},{5,7},{6,4},{7,5},{8,10},{9,11},{10,... | collective-permute-start | bytes 491528 | tf_op jit(solution)/shard_map/ppermute | solution.py:134
  23.6 2.5 %shard_map.99.refs_3_.refs_5_.refs_4_ = f32[1920,640]{1,0:T(8,128)S(1)} custom-call(bf16[768,1920]{1,0:T(8,128)(2,1)S(1)} %shard_map.95.refs_1_.refs_2_.refs_0_, bf16[256,640]{1,0:T(8,128)(2,1)S(1)} %get-tuple-element.39.refs_1_.refs_2_, bf16[256,640]{1,0:T(8,128)(2,1)S(1)} %get-tuple-element.43.refs_2_.refs_3_, ...), custom_call_target="tpu_custom_call" | custom-call | tf_op jit(solution)/shard_map/pallas_call | solution.py:145
  26.6 1.1 %collective-permute-done.7.refs_2_.refs_1_.refs_5_ = bf16[128,640]{1,0:T(8,128)(2,1)S(1)} collective-permute-done((bf16[128,640]{1,0:T(8,128)(2,1)S(1)}, bf16[128,640]{1,0:T(8,128)(2,1)S(1)}, u32[]{:S(2)}, u32[]{:S(2)}) %collective-permute-start.7) | collective-permute-done | bytes 163872 | tf_op jit(solution)/shard_map/ppermute | solution.py:134
  28.5 1.5 %shard_map.102 = bf16[720,640]{1,0:T(8,128)(2,1)S(1)} custom-call(s32[3]{0:T(128)S(1)} %pad_add_fusion.refs_0_, bf16[128,640]{1,0:T(8,128)(2,1)S(1)} %collective-permute-done.7.refs_2_.refs_1_.refs_5_, bf16[128,640]{1,0:T(8,128)(2,1)S(1)} %collective-permute-done.8.refs_3_.refs_2_.refs_6_, bf16[256,1920]{1,0:T(8,128)(2,1)S(1)} %shard_map.100.refs_4_.refs_3_, ...), custom_call_target="tpu_custom_call" | custom-call | tf_op jit(solution)/shard_map/pallas_call | solution.py:145
  30.1 2.3 %shard_map.101 = (f32[720,640]{1,0:T(8,128)S(1)}, bf16[256,640]{1,0:T(8,128)(2,1)S(1)}) custom-call(s32[3]{0:T(128)S(1)} %pad_add_fusion.refs_0_, bf16[1920,640]{1,0:T(8,128)(2,1)S(1)} %get-tuple-element.40.refs_0_.refs_1_, bf16[128,640]{1,0:T(8,128)(2,1)S(1)} %collective-permute-done.7.refs_2_.refs_1_.refs_5_, ...), custom_call_target="tpu_custom_call" | custom-call | tf_op jit(solution)/shard_map/pallas_call | solution.py:145
  32.7 2.7 %collective-permute-start.19 = (bf16[720,640]{1,0:T(8,128)(2,1)S(1)}, bf16[720,640]{1,0:T(8,128)(2,1)S(1)}, u32[]{:S(2)}, u32[]{:S(2)}) collective-permute-start(bf16[720,640]{1,0:T(8,128)(2,1)S(1)} %shard_map.103.refs_7_.refs_2_.refs_3_.refs_1_), channel_id=1, source_target_pairs={{0,16},{8,24},{16,0},{24,8},{1,17},{9,25},{17,1},{25,9},{2,18},{10... | collective-permute-start | bytes 2764808 | tf_op jit(solution)/shard_map/ppermute | solution.py:134
  35.4 1.6 %collective-permute-start.18 = (bf16[720,640]{1,0:T(8,128)(2,1)S(1)}, bf16[720,640]{1,0:T(8,128)(2,1)}, u32[]{:S(2)}, u32[]{:S(2)}) collective-permute-start(bf16[720,640]{1,0:T(8,128)(2,1)S(1)} %shard_map.103.refs_7_.refs_2_.refs_3_.refs_1_), channel_id=1, source_target_pairs={{0,8},{8,0},{16,24},{24,16},{1,9},{9,1},{17,25},{25,17},{2,10},{10... | collective-permute-start | bytes 2764808 | tf_op jit(solution)/shard_map/ppermute | solution.py:134
  38.3 2.2 %collective-permute-start.16 = (bf16[256,640]{1,0:T(8,128)(2,1)S(1)}, bf16[256,640]{1,0:T(8,128)(2,1)S(1)}, u32[]{:S(2)}, u32[]{:S(2)}) collective-permute-start(bf16[256,640]{1,0:T(8,128)(2,1)S(1)} %get-tuple-element.59), channel_id=1, source_target_pairs={{0,6},{1,7},{2,4},{3,5},{4,2},{5,3},{6,0},{7,1},{8,14},{9,15},{10,... | collective-permute-start | bytes 983048 | tf_op jit(solution)/shard_map/ppermute | solution.py:134
  40.5 4.8 %shard_map.104 = (f32[256,640]{1,0:T(8,128)S(1)}, bf16[256,640]{1,0:T(8,128)(2,1)S(1)}, bf16[256,640]{1,0:T(8,128)(2,1)S(1)}, bf16[256,640]{1,0:T(8,128)(2,1)S(1)}) custom-call(bf16[768,256]{1,0:T(8,128)(2,1)S(1)} %get-tuple-element.37.refs_0_, bf16[1920,640]{1,0:T(8,128)(2,1)S(1)} %get-tuple-element.38.refs_1_, ...), custom_call_target="tpu_custom_call" | custom-call | tf_op jit(solution)/shard_map/pallas_call | solution.py:145
  45.3 2.3 %collective-permute-done.14.refs_4_ = bf16[256,640]{1,0:T(8,128)(2,1)S(1)} collective-permute-done((bf16[256,640]{1,0:T(8,128)(2,1)S(1)}, bf16[256,640]{1,0:T(8,128)(2,1)S(1)}, u32[]{:S(2)}, u32[]{:S(2)}) %collective-permute-start.14) | collective-permute-done | bytes 327712 | tf_op jit(solution)/shard_map/ppermute | solution.py:134
  48.4 5.8 %collective-permute-done.15.refs_5_ = bf16[256,640]{1,0:T(8,128)(2,1)S(1)} collective-permute-done((bf16[256,640]{1,0:T(8,128)(2,1)S(1)}, bf16[256,640]{1,0:T(8,128)(2,1)S(1)}, u32[]{:S(2)}, u32[]{:S(2)}) %collective-permute-start.15) | collective-permute-done | bytes 327712 | tf_op jit(solution)/shard_map/ppermute | solution.py:134
  54.6 2.1 %shard_map.107 = (bf16[256,640]{1,0:T(8,128)(2,1)}, f32[2,640]{1,0:T(2,128)S(1)}) custom-call(bf16[256,640]{1,0:T(8,128)(2,1)S(1)} %bitcast.16, f32[2,640]{1,0:T(2,128)S(1)} %get-tuple-element.36.refs_3_.refs_1_, f32[2,640]{1,0:T(2,128)S(1)} %pad_maximum_fusion.refs_1_.refs_2_, f32[256,640]{1,0:T(8,128)S(1)} %get-tuple-element.42.refs_2_.refs_3_, ...), custom_call_target="tpu_custom_call" | custom-call | tf_op jit(solution)/shard_map/pallas_call | solution.py:145
  56.7 1.4 %collective-permute-start.20 = (f32[2,640]{1,0:T(2,128)S(1)}, f32[2,640]{1,0:T(2,128)S(1)}, u32[]{:S(2)}, u32[]{:S(2)}) collective-permute-start(f32[2,640]{1,0:T(2,128)S(1)} %get-tuple-element.60.refs_1_), channel_id=1, source_target_pairs={{0,2},{1,3},{2,0},{3,1},{4,6},{5,7},{6,4},{7,5},{8,10},{9,11},{10,... | collective-permute-start | bytes 15368 | tf_op jit(solution)/shard_map/ppermute | solution.py:134
  58.1 2.5 %collective-permute-done.20 = f32[2,640]{1,0:T(2,128)S(1)} collective-permute-done((f32[2,640]{1,0:T(2,128)S(1)}, f32[2,640]{1,0:T(2,128)S(1)}, u32[]{:S(2)}, u32[]{:S(2)}) %collective-permute-start.20) | collective-permute-done | bytes 5152 | tf_op jit(solution)/shard_map/ppermute | solution.py:134
  60.6 2.6 %collective-permute-start.17 = (bf16[256,640]{1,0:T(8,128)(2,1)S(1)}, bf16[256,640]{1,0:T(8,128)(2,1)S(1)}, u32[]{:S(2)}, u32[]{:S(2)}) collective-permute-start(bf16[256,640]{1,0:T(8,128)(2,1)S(1)} %shard_map.108), channel_id=1, source_target_pairs={{0,6},{1,7},{2,4},{3,5},{4,2},{5,3},{6,0},{7,1},{8,14},{9,15},{10,... | collective-permute-start | bytes 983048 | tf_op jit(solution)/shard_map/ppermute | solution.py:134
  63.3 4.1 %collective-permute-done.21 = f32[2,640]{1,0:T(2,128)S(1)} collective-permute-done((f32[2,640]{1,0:T(2,128)S(1)}, f32[2,640]{1,0:T(2,128)S(1)}, u32[]{:S(2)}, u32[]{:S(2)}) %collective-permute-start.21) | collective-permute-done | bytes 5152 | tf_op jit(solution)/shard_map/ppermute | solution.py:134
  68.8 1.4 %collective-permute-done.17.refs_3_ = bf16[256,640]{1,0:T(8,128)(2,1)S(1)} collective-permute-done((bf16[256,640]{1,0:T(8,128)(2,1)S(1)}, bf16[256,640]{1,0:T(8,128)(2,1)S(1)}, u32[]{:S(2)}, u32[]{:S(2)}) %collective-permute-start.17) | collective-permute-done | bytes 327712 | tf_op jit(solution)/shard_map/ppermute | solution.py:134
  70.2 1.1 %copy-done.5 = f32[256,640]{1,0:T(8,128)S(1)} copy-done((f32[256,640]{1,0:T(8,128)S(1)}, f32[256,640]{1,0:T(8,128)}, u32[]{:S(2)}) %copy-start.5) | copy-done | bytes 655384
  72.2 1.0 %copy-done = bf16[256,640]{1,0:T(8,128)(2,1)S(1)} copy-done((bf16[256,640]{1,0:T(8,128)(2,1)S(1)}, bf16[256,640]{1,0:T(8,128)(2,1)}, u32[]{:S(2)}) %copy-start) | copy-done | bytes 327704
  73.1 3.6 %conditional.1 = (f32[1,2,640]{2,1,0:T(2,128)S(1)}) conditional(s32[]{:T(128)} %bitcast.11, f32[2,640]{1,0:T(2,128)S(1)} %shard_map.112, f32[2,640]{1,0:T(2,128)S(1)} %shard_map.112), branch_computations={%region_0.1_spmd, %region_1.2_spmd} | conditional | flops 2560 | bytes 35888 | solution.py:483
  73.6 3.2 %collective-permute-done.1 = f32[2,640]{1,0:T(2,128)S(1)} collective-permute-done((f32[2,640]{1,0:T(2,128)S(1)}, f32[2,640]{1,0:T(2,128)S(1)}, u32[]{:S(2)}, u32[]{:S(2)}) %collective-permute-start.1) | collective-permute-done | bytes 5152 | tf_op jit(solution)/shard_map/cond/branch_1_fun/ppermute | solution.py:134
  76.8 3.0 %shard_map.110 = f32[720,640]{1,0:T(8,128)} custom-call(s32[1]{0:T(128)} %get-tuple-element.63.refs_0_, bf16[720,640]{1,0:T(8,128)(2,1)S(1)} %shard_map.103.refs_7_.refs_2_.refs_3_.refs_1_, bf16[720,640]{1,0:T(8,128)(2,1)} %collective-permute-done.18.refs_2_, bf16[720,640]{1,0:T(8,128)(2,1)S(1)} %collective-permute-done.19.refs_3_), custom_call_target="tpu_custom_call" | custom-call | tf_op jit(solution)/shard_map/pallas_call | solution.py:145
  (62 shorter events, 10.2 us)
Async XLA Ops:
  0.6 8.5 %collective-permute-start.2 = (bf16[720,640]{1,0:T(8,128)(2,1)}, bf16[720,640]{1,0:T(8,128)(2,1)S(1)}, u32[]{:S(2)}, u32[]{:S(2)}) collective-permute-start(bf16[720,640]{1,0:T(8,128)(2,1)} %bitcast.17), channel_id=1, source_target_pairs={{0,1},{1,0},{2,3},{3,2},{4,5},{5,4},{6,7},{7,6},{8,9},{9,8},{10,11... | collective-permute-start | bytes 2764808 | tf_op jit(solution)/shard_map/ppermute | solution.py:134
  1.1 11.4 %collective-permute-start.6 = (bf16[256,640]{1,0:T(8,128)(2,1)}, bf16[256,640]{1,0:T(8,128)(2,1)S(1)}, u32[]{:S(2)}, u32[]{:S(2)}) collective-permute-start(bf16[256,640]{1,0:T(8,128)(2,1)} %bitcast.19), channel_id=1, source_target_pairs={{0,4},{1,5},{2,6},{3,7},{4,0},{5,1},{6,2},{7,3},{8,12},{9,13},{10,... | collective-permute-start | bytes 983048 | tf_op jit(solution)/shard_map/ppermute | solution.py:134
  3.7 10.8 %collective-permute-start.5 = (bf16[256,640]{1,0:T(8,128)(2,1)}, bf16[256,640]{1,0:T(8,128)(2,1)S(1)}, u32[]{:S(2)}, u32[]{:S(2)}) collective-permute-start(bf16[256,640]{1,0:T(8,128)(2,1)} %bitcast.20), channel_id=1, source_target_pairs={{0,2},{1,3},{2,0},{3,1},{4,6},{5,7},{6,4},{7,5},{8,10},{9,11},{10,... | collective-permute-start | bytes 983048 | tf_op jit(solution)/shard_map/ppermute | solution.py:134
  5.9 1.0 %copy-start.1 = (bf16[1,16,16,640]{3,2,1,0:T(8,128)(2,1)S(1)}, bf16[1,16,16,640]{3,2,1,0:T(8,128)(2,1)}, u32[]{:S(2)}) copy-start(bf16[1,16,16,640]{3,2,1,0:T(8,128)(2,1)} %param.8) | copy-start | bytes 983044
  6.9 7.6 %copy-start.6 = (bf16[1,16,16,640]{3,2,1,0:T(8,128)(2,1)S(1)}, bf16[1,16,16,640]{3,2,1,0:T(8,128)(2,1)}, u32[]{:S(2)}) copy-start(bf16[1,16,16,640]{3,2,1,0:T(8,128)(2,1)} %param.9) | copy-start | bytes 983044
  8.4 13.1 %collective-permute-start.4 = (bf16[256,640]{1,0:T(8,128)(2,1)S(1)}, bf16[256,640]{1,0:T(8,128)(2,1)S(1)}, u32[]{:S(2)}, u32[]{:S(2)}) collective-permute-start(bf16[256,640]{1,0:T(8,128)(2,1)S(1)} %get-tuple-element.39.refs_1_.refs_2_), channel_id=1, source_target_pairs={{0,2},{1,3},{2,0},{3,1},{4,6},{5,7},{6,4},{7,5},{8,10},{9,11},{10,... | collective-permute-start | bytes 983048 | tf_op jit(solution)/shard_map/ppermute | solution.py:134
  9.0 12.5 %collective-permute-start.3 = (bf16[256,640]{1,0:T(8,128)(2,1)S(1)}, bf16[256,640]{1,0:T(8,128)(2,1)S(1)}, u32[]{:S(2)}, u32[]{:S(2)}) collective-permute-start(bf16[256,640]{1,0:T(8,128)(2,1)S(1)} %get-tuple-element.39.refs_1_.refs_2_), channel_id=1, source_target_pairs={{0,4},{1,5},{2,6},{3,7},{4,0},{5,1},{6,2},{7,3},{8,12},{9,13},{10,... | collective-permute-start | bytes 983048 | tf_op jit(solution)/shard_map/ppermute | solution.py:134
  9.2 1.2 %copy-start.3 = (bf16[1,720,640]{2,1,0:T(8,128)(2,1)S(1)}, bf16[1,720,640]{2,1,0:T(8,128)(2,1)}, u32[]{:S(2)}) copy-start(bf16[1,720,640]{2,1,0:T(8,128)(2,1)} %param.10) | copy-start | bytes 2764804
  15.7 10.5 %collective-permute-start.10 = (bf16[128,640]{1,0:T(8,128)(2,1)S(1)}, bf16[128,640]{1,0:T(8,128)(2,1)S(1)}, u32[]{:S(2)}, u32[]{:S(2)}) collective-permute-start(bf16[128,640]{1,0:T(8,128)(2,1)S(1)} %slice.18), channel_id=1, source_target_pairs={{0,4},{1,5},{2,6},{3,7},{4,0},{5,1},{6,2},{7,3},{8,12},{9,13},{10,... | collective-permute-start | bytes 491528 | tf_op jit(solution)/shard_map/ppermute | solution.py:134
  15.8 10.4 %collective-permute-start.9 = (bf16[128,640]{1,0:T(8,128)(2,1)S(1)}, bf16[128,640]{1,0:T(8,128)(2,1)S(1)}, u32[]{:S(2)}, u32[]{:S(2)}) collective-permute-start(bf16[128,640]{1,0:T(8,128)(2,1)S(1)} %slice.17), channel_id=1, source_target_pairs={{0,2},{1,3},{2,0},{3,1},{4,6},{5,7},{6,4},{7,5},{8,10},{9,11},{10,... | collective-permute-start | bytes 491528 | tf_op jit(solution)/shard_map/ppermute | solution.py:134
  21.6 6.2 %collective-permute-start.7 = (bf16[128,640]{1,0:T(8,128)(2,1)S(1)}, bf16[128,640]{1,0:T(8,128)(2,1)S(1)}, u32[]{:S(2)}, u32[]{:S(2)}) collective-permute-start(bf16[128,640]{1,0:T(8,128)(2,1)S(1)} %slice.15), channel_id=1, source_target_pairs={{0,2},{1,3},{2,0},{3,1},{4,6},{5,7},{6,4},{7,5},{8,10},{9,11},{10,... | collective-permute-start | bytes 491528 | tf_op jit(solution)/shard_map/ppermute | solution.py:134
  23.1 5.3 %collective-permute-start.8 = (bf16[128,640]{1,0:T(8,128)(2,1)S(1)}, bf16[128,640]{1,0:T(8,128)(2,1)S(1)}, u32[]{:S(2)}, u32[]{:S(2)}) collective-permute-start(bf16[128,640]{1,0:T(8,128)(2,1)S(1)} %slice.16), channel_id=1, source_target_pairs={{0,4},{1,5},{2,6},{3,7},{4,0},{5,1},{6,2},{7,3},{8,12},{9,13},{10,... | collective-permute-start | bytes 491528 | tf_op jit(solution)/shard_map/ppermute | solution.py:134
  30.0 2.5 %collective-permute-start.11 = (bf16[720,640]{1,0:T(8,128)(2,1)S(1)}, bf16[720,640]{1,0:T(8,128)(2,1)S(1)}, u32[]{:S(2)}, u32[]{:S(2)}) collective-permute-start(bf16[720,640]{1,0:T(8,128)(2,1)S(1)} %shard_map.102), channel_id=1, source_target_pairs={{0,1},{1,0},{2,3},{3,2},{4,5},{5,4},{6,7},{7,6},{8,9},{9,8},{10,11... | collective-permute-start | bytes 2764808 | tf_op jit(solution)/shard_map/ppermute | solution.py:134
  32.7 44.1 %collective-permute-start.19 = (bf16[720,640]{1,0:T(8,128)(2,1)S(1)}, bf16[720,640]{1,0:T(8,128)(2,1)S(1)}, u32[]{:S(2)}, u32[]{:S(2)}) collective-permute-start(bf16[720,640]{1,0:T(8,128)(2,1)S(1)} %shard_map.103.refs_7_.refs_2_.refs_3_.refs_1_), channel_id=1, source_target_pairs={{0,16},{8,24},{16,0},{24,8},{1,17},{9,25},{17,1},{25,9},{2,18},{10... | collective-permute-start | bytes 2764808 | tf_op jit(solution)/shard_map/ppermute | solution.py:134
  35.4 41.4 %collective-permute-start.18 = (bf16[720,640]{1,0:T(8,128)(2,1)S(1)}, bf16[720,640]{1,0:T(8,128)(2,1)}, u32[]{:S(2)}, u32[]{:S(2)}) collective-permute-start(bf16[720,640]{1,0:T(8,128)(2,1)S(1)} %shard_map.103.refs_7_.refs_2_.refs_3_.refs_1_), channel_id=1, source_target_pairs={{0,8},{8,0},{16,24},{24,16},{1,9},{9,1},{17,25},{25,17},{2,10},{10... | collective-permute-start | bytes 2764808 | tf_op jit(solution)/shard_map/ppermute | solution.py:134
  37.0 10.6 %collective-permute-start.14 = (bf16[256,640]{1,0:T(8,128)(2,1)S(1)}, bf16[256,640]{1,0:T(8,128)(2,1)S(1)}, u32[]{:S(2)}, u32[]{:S(2)}) collective-permute-start(bf16[256,640]{1,0:T(8,128)(2,1)S(1)} %get-tuple-element.57), channel_id=1, source_target_pairs={{0,2},{1,3},{2,0},{3,1},{4,6},{5,7},{6,4},{7,5},{8,10},{9,11},{10,... | collective-permute-start | bytes 983048 | tf_op jit(solution)/shard_map/ppermute | solution.py:134
  37.8 16.4 %collective-permute-start.15 = (bf16[256,640]{1,0:T(8,128)(2,1)S(1)}, bf16[256,640]{1,0:T(8,128)(2,1)S(1)}, u32[]{:S(2)}, u32[]{:S(2)}) collective-permute-start(bf16[256,640]{1,0:T(8,128)(2,1)S(1)} %get-tuple-element.58), channel_id=1, source_target_pairs={{0,4},{1,5},{2,6},{3,7},{4,0},{5,1},{6,2},{7,3},{8,12},{9,13},{10,... | collective-permute-start | bytes 983048 | tf_op jit(solution)/shard_map/ppermute | solution.py:134
  38.3 16.3 %collective-permute-start.16 = (bf16[256,640]{1,0:T(8,128)(2,1)S(1)}, bf16[256,640]{1,0:T(8,128)(2,1)S(1)}, u32[]{:S(2)}, u32[]{:S(2)}) collective-permute-start(bf16[256,640]{1,0:T(8,128)(2,1)S(1)} %get-tuple-element.59), channel_id=1, source_target_pairs={{0,6},{1,7},{2,4},{3,5},{4,2},{5,3},{6,0},{7,1},{8,14},{9,15},{10,... | collective-permute-start | bytes 983048 | tf_op jit(solution)/shard_map/ppermute | solution.py:134
  40.5 14.1 %copy-start.2 = (bf16[1,16,16,640]{3,2,1,0:T(8,128)(2,1)S(1)}, bf16[1,16,16,640]{3,2,1,0:T(8,128)(2,1)}, u32[]{:S(2)}) copy-start(bf16[1,16,16,640]{3,2,1,0:T(8,128)(2,1)} %param.8) | copy-start | bytes 983044
  45.3 8.9 %copy-start.4 = (f32[256,640]{1,0:T(8,128)}, f32[256,640]{1,0:T(8,128)S(1)}, u32[]{:S(2)}) copy-start(f32[256,640]{1,0:T(8,128)S(1)} %get-tuple-element.48.refs_0_) | copy-start | bytes 1966084
  45.3 22.1 %copy-start.8 = (s32[8]{0:T(128)S(1)}, s32[8]{0:T(128)}, u32[]{:S(2)}) copy-start(s32[8]{0:T(128)} %param.13) | copy-start | bytes 100
  47.6 15.6 %collective-permute-start.12 = (bf16[256,640]{1,0:T(8,128)(2,1)S(1)}, bf16[256,640]{1,0:T(8,128)(2,1)S(1)}, u32[]{:S(2)}, u32[]{:S(2)}) collective-permute-start(bf16[256,640]{1,0:T(8,128)(2,1)S(1)} %get-tuple-element.51), channel_id=1, source_target_pairs={{0,2},{1,3},{2,0},{3,1},{4,6},{5,7},{6,4},{7,5},{8,10},{9,11},{10,... | collective-permute-start | bytes 983048 | tf_op jit(solution)/shard_map/ppermute | solution.py:134
  54.2 9.0 %collective-permute-start.13 = (bf16[256,640]{1,0:T(8,128)(2,1)S(1)}, bf16[256,640]{1,0:T(8,128)(2,1)S(1)}, u32[]{:S(2)}, u32[]{:S(2)}) collective-permute-start(bf16[256,640]{1,0:T(8,128)(2,1)S(1)} %get-tuple-element.52), channel_id=1, source_target_pairs={{0,4},{1,5},{2,6},{3,7},{4,0},{5,1},{6,2},{7,3},{8,12},{9,13},{10,... | collective-permute-start | bytes 983048 | tf_op jit(solution)/shard_map/ppermute | solution.py:134
  56.7 3.9 %collective-permute-start.20 = (f32[2,640]{1,0:T(2,128)S(1)}, f32[2,640]{1,0:T(2,128)S(1)}, u32[]{:S(2)}, u32[]{:S(2)}) collective-permute-start(f32[2,640]{1,0:T(2,128)S(1)} %get-tuple-element.60.refs_1_), channel_id=1, source_target_pairs={{0,2},{1,3},{2,0},{3,1},{4,6},{5,7},{6,4},{7,5},{8,10},{9,11},{10,... | collective-permute-start | bytes 15368 | tf_op jit(solution)/shard_map/ppermute | solution.py:134
  60.6 9.6 %collective-permute-start.17 = (bf16[256,640]{1,0:T(8,128)(2,1)S(1)}, bf16[256,640]{1,0:T(8,128)(2,1)S(1)}, u32[]{:S(2)}, u32[]{:S(2)}) collective-permute-start(bf16[256,640]{1,0:T(8,128)(2,1)S(1)} %shard_map.108), channel_id=1, source_target_pairs={{0,6},{1,7},{2,4},{3,5},{4,2},{5,3},{6,0},{7,1},{8,14},{9,15},{10,... | collective-permute-start | bytes 983048 | tf_op jit(solution)/shard_map/ppermute | solution.py:134
  63.2 4.2 %collective-permute-start.21 = (f32[2,640]{1,0:T(2,128)S(1)}, f32[2,640]{1,0:T(2,128)S(1)}, u32[]{:S(2)}, u32[]{:S(2)}) collective-permute-start(f32[2,640]{1,0:T(2,128)S(1)} %shard_map.111), channel_id=1, source_target_pairs={{0,4},{1,5},{2,6},{3,7},{4,0},{5,1},{6,2},{7,3},{8,12},{9,13},{10,... | collective-permute-start | bytes 15368 | tf_op jit(solution)/shard_map/ppermute | solution.py:134
  67.4 1.3 %collective-permute-start.22 = (f32[2,640]{1,0:T(2,128)S(1)}, f32[2,640]{1,0:T(2,128)S(1)}, u32[]{:S(2)}, u32[]{:S(2)}) collective-permute-start(f32[2,640]{1,0:T(2,128)S(1)} %add.35), channel_id=1, source_target_pairs={{0,1},{1,0},{2,3},{3,2},{4,5},{5,4},{6,7},{7,6},{8,9},{9,8},{10,11... | collective-permute-start | bytes 15368 | tf_op jit(solution)/shard_map/ppermute | solution.py:134
  70.2 1.1 %copy-start.5 = (f32[256,640]{1,0:T(8,128)S(1)}, f32[256,640]{1,0:T(8,128)}, u32[]{:S(2)}) copy-start(f32[256,640]{1,0:T(8,128)} %copy-done.4) | copy-start | bytes 1966084
  72.2 1.0 %copy-start = (bf16[256,640]{1,0:T(8,128)(2,1)S(1)}, bf16[256,640]{1,0:T(8,128)(2,1)}, u32[]{:S(2)}) copy-start(bf16[256,640]{1,0:T(8,128)(2,1)} %shard_map.109.refs_1_) | copy-start | bytes 983044
  73.1 3.6 %collective-permute-start.1 = (f32[2,640]{1,0:T(2,128)S(1)}, f32[2,640]{1,0:T(2,128)S(1)}, u32[]{:S(2)}, u32[]{:S(2)}) collective-permute-start(f32[2,640]{1,0:T(2,128)S(1)} %param.1), channel_id=1, source_target_pairs={{0,8},{8,0},{16,24},{24,16},{1,9},{9,1},{17,25},{25,17},{2,10},{10... | collective-permute-start | bytes 15368 | tf_op jit(solution)/shard_map/cond/branch_1_fun/ppermute | solution.py:134
  76.8 3.1 %copy-start.7 = (f32[1,2,640]{2,1,0:T(2,128)}, f32[1,2,640]{2,1,0:T(2,128)S(1)}, u32[]{:S(2)}) copy-start(f32[1,2,640]{2,1,0:T(2,128)S(1)} %get-tuple-element.64) | copy-start | bytes 15364

commit v4 on v2

--- a/solution.py
+++ b/solution.py
@@ -283,9 +283,10 @@
 
 def turn_twice(top, bottom, across):
     chans, half = top.shape[1], top.shape[0]
+    left, right = top[...].T, bottom[...].T
     for start in (0, chans):
-        across[start : start + chans, :half] = top[...].T
-        across[start : start + chans, half:] = bottom[...].T
+        across[start : start + chans, :half] = left
+        across[start : start + chans, half:] = right
 
 
 def window_terms(start, rows, chans, across, moved, part):

time: 80.3 us -> 80.2 us (level)
  Pallas kernels: 24.8 us -> 23.8 us
  waiting for transfers between devices: 25.1 us -> 26.1 us
    ppermute x22, waiting for transfers between devices: 25.1 us -> 26.1 us  [swap(): return lax.ppermute(value, axis, pairs)]
    pallas_call x13, Pallas kernels: 24.8 us -> 23.8 us  [call(): pl.pallas_call(body, out_shape=tuple(outs), in_specs=[untouched if index...]
where the time goes in v4:
time: 80.2 us; the launch traced here: 79.8 us
  waiting for transfers between devices  26.1 us (33%)
  Pallas kernels  23.8 us (30%)
  starting transfers between devices  22.4 us (28%)
  local copies, waits for them, and re-layouts  4.97 us (6%)
  between operations  1.7 us (2%)
    ppermute x22, waiting for transfers between devices, swap(): return lax.ppermute(value, axis, pairs)  26.1 us
    pallas_call x13, Pallas kernels, call(): pl.pallas_call(body, out_shape=tuple(outs), in_specs=[untouched if index...  23.8 us
    ppermute x22, starting transfers between devices, swap(): return lax.ppermute(value, axis, pairs)  22.4 us
    unnamed x18, local copies, waits for them, and re-layouts  4.23 us
  transfers between devices with their start and end apart: 22, of which 13 were waited for; matrix products, arithmetic and copies ran while one was open for 2% of the time, Pallas kernels for 25%

profile of v4, /device:TPU:0, one launch (start us, length us, event | category | flops | bytes accessed | tf_op | source)
XLA Modules:
  0.0 79.8 jit_solution(9916188106628151863)
XLA Ops:
  1.1 2.6 %collective-permute-start.6 = (bf16[256,640]{1,0:T(8,128)(2,1)}, bf16[256,640]{1,0:T(8,128)(2,1)S(1)}, u32[]{:S(2)}, u32[]{:S(2)}) collective-permute-start(bf16[256,640]{1,0:T(8,128)(2,1)} %bitcast.19), channel_id=1, source_target_pairs={{0,4},{1,5},{2,6},{3,7},{4,0},{5,1},{6,2},{7,3},{8,12},{9,13},{10,... | collective-permute-start | bytes 983048 | tf_op jit(solution)/shard_map/ppermute | solution.py:134
  3.7 1.5 %collective-permute-start.5 = (bf16[256,640]{1,0:T(8,128)(2,1)}, bf16[256,640]{1,0:T(8,128)(2,1)S(1)}, u32[]{:S(2)}, u32[]{:S(2)}) collective-permute-start(bf16[256,640]{1,0:T(8,128)(2,1)} %bitcast.20), channel_id=1, source_target_pairs={{0,2},{1,3},{2,0},{3,1},{4,6},{5,7},{6,4},{7,5},{8,10},{9,11},{10,... | collective-permute-start | bytes 983048 | tf_op jit(solution)/shard_map/ppermute | solution.py:134
  6.9 1.5 %shard_map.93 = (bf16[256,640]{1,0:T(8,128)(2,1)S(1)}, f32[2,640]{1,0:T(2,128)S(1)}) custom-call(bf16[256,640]{1,0:T(8,128)(2,1)S(1)} %bitcast.15, f32[2,640]{1,0:T(2,128)S(1)} %pad_maximum_fusion.refs_1_.refs_2_), custom_call_target="tpu_custom_call" | custom-call | tf_op jit(solution)/shard_map/pallas_call | solution.py:145
  9.2 1.2 %copy-done.3 = bf16[1,720,640]{2,1,0:T(8,128)(2,1)S(1)} copy-done((bf16[1,720,640]{2,1,0:T(8,128)(2,1)S(1)}, bf16[1,720,640]{2,1,0:T(8,128)(2,1)}, u32[]{:S(2)}) %copy-start.3) | copy-done | bytes 921624
  10.3 1.9 %shard_map.94 = (bf16[1920,640]{1,0:T(8,128)(2,1)S(1)}, bf16[1920,640]{1,0:T(8,128)(2,1)S(1)}, bf16[768,256]{1,0:T(8,128)(2,1)S(1)}, bf16[768,256]{1,0:T(8,128)(2,1)S(1)}) custom-call(s32[3]{0:T(128)S(1)} %pad_add_fusion.refs_0_, bf16[720,640]{1,0:T(8,128)(2,1)S(1)} %bitcast.18, bf16[720,640]{1,0:T(8,128)(2,1)S(1)} %collective-permute-done.2.refs_2_, ...), custom_call_target="tpu_custom_call" | custom-call | tf_op jit(solution)/shard_map/pallas_call | solution.py:145
  12.5 2.0 %collective-permute-done.5.refs_2_.refs_0_ = bf16[256,640]{1,0:T(8,128)(2,1)S(1)} collective-permute-done((bf16[256,640]{1,0:T(8,128)(2,1)}, bf16[256,640]{1,0:T(8,128)(2,1)S(1)}, u32[]{:S(2)}, u32[]{:S(2)}) %collective-permute-start.5) | collective-permute-done | bytes 327712 | tf_op jit(solution)/shard_map/ppermute | solution.py:134
  14.5 1.1 %shard_map.95.refs_1_.refs_2_.refs_0_ = bf16[768,1920]{1,0:T(8,128)(2,1)S(1)} custom-call(bf16[768,256]{1,0:T(8,128)(2,1)S(1)} %get-tuple-element.41.refs_0_, bf16[256,640]{1,0:T(8,128)(2,1)S(1)} %bitcast.21, bf16[256,640]{1,0:T(8,128)(2,1)S(1)} %collective-permute-done.5.refs_2_.refs_0_, bf16[256,640]{1,0:T(8,128)(2,1)S(1)} %collective-permute-done.6.refs_3_.refs_1_), custom_call_target="tpu_custom_call" | custom-call | tf_op jit(solution)/shard_map/pallas_call | solution.py:145
  15.8 1.9 %collective-permute-start.9 = (bf16[128,640]{1,0:T(8,128)(2,1)S(1)}, bf16[128,640]{1,0:T(8,128)(2,1)S(1)}, u32[]{:S(2)}, u32[]{:S(2)}) collective-permute-start(bf16[128,640]{1,0:T(8,128)(2,1)S(1)} %slice.17), channel_id=1, source_target_pairs={{0,2},{1,3},{2,0},{3,1},{4,6},{5,7},{6,4},{7,5},{8,10},{9,11},{10,... | collective-permute-start | bytes 491528 | tf_op jit(solution)/shard_map/ppermute | solution.py:134
  17.7 2.6 %shard_map.96 = (f32[256,640]{1,0:T(8,128)S(1)}, bf16[256,640]{1,0:T(8,128)(2,1)S(1)}, bf16[256,640]{1,0:T(8,128)(2,1)S(1)}) custom-call(bf16[1920,640]{1,0:T(8,128)(2,1)S(1)} %get-tuple-element.40.refs_0_.refs_1_, bf16[768,1920]{1,0:T(8,128)(2,1)S(1)} %shard_map.95.refs_1_.refs_2_.refs_0_), custom_call_target="tpu_custom_call" | custom-call | tf_op jit(solution)/shard_map/pallas_call | solution.py:145
  20.3 1.2 %collective-permute-done.4.refs_1_ = bf16[256,640]{1,0:T(8,128)(2,1)S(1)} collective-permute-done((bf16[256,640]{1,0:T(8,128)(2,1)S(1)}, bf16[256,640]{1,0:T(8,128)(2,1)S(1)}, u32[]{:S(2)}, u32[]{:S(2)}) %collective-permute-start.4) | collective-permute-done | bytes 327712 | tf_op jit(solution)/shard_map/ppermute | solution.py:134
  21.6 1.6 %collective-permute-start.7 = (bf16[128,640]{1,0:T(8,128)(2,1)S(1)}, bf16[128,640]{1,0:T(8,128)(2,1)S(1)}, u32[]{:S(2)}, u32[]{:S(2)}) collective-permute-start(bf16[128,640]{1,0:T(8,128)(2,1)S(1)} %slice.15), channel_id=1, source_target_pairs={{0,2},{1,3},{2,0},{3,1},{4,6},{5,7},{6,4},{7,5},{8,10},{9,11},{10,... | collective-permute-start | bytes 491528 | tf_op jit(solution)/shard_map/ppermute | solution.py:134
  23.6 2.5 %shard_map.99.refs_3_.refs_5_.refs_4_ = f32[1920,640]{1,0:T(8,128)S(1)} custom-call(bf16[768,1920]{1,0:T(8,128)(2,1)S(1)} %shard_map.95.refs_1_.refs_2_.refs_0_, bf16[256,640]{1,0:T(8,128)(2,1)S(1)} %get-tuple-element.39.refs_1_.refs_2_, bf16[256,640]{1,0:T(8,128)(2,1)S(1)} %get-tuple-element.43.refs_2_.refs_3_, ...), custom_call_target="tpu_custom_call" | custom-call | tf_op jit(solution)/shard_map/pallas_call | solution.py:145
  26.6 1.1 %collective-permute-done.7.refs_2_.refs_1_.refs_5_ = bf16[128,640]{1,0:T(8,128)(2,1)S(1)} collective-permute-done((bf16[128,640]{1,0:T(8,128)(2,1)S(1)}, bf16[128,640]{1,0:T(8,128)(2,1)S(1)}, u32[]{:S(2)}, u32[]{:S(2)}) %collective-permute-start.7) | collective-permute-done | bytes 163872 | tf_op jit(solution)/shard_map/ppermute | solution.py:134
  28.5 1.5 %shard_map.102 = bf16[720,640]{1,0:T(8,128)(2,1)S(1)} custom-call(s32[3]{0:T(128)S(1)} %pad_add_fusion.refs_0_, bf16[128,640]{1,0:T(8,128)(2,1)S(1)} %collective-permute-done.7.refs_2_.refs_1_.refs_5_, bf16[128,640]{1,0:T(8,128)(2,1)S(1)} %collective-permute-done.8.refs_3_.refs_2_.refs_6_, bf16[256,1920]{1,0:T(8,128)(2,1)S(1)} %shard_map.100.refs_4_.refs_3_, ...), custom_call_target="tpu_custom_call" | custom-call | tf_op jit(solution)/shard_map/pallas_call | solution.py:145
  30.0 2.3 %shard_map.101 = (f32[720,640]{1,0:T(8,128)S(1)}, bf16[256,640]{1,0:T(8,128)(2,1)S(1)}) custom-call(s32[3]{0:T(128)S(1)} %pad_add_fusion.refs_0_, bf16[1920,640]{1,0:T(8,128)(2,1)S(1)} %get-tuple-element.40.refs_0_.refs_1_, bf16[128,640]{1,0:T(8,128)(2,1)S(1)} %collective-permute-done.7.refs_2_.refs_1_.refs_5_, ...), custom_call_target="tpu_custom_call" | custom-call | tf_op jit(solution)/shard_map/pallas_call | solution.py:145
  32.7 2.7 %collective-permute-start.19 = (bf16[720,640]{1,0:T(8,128)(2,1)S(1)}, bf16[720,640]{1,0:T(8,128)(2,1)S(1)}, u32[]{:S(2)}, u32[]{:S(2)}) collective-permute-start(bf16[720,640]{1,0:T(8,128)(2,1)S(1)} %shard_map.103.refs_7_.refs_2_.refs_3_.refs_1_), channel_id=1, source_target_pairs={{0,16},{8,24},{16,0},{24,8},{1,17},{9,25},{17,1},{25,9},{2,18},{10... | collective-permute-start | bytes 2764808 | tf_op jit(solution)/shard_map/ppermute | solution.py:134
  35.3 1.6 %collective-permute-start.18 = (bf16[720,640]{1,0:T(8,128)(2,1)S(1)}, bf16[720,640]{1,0:T(8,128)(2,1)}, u32[]{:S(2)}, u32[]{:S(2)}) collective-permute-start(bf16[720,640]{1,0:T(8,128)(2,1)S(1)} %shard_map.103.refs_7_.refs_2_.refs_3_.refs_1_), channel_id=1, source_target_pairs={{0,8},{8,0},{16,24},{24,16},{1,9},{9,1},{17,25},{25,17},{2,10},{10... | collective-permute-start | bytes 2764808 | tf_op jit(solution)/shard_map/ppermute | solution.py:134
  38.2 2.2 %collective-permute-start.16 = (bf16[256,640]{1,0:T(8,128)(2,1)S(1)}, bf16[256,640]{1,0:T(8,128)(2,1)S(1)}, u32[]{:S(2)}, u32[]{:S(2)}) collective-permute-start(bf16[256,640]{1,0:T(8,128)(2,1)S(1)} %get-tuple-element.59), channel_id=1, source_target_pairs={{0,6},{1,7},{2,4},{3,5},{4,2},{5,3},{6,0},{7,1},{8,14},{9,15},{10,... | collective-permute-start | bytes 983048 | tf_op jit(solution)/shard_map/ppermute | solution.py:134
  40.4 4.8 %shard_map.104 = (f32[256,640]{1,0:T(8,128)S(1)}, bf16[256,640]{1,0:T(8,128)(2,1)S(1)}, bf16[256,640]{1,0:T(8,128)(2,1)S(1)}, bf16[256,640]{1,0:T(8,128)(2,1)S(1)}) custom-call(bf16[768,256]{1,0:T(8,128)(2,1)S(1)} %get-tuple-element.37.refs_0_, bf16[1920,640]{1,0:T(8,128)(2,1)S(1)} %get-tuple-element.38.refs_1_, ...), custom_call_target="tpu_custom_call" | custom-call | tf_op jit(solution)/shard_map/pallas_call | solution.py:145
  45.2 2.3 %collective-permute-done.14.refs_4_ = bf16[256,640]{1,0:T(8,128)(2,1)S(1)} collective-permute-done((bf16[256,640]{1,0:T(8,128)(2,1)S(1)}, bf16[256,640]{1,0:T(8,128)(2,1)S(1)}, u32[]{:S(2)}, u32[]{:S(2)}) %collective-permute-start.14) | collective-permute-done | bytes 327712 | tf_op jit(solution)/shard_map/ppermute | solution.py:134
  48.3 5.7 %collective-permute-done.15.refs_5_ = bf16[256,640]{1,0:T(8,128)(2,1)S(1)} collective-permute-done((bf16[256,640]{1,0:T(8,128)(2,1)S(1)}, bf16[256,640]{1,0:T(8,128)(2,1)S(1)}, u32[]{:S(2)}, u32[]{:S(2)}) %collective-permute-start.15) | collective-permute-done | bytes 327712 | tf_op jit(solution)/shard_map/ppermute | solution.py:134
  54.5 2.1 %shard_map.107 = (bf16[256,640]{1,0:T(8,128)(2,1)}, f32[2,640]{1,0:T(2,128)S(1)}) custom-call(bf16[256,640]{1,0:T(8,128)(2,1)S(1)} %bitcast.16, f32[2,640]{1,0:T(2,128)S(1)} %get-tuple-element.36.refs_3_.refs_1_, f32[2,640]{1,0:T(2,128)S(1)} %pad_maximum_fusion.refs_1_.refs_2_, f32[256,640]{1,0:T(8,128)S(1)} %get-tuple-element.42.refs_2_.refs_3_, ...), custom_call_target="tpu_custom_call" | custom-call | tf_op jit(solution)/shard_map/pallas_call | solution.py:145
  56.6 1.4 %collective-permute-start.20 = (f32[2,640]{1,0:T(2,128)S(1)}, f32[2,640]{1,0:T(2,128)S(1)}, u32[]{:S(2)}, u32[]{:S(2)}) collective-permute-start(f32[2,640]{1,0:T(2,128)S(1)} %get-tuple-element.60.refs_1_), channel_id=1, source_target_pairs={{0,2},{1,3},{2,0},{3,1},{4,6},{5,7},{6,4},{7,5},{8,10},{9,11},{10,... | collective-permute-start | bytes 15368 | tf_op jit(solution)/shard_map/ppermute | solution.py:134
  58.0 2.5 %collective-permute-done.20 = f32[2,640]{1,0:T(2,128)S(1)} collective-permute-done((f32[2,640]{1,0:T(2,128)S(1)}, f32[2,640]{1,0:T(2,128)S(1)}, u32[]{:S(2)}, u32[]{:S(2)}) %collective-permute-start.20) | collective-permute-done | bytes 5152 | tf_op jit(solution)/shard_map/ppermute | solution.py:134
  60.5 2.6 %collective-permute-start.17 = (bf16[256,640]{1,0:T(8,128)(2,1)S(1)}, bf16[256,640]{1,0:T(8,128)(2,1)S(1)}, u32[]{:S(2)}, u32[]{:S(2)}) collective-permute-start(bf16[256,640]{1,0:T(8,128)(2,1)S(1)} %shard_map.108), channel_id=1, source_target_pairs={{0,6},{1,7},{2,4},{3,5},{4,2},{5,3},{6,0},{7,1},{8,14},{9,15},{10,... | collective-permute-start | bytes 983048 | tf_op jit(solution)/shard_map/ppermute | solution.py:134
  63.2 4.1 %collective-permute-done.21 = f32[2,640]{1,0:T(2,128)S(1)} collective-permute-done((f32[2,640]{1,0:T(2,128)S(1)}, f32[2,640]{1,0:T(2,128)S(1)}, u32[]{:S(2)}, u32[]{:S(2)}) %collective-permute-start.21) | collective-permute-done | bytes 5152 | tf_op jit(solution)/shard_map/ppermute | solution.py:134
  68.6 1.4 %collective-permute-done.17.refs_3_ = bf16[256,640]{1,0:T(8,128)(2,1)S(1)} collective-permute-done((bf16[256,640]{1,0:T(8,128)(2,1)S(1)}, bf16[256,640]{1,0:T(8,128)(2,1)S(1)}, u32[]{:S(2)}, u32[]{:S(2)}) %collective-permute-start.17) | collective-permute-done | bytes 327712 | tf_op jit(solution)/shard_map/ppermute | solution.py:134
  70.1 1.1 %copy-done.5 = f32[256,640]{1,0:T(8,128)S(1)} copy-done((f32[256,640]{1,0:T(8,128)S(1)}, f32[256,640]{1,0:T(8,128)}, u32[]{:S(2)}) %copy-start.5) | copy-done | bytes 655384
  72.0 1.0 %copy-done = bf16[256,640]{1,0:T(8,128)(2,1)S(1)} copy-done((bf16[256,640]{1,0:T(8,128)(2,1)S(1)}, bf16[256,640]{1,0:T(8,128)(2,1)}, u32[]{:S(2)}) %copy-start) | copy-done | bytes 327704
  73.0 4.5 %conditional.1 = (f32[1,2,640]{2,1,0:T(2,128)S(1)}) conditional(s32[]{:T(128)} %bitcast.11, f32[2,640]{1,0:T(2,128)S(1)} %shard_map.112, f32[2,640]{1,0:T(2,128)S(1)} %shard_map.112), branch_computations={%region_0.1_spmd, %region_1.2_spmd} | conditional | flops 2560 | bytes 35888 | solution.py:484
  73.4 4.1 %collective-permute-done = f32[2,640]{1,0:T(2,128)S(1)} collective-permute-done((f32[2,640]{1,0:T(2,128)S(1)}, f32[2,640]{1,0:T(2,128)S(1)}, u32[]{:S(2)}, u32[]{:S(2)}) %collective-permute-start) | collective-permute-done | bytes 5152 | tf_op jit(solution)/shard_map/cond/branch_0_fun/ppermute | solution.py:134
  77.6 2.1 %shard_map.110 = f32[720,640]{1,0:T(8,128)} custom-call(s32[1]{0:T(128)} %get-tuple-element.63.refs_0_, bf16[720,640]{1,0:T(8,128)(2,1)S(1)} %shard_map.103.refs_7_.refs_2_.refs_3_.refs_1_, bf16[720,640]{1,0:T(8,128)(2,1)} %collective-permute-done.18.refs_2_, bf16[720,640]{1,0:T(8,128)(2,1)S(1)} %collective-permute-done.19.refs_3_), custom_call_target="tpu_custom_call" | custom-call | tf_op jit(solution)/shard_map/pallas_call | solution.py:145
  (62 shorter events, 10.2 us)
Async XLA Ops:
  0.6 8.5 %collective-permute-start.2 = (bf16[720,640]{1,0:T(8,128)(2,1)}, bf16[720,640]{1,0:T(8,128)(2,1)S(1)}, u32[]{:S(2)}, u32[]{:S(2)}) collective-permute-start(bf16[720,640]{1,0:T(8,128)(2,1)} %bitcast.17), channel_id=1, source_target_pairs={{0,1},{1,0},{2,3},{3,2},{4,5},{5,4},{6,7},{7,6},{8,9},{9,8},{10,11... | collective-permute-start | bytes 2764808 | tf_op jit(solution)/shard_map/ppermute | solution.py:134
  1.1 11.4 %collective-permute-start.6 = (bf16[256,640]{1,0:T(8,128)(2,1)}, bf16[256,640]{1,0:T(8,128)(2,1)S(1)}, u32[]{:S(2)}, u32[]{:S(2)}) collective-permute-start(bf16[256,640]{1,0:T(8,128)(2,1)} %bitcast.19), channel_id=1, source_target_pairs={{0,4},{1,5},{2,6},{3,7},{4,0},{5,1},{6,2},{7,3},{8,12},{9,13},{10,... | collective-permute-start | bytes 983048 | tf_op jit(solution)/shard_map/ppermute | solution.py:134
  3.7 10.8 %collective-permute-start.5 = (bf16[256,640]{1,0:T(8,128)(2,1)}, bf16[256,640]{1,0:T(8,128)(2,1)S(1)}, u32[]{:S(2)}, u32[]{:S(2)}) collective-permute-start(bf16[256,640]{1,0:T(8,128)(2,1)} %bitcast.20), channel_id=1, source_target_pairs={{0,2},{1,3},{2,0},{3,1},{4,6},{5,7},{6,4},{7,5},{8,10},{9,11},{10,... | collective-permute-start | bytes 983048 | tf_op jit(solution)/shard_map/ppermute | solution.py:134
  5.9 1.0 %copy-start.1 = (bf16[1,16,16,640]{3,2,1,0:T(8,128)(2,1)S(1)}, bf16[1,16,16,640]{3,2,1,0:T(8,128)(2,1)}, u32[]{:S(2)}) copy-start(bf16[1,16,16,640]{3,2,1,0:T(8,128)(2,1)} %param.8) | copy-start | bytes 983044
  6.9 7.6 %copy-start.6 = (bf16[1,16,16,640]{3,2,1,0:T(8,128)(2,1)S(1)}, bf16[1,16,16,640]{3,2,1,0:T(8,128)(2,1)}, u32[]{:S(2)}) copy-start(bf16[1,16,16,640]{3,2,1,0:T(8,128)(2,1)} %param.9) | copy-start | bytes 983044
  8.4 13.1 %collective-permute-start.4 = (bf16[256,640]{1,0:T(8,128)(2,1)S(1)}, bf16[256,640]{1,0:T(8,128)(2,1)S(1)}, u32[]{:S(2)}, u32[]{:S(2)}) collective-permute-start(bf16[256,640]{1,0:T(8,128)(2,1)S(1)} %get-tuple-element.39.refs_1_.refs_2_), channel_id=1, source_target_pairs={{0,2},{1,3},{2,0},{3,1},{4,6},{5,7},{6,4},{7,5},{8,10},{9,11},{10,... | collective-permute-start | bytes 983048 | tf_op jit(solution)/shard_map/ppermute | solution.py:134
  9.0 12.5 %collective-permute-start.3 = (bf16[256,640]{1,0:T(8,128)(2,1)S(1)}, bf16[256,640]{1,0:T(8,128)(2,1)S(1)}, u32[]{:S(2)}, u32[]{:S(2)}) collective-permute-start(bf16[256,640]{1,0:T(8,128)(2,1)S(1)} %get-tuple-element.39.refs_1_.refs_2_), channel_id=1, source_target_pairs={{0,4},{1,5},{2,6},{3,7},{4,0},{5,1},{6,2},{7,3},{8,12},{9,13},{10,... | collective-permute-start | bytes 983048 | tf_op jit(solution)/shard_map/ppermute | solution.py:134
  9.2 1.2 %copy-start.3 = (bf16[1,720,640]{2,1,0:T(8,128)(2,1)S(1)}, bf16[1,720,640]{2,1,0:T(8,128)(2,1)}, u32[]{:S(2)}) copy-start(bf16[1,720,640]{2,1,0:T(8,128)(2,1)} %param.10) | copy-start | bytes 2764804
  15.7 10.5 %collective-permute-start.10 = (bf16[128,640]{1,0:T(8,128)(2,1)S(1)}, bf16[128,640]{1,0:T(8,128)(2,1)S(1)}, u32[]{:S(2)}, u32[]{:S(2)}) collective-permute-start(bf16[128,640]{1,0:T(8,128)(2,1)S(1)} %slice.18), channel_id=1, source_target_pairs={{0,4},{1,5},{2,6},{3,7},{4,0},{5,1},{6,2},{7,3},{8,12},{9,13},{10,... | collective-permute-start | bytes 491528 | tf_op jit(solution)/shard_map/ppermute | solution.py:134
  15.8 10.4 %collective-permute-start.9 = (bf16[128,640]{1,0:T(8,128)(2,1)S(1)}, bf16[128,640]{1,0:T(8,128)(2,1)S(1)}, u32[]{:S(2)}, u32[]{:S(2)}) collective-permute-start(bf16[128,640]{1,0:T(8,128)(2,1)S(1)} %slice.17), channel_id=1, source_target_pairs={{0,2},{1,3},{2,0},{3,1},{4,6},{5,7},{6,4},{7,5},{8,10},{9,11},{10,... | collective-permute-start | bytes 491528 | tf_op jit(solution)/shard_map/ppermute | solution.py:134
  21.6 6.2 %collective-permute-start.7 = (bf16[128,640]{1,0:T(8,128)(2,1)S(1)}, bf16[128,640]{1,0:T(8,128)(2,1)S(1)}, u32[]{:S(2)}, u32[]{:S(2)}) collective-permute-start(bf16[128,640]{1,0:T(8,128)(2,1)S(1)} %slice.15), channel_id=1, source_target_pairs={{0,2},{1,3},{2,0},{3,1},{4,6},{5,7},{6,4},{7,5},{8,10},{9,11},{10,... | collective-permute-start | bytes 491528 | tf_op jit(solution)/shard_map/ppermute | solution.py:134
  23.1 5.3 %collective-permute-start.8 = (bf16[128,640]{1,0:T(8,128)(2,1)S(1)}, bf16[128,640]{1,0:T(8,128)(2,1)S(1)}, u32[]{:S(2)}, u32[]{:S(2)}) collective-permute-start(bf16[128,640]{1,0:T(8,128)(2,1)S(1)} %slice.16), channel_id=1, source_target_pairs={{0,4},{1,5},{2,6},{3,7},{4,0},{5,1},{6,2},{7,3},{8,12},{9,13},{10,... | collective-permute-start | bytes 491528 | tf_op jit(solution)/shard_map/ppermute | solution.py:134
  29.9 2.5 %collective-permute-start.11 = (bf16[720,640]{1,0:T(8,128)(2,1)S(1)}, bf16[720,640]{1,0:T(8,128)(2,1)S(1)}, u32[]{:S(2)}, u32[]{:S(2)}) collective-permute-start(bf16[720,640]{1,0:T(8,128)(2,1)S(1)} %shard_map.102), channel_id=1, source_target_pairs={{0,1},{1,0},{2,3},{3,2},{4,5},{5,4},{6,7},{7,6},{8,9},{9,8},{10,11... | collective-permute-start | bytes 2764808 | tf_op jit(solution)/shard_map/ppermute | solution.py:134
  32.7 44.9 %collective-permute-start.19 = (bf16[720,640]{1,0:T(8,128)(2,1)S(1)}, bf16[720,640]{1,0:T(8,128)(2,1)S(1)}, u32[]{:S(2)}, u32[]{:S(2)}) collective-permute-start(bf16[720,640]{1,0:T(8,128)(2,1)S(1)} %shard_map.103.refs_7_.refs_2_.refs_3_.refs_1_), channel_id=1, source_target_pairs={{0,16},{8,24},{16,0},{24,8},{1,17},{9,25},{17,1},{25,9},{2,18},{10... | collective-permute-start | bytes 2764808 | tf_op jit(solution)/shard_map/ppermute | solution.py:134
  35.3 42.2 %collective-permute-start.18 = (bf16[720,640]{1,0:T(8,128)(2,1)S(1)}, bf16[720,640]{1,0:T(8,128)(2,1)}, u32[]{:S(2)}, u32[]{:S(2)}) collective-permute-start(bf16[720,640]{1,0:T(8,128)(2,1)S(1)} %shard_map.103.refs_7_.refs_2_.refs_3_.refs_1_), channel_id=1, source_target_pairs={{0,8},{8,0},{16,24},{24,16},{1,9},{9,1},{17,25},{25,17},{2,10},{10... | collective-permute-start | bytes 2764808 | tf_op jit(solution)/shard_map/ppermute | solution.py:134
  36.9 10.6 %collective-permute-start.14 = (bf16[256,640]{1,0:T(8,128)(2,1)S(1)}, bf16[256,640]{1,0:T(8,128)(2,1)S(1)}, u32[]{:S(2)}, u32[]{:S(2)}) collective-permute-start(bf16[256,640]{1,0:T(8,128)(2,1)S(1)} %get-tuple-element.57), channel_id=1, source_target_pairs={{0,2},{1,3},{2,0},{3,1},{4,6},{5,7},{6,4},{7,5},{8,10},{9,11},{10,... | collective-permute-start | bytes 983048 | tf_op jit(solution)/shard_map/ppermute | solution.py:134
  37.7 16.3 %collective-permute-start.15 = (bf16[256,640]{1,0:T(8,128)(2,1)S(1)}, bf16[256,640]{1,0:T(8,128)(2,1)S(1)}, u32[]{:S(2)}, u32[]{:S(2)}) collective-permute-start(bf16[256,640]{1,0:T(8,128)(2,1)S(1)} %get-tuple-element.58), channel_id=1, source_target_pairs={{0,4},{1,5},{2,6},{3,7},{4,0},{5,1},{6,2},{7,3},{8,12},{9,13},{10,... | collective-permute-start | bytes 983048 | tf_op jit(solution)/shard_map/ppermute | solution.py:134
  38.2 16.3 %collective-permute-start.16 = (bf16[256,640]{1,0:T(8,128)(2,1)S(1)}, bf16[256,640]{1,0:T(8,128)(2,1)S(1)}, u32[]{:S(2)}, u32[]{:S(2)}) collective-permute-start(bf16[256,640]{1,0:T(8,128)(2,1)S(1)} %get-tuple-element.59), channel_id=1, source_target_pairs={{0,6},{1,7},{2,4},{3,5},{4,2},{5,3},{6,0},{7,1},{8,14},{9,15},{10,... | collective-permute-start | bytes 983048 | tf_op jit(solution)/shard_map/ppermute | solution.py:134
  40.4 14.1 %copy-start.2 = (bf16[1,16,16,640]{3,2,1,0:T(8,128)(2,1)S(1)}, bf16[1,16,16,640]{3,2,1,0:T(8,128)(2,1)}, u32[]{:S(2)}) copy-start(bf16[1,16,16,640]{3,2,1,0:T(8,128)(2,1)} %param.8) | copy-start | bytes 983044
  45.2 8.8 %copy-start.4 = (f32[256,640]{1,0:T(8,128)}, f32[256,640]{1,0:T(8,128)S(1)}, u32[]{:S(2)}) copy-start(f32[256,640]{1,0:T(8,128)S(1)} %get-tuple-element.48.refs_0_) | copy-start | bytes 1966084
  45.2 22.1 %copy-start.8 = (s32[8]{0:T(128)S(1)}, s32[8]{0:T(128)}, u32[]{:S(2)}) copy-start(s32[8]{0:T(128)} %param.13) | copy-start | bytes 100
  47.5 15.6 %collective-permute-start.12 = (bf16[256,640]{1,0:T(8,128)(2,1)S(1)}, bf16[256,640]{1,0:T(8,128)(2,1)S(1)}, u32[]{:S(2)}, u32[]{:S(2)}) collective-permute-start(bf16[256,640]{1,0:T(8,128)(2,1)S(1)} %get-tuple-element.51), channel_id=1, source_target_pairs={{0,2},{1,3},{2,0},{3,1},{4,6},{5,7},{6,4},{7,5},{8,10},{9,11},{10,... | collective-permute-start | bytes 983048 | tf_op jit(solution)/shard_map/ppermute | solution.py:134
  54.0 9.0 %collective-permute-start.13 = (bf16[256,640]{1,0:T(8,128)(2,1)S(1)}, bf16[256,640]{1,0:T(8,128)(2,1)S(1)}, u32[]{:S(2)}, u32[]{:S(2)}) collective-permute-start(bf16[256,640]{1,0:T(8,128)(2,1)S(1)} %get-tuple-element.52), channel_id=1, source_target_pairs={{0,4},{1,5},{2,6},{3,7},{4,0},{5,1},{6,2},{7,3},{8,12},{9,13},{10,... | collective-permute-start | bytes 983048 | tf_op jit(solution)/shard_map/ppermute | solution.py:134
  56.6 3.9 %collective-permute-start.20 = (f32[2,640]{1,0:T(2,128)S(1)}, f32[2,640]{1,0:T(2,128)S(1)}, u32[]{:S(2)}, u32[]{:S(2)}) collective-permute-start(f32[2,640]{1,0:T(2,128)S(1)} %get-tuple-element.60.refs_1_), channel_id=1, source_target_pairs={{0,2},{1,3},{2,0},{3,1},{4,6},{5,7},{6,4},{7,5},{8,10},{9,11},{10,... | collective-permute-start | bytes 15368 | tf_op jit(solution)/shard_map/ppermute | solution.py:134
  60.5 9.6 %collective-permute-start.17 = (bf16[256,640]{1,0:T(8,128)(2,1)S(1)}, bf16[256,640]{1,0:T(8,128)(2,1)S(1)}, u32[]{:S(2)}, u32[]{:S(2)}) collective-permute-start(bf16[256,640]{1,0:T(8,128)(2,1)S(1)} %shard_map.108), channel_id=1, source_target_pairs={{0,6},{1,7},{2,4},{3,5},{4,2},{5,3},{6,0},{7,1},{8,14},{9,15},{10,... | collective-permute-start | bytes 983048 | tf_op jit(solution)/shard_map/ppermute | solution.py:134
  63.1 4.2 %collective-permute-start.21 = (f32[2,640]{1,0:T(2,128)S(1)}, f32[2,640]{1,0:T(2,128)S(1)}, u32[]{:S(2)}, u32[]{:S(2)}) collective-permute-start(f32[2,640]{1,0:T(2,128)S(1)} %shard_map.111), channel_id=1, source_target_pairs={{0,4},{1,5},{2,6},{3,7},{4,0},{5,1},{6,2},{7,3},{8,12},{9,13},{10,... | collective-permute-start | bytes 15368 | tf_op jit(solution)/shard_map/ppermute | solution.py:134
  67.3 1.3 %collective-permute-start.22 = (f32[2,640]{1,0:T(2,128)S(1)}, f32[2,640]{1,0:T(2,128)S(1)}, u32[]{:S(2)}, u32[]{:S(2)}) collective-permute-start(f32[2,640]{1,0:T(2,128)S(1)} %add.35), channel_id=1, source_target_pairs={{0,1},{1,0},{2,3},{3,2},{4,5},{5,4},{6,7},{7,6},{8,9},{9,8},{10,11... | collective-permute-start | bytes 15368 | tf_op jit(solution)/shard_map/ppermute | solution.py:134
  70.1 1.1 %copy-start.5 = (f32[256,640]{1,0:T(8,128)S(1)}, f32[256,640]{1,0:T(8,128)}, u32[]{:S(2)}) copy-start(f32[256,640]{1,0:T(8,128)} %copy-done.4) | copy-start | bytes 1966084
  72.0 1.0 %copy-start = (bf16[256,640]{1,0:T(8,128)(2,1)S(1)}, bf16[256,640]{1,0:T(8,128)(2,1)}, u32[]{:S(2)}) copy-start(bf16[256,640]{1,0:T(8,128)(2,1)} %shard_map.109.refs_1_) | copy-start | bytes 983044
  73.0 4.5 %collective-permute-start = (f32[2,640]{1,0:T(2,128)S(1)}, f32[2,640]{1,0:T(2,128)S(1)}, u32[]{:S(2)}, u32[]{:S(2)}) collective-permute-start(f32[2,640]{1,0:T(2,128)S(1)} %param), channel_id=1, source_target_pairs={{0,16},{8,24},{16,0},{24,8},{1,17},{9,25},{17,1},{25,9},{2,18},{10... | collective-permute-start | bytes 15368 | tf_op jit(solution)/shard_map/cond/branch_0_fun/ppermute | solution.py:134
  77.5 2.2 %copy-start.7 = (f32[1,2,640]{2,1,0:T(2,128)}, f32[1,2,640]{2,1,0:T(2,128)S(1)}, u32[]{:S(2)}) copy-start(f32[1,2,640]{2,1,0:T(2,128)S(1)} %get-tuple-element.64) | copy-start | bytes 15364
